TPU v7x, 128 devices: a whole 4x4x4 slice. The times are simulated.
128 devices in a mesh: dp: 16 (over x, z_lo, core), ctx: 8 (over y, z_hi).
Axes of the slice: x: 4, y: 4, z: 4 (z_hi: 2, z_lo: 2; z = z_hi * 2 + z_lo), core: 2. Of those that a mesh axis runs over, the one named last changes fastest.
Arguments:
- layer_input: bfloat16 [16, 2048, 768], P('dp', 'ctx'), may hold values from -6 to 6
- cotangent: bfloat16 [16, 2048, 768], P('dp', 'ctx'), may hold values from -6 to 6
- lengths: int32 [16], P('dp'), may hold values from 1434 to 2048, as said below
- order: int32 [16, 16], P('dp'), may hold values from 0 to 15, each once within a row
- files: int32 [16, 2048], P('dp'), may hold values from 0 to 3, as said below
- ln1_gain: float32 [768], P(('dp', 'ctx')), may hold values from 0.25 to 1.75
- ln1_bias: float32 [768], P(('dp', 'ctx')), may hold values from -1.75 to 1.75
- w_attn: bfloat16 [768, 896], P(('dp', 'ctx')), may hold values from -0.21875 to 0.21875
- query_bias: float32 [768], P(('dp', 'ctx')), may hold values from -1.75 to 1.75
- value_bias: float32 [64], replicated, may hold values from -1.75 to 1.75
- w_out: bfloat16 [768, 768], P(('dp', 'ctx')), may hold values from -0.875 to 0.875
- out_bias: float32 [768], P(('dp', 'ctx')), may hold values from -1.75 to 1.75
- ln2_gain: float32 [768], P(('dp', 'ctx')), may hold values from 0.25 to 1.75
- ln2_bias: float32 [768], P(('dp', 'ctx')), may hold values from -1.75 to 1.75
- w_fc: bfloat16 [768, 3072], P(('dp', 'ctx')), may hold values from -0.21875 to 0.21875
- fc_bias: float32 [3072], P(('dp', 'ctx')), may hold values from -1.75 to 1.75
- w_proj: bfloat16 [768, 3072], P(('dp', 'ctx')), may hold values from -0.109375 to 0.109375
- proj_bias: float32 [768], P(('dp', 'ctx')), may hold values from -1.75 to 1.75
Outputs:
- output: bfloat16 [16, 2048, 768], P('dp', 'ctx')
- grad_input: bfloat16 [16, 2048, 768], P('dp', 'ctx')
- grad_ln1_gain: float32 [768], P(('dp', 'ctx'))
- grad_ln1_bias: float32 [768], P(('dp', 'ctx'))
- grad_w_attn: float32 [768, 896], P(('dp', 'ctx'))
- grad_query_bias: float32 [768], P(('dp', 'ctx'))
- grad_value_bias: float32 [64], replicated
- grad_w_out: float32 [768, 768], P(('dp', 'ctx'))
- grad_out_bias: float32 [768], P(('dp', 'ctx'))
- grad_ln2_gain: float32 [768], P(('dp', 'ctx'))
- grad_ln2_bias: float32 [768], P(('dp', 'ctx'))
- grad_w_fc: float32 [768, 3072], P(('dp', 'ctx'))
- grad_fc_bias: float32 [3072], P(('dp', 'ctx'))
- grad_w_proj: float32 [768, 3072], P(('dp', 'ctx'))
- grad_proj_bias: float32 [768], P(('dp', 'ctx'))
Inputs may be any that keep to these rules, and one draw needn't show every extreme that they name: `lengths`: positions at or past a row's length are padding; some row's length is 2048. `order`: each row is a permutation of the 16 block numbers. `files`: file numbers never fall along initial positions and start at 0.
All inputs are finite; a program needn't handle non-finite values.
Results may differ from a plain program's by a relative error of at most 0.017.
Values may be sent and summed in bfloat16 or wider, within the bound.
No kernel may reach another device: no remote copies, remote signals or barrier semaphores. Data moves between devices by JAX's collectives and lax.ppermute only.
A program may use at most 128 MiB of HBM per device.

v0:
```python
import math

import jax
import jax.numpy as jnp
from jax import lax
from jax.sharding import PartitionSpec as P

D = 768
HEADS = 12
HD = 64
FF = 3072


def normalize(values):
    center = values - jnp.mean(values, -1, keepdims=True)
    spread = jnp.mean(center * center, -1, keepdims=True)
    factor = lax.rsqrt(spread + 1e-05)
    return (center * factor, factor)


def norm_back(grad_normed, normed, factor):
    return factor * (
        grad_normed
        - jnp.mean(grad_normed, -1, keepdims=True)
        - normed * jnp.mean(grad_normed * normed, -1, keepdims=True)
    )


def right_product(left, piece):
    return lax.dot_general(
        left, piece, (((1,), (1,)), ((), ())), preferred_element_type=jnp.float32
    )


def token_product(left, right):
    return lax.dot_general(
        left, right, (((0,), (0,)), ((), ())), preferred_element_type=jnp.float32
    )


def local(
    layer_input,
    cotangent,
    lengths,
    order,
    files,
    ln1_gain,
    ln1_bias,
    w_attn,
    query_bias,
    value_bias,
    w_out,
    out_bias,
    ln2_gain,
    ln2_bias,
    w_fc,
    fc_bias,
    w_proj,
    proj_bias,
):
    tokens = layer_input[0].astype(jnp.float32)
    grad_out = cotangent[0].astype(jnp.float32)
    tok_count = tokens.shape[0]
    ctx_count = lax.axis_size("ctx")
    block_len = tok_count // 2
    full_length = tok_count * ctx_count
    score_scale = 1.0 / math.sqrt(HD)
    order_row = order[0]
    file_row = files[0]
    valid_length = lengths[0]
    key_place = jnp.repeat(order_row * block_len, block_len) + jnp.tile(
        jnp.arange(block_len, dtype=jnp.int32), 2 * ctx_count
    )
    own_index = lax.axis_index("ctx")
    query_place = lax.dynamic_slice_in_dim(key_place, own_index * tok_count, tok_count)
    key_file = jnp.take(file_row, key_place)
    query_file = lax.dynamic_slice_in_dim(key_file, own_index * tok_count, tok_count)
    allowed = (key_place[None, :] <= query_place[:, None]) & (
        key_file[None, :] == query_file[:, None]
    )
    allowed = allowed & (
        (key_place[None, :] < valid_length) | (key_place[None, :] == query_place[:, None])
    )
    vectors = (
        lax.all_gather(ln1_gain, ("dp", "ctx"), axis=0, tiled=True),
        lax.all_gather(ln1_bias, ("dp", "ctx"), axis=0, tiled=True),
        lax.all_gather(query_bias, ("dp", "ctx"), axis=0, tiled=True),
        lax.all_gather(out_bias, ("dp", "ctx"), axis=0, tiled=True),
        lax.all_gather(ln2_gain, ("dp", "ctx"), axis=0, tiled=True),
        lax.all_gather(ln2_bias, ("dp", "ctx"), axis=0, tiled=True),
        lax.all_gather(fc_bias, ("dp", "ctx"), axis=0, tiled=True),
        lax.all_gather(proj_bias, ("dp", "ctx"), axis=0, tiled=True),
    )
    gain_one, bias_one, bias_query, bias_out, gain_two, bias_two, bias_fc, bias_proj = vectors
    norm_one, factor_one = normalize(tokens)
    input_one = (norm_one * gain_one + bias_one).astype(jnp.bfloat16)
    columns = input_one
    raw_projected = jnp.dot(
        columns,
        lax.all_gather(w_attn, ("dp", "ctx"), axis=0, tiled=True),
        preferred_element_type=jnp.float32,
    )
    bias_full = jnp.concatenate([bias_query, jnp.zeros((HD,), jnp.float32), value_bias])
    projected = (raw_projected + bias_full).astype(jnp.bfloat16)
    query = projected[:, :D]
    pairs_local = projected[:, D:]

    def gather_pairs():
        return lax.all_gather(pairs_local, "ctx", axis=0, tiled=True)

    pairs_all = gather_pairs()
    per_group = min(HEADS, max(1, 512 // tok_count))
    groups = HEADS // per_group
    query_groups = query.reshape(tok_count, groups, per_group, HD).transpose(1, 0, 2, 3)

    def scores_for(query_block, key_rows):
        scores = (
            jnp.einsum("tgd,kd->tgk", query_block, key_rows, preferred_element_type=jnp.float32)
            * score_scale
        )
        return jnp.where(allowed[:, None, :], scores, -1e30)

    def forward_group(query_block):
        scores = scores_for(query_block, pairs_all[:, :HD])
        row_top = jnp.max(scores, -1, keepdims=True)
        weights = jnp.exp(scores - row_top)
        totals = jnp.sum(weights, -1, keepdims=True)
        attn_probs = (weights / totals).astype(jnp.bfloat16)
        mixed = jnp.einsum(
            "tgk,kd->tgd", attn_probs, pairs_all[:, HD:], preferred_element_type=jnp.float32
        )
        return (mixed.astype(jnp.bfloat16), (row_top + jnp.log(totals))[..., 0])

    mixed_groups, lse_groups = lax.map(forward_group, query_groups)
    attended = mixed_groups.transpose(1, 0, 2, 3).reshape(tok_count, D)
    branch_one = (
        right_product(attended, lax.all_gather(w_out, ("dp", "ctx"), axis=0, tiled=True)) + bias_out
    )
    middle = tokens + branch_one
    norm_two, factor_two = normalize(middle)
    input_two = (norm_two * gain_two + bias_two).astype(jnp.bfloat16)

    def fold_fc(piece):
        return jnp.dot(input_two, piece, preferred_element_type=jnp.float32)

    def expand_hidden():
        return fold_fc(lax.all_gather(w_fc, ("dp", "ctx"), axis=0, tiled=True)) + bias_fc

    before_gelu = expand_hidden()
    hidden = jax.nn.gelu(before_gelu, approximate=True).astype(jnp.bfloat16)
    branch_two = (
        right_product(hidden, lax.all_gather(w_proj, ("dp", "ctx"), axis=0, tiled=True)) + bias_proj
    )
    output = (middle + branch_two).astype(jnp.bfloat16)
    grad_two = grad_out.astype(jnp.bfloat16)
    columns = grad_two
    grad_hidden = jnp.dot(
        columns,
        lax.all_gather(w_proj, ("dp", "ctx"), axis=0, tiled=True),
        preferred_element_type=jnp.float32,
    )
    inner_back = expand_hidden()
    pairs_back = gather_pairs()
    gelu_pull = jax.vjp(lambda values: jax.nn.gelu(values, approximate=True), inner_back)[1]
    grad_pre = gelu_pull(grad_hidden)[0].astype(jnp.bfloat16)
    grad_input_two = right_product(
        grad_pre, lax.all_gather(w_fc, ("dp", "ctx"), axis=0, tiled=True)
    )
    grad_middle = grad_out + norm_back(grad_input_two * gain_two, norm_two, factor_two)
    grad_branch = grad_middle.astype(jnp.bfloat16)
    columns = grad_branch
    grad_attended = jnp.dot(
        columns,
        lax.all_gather(w_out, ("dp", "ctx"), axis=0, tiled=True),
        preferred_element_type=jnp.float32,
    ).astype(jnp.bfloat16)
    grad_groups = grad_attended.reshape(tok_count, groups, per_group, HD).transpose(1, 0, 2, 3)
    key_back = pairs_back[:, :HD]
    value_back = pairs_back[:, HD:]

    def backward_group(carry, items):
        query_block, grad_block, lse_block = items
        scores = scores_for(query_block, key_back)
        attn_probs = jnp.exp(scores - lse_block[..., None])
        probs_low = attn_probs.astype(jnp.bfloat16)
        grad_prob = jnp.einsum(
            "tgd,kd->tgk", grad_block, value_back, preferred_element_type=jnp.float32
        )
        delta = jnp.sum(attn_probs * grad_prob, -1, keepdims=True)
        grad_score = (attn_probs * (grad_prob - delta)).astype(jnp.bfloat16)
        grad_query = (
            jnp.einsum("tgk,kd->tgd", grad_score, key_back, preferred_element_type=jnp.float32)
            * score_scale
        )
        grad_key = (
            jnp.einsum("tgk,tgd->kd", grad_score, query_block, preferred_element_type=jnp.float32)
            * score_scale
        )
        grad_value = jnp.einsum(
            "tgk,tgd->kd", probs_low, grad_block, preferred_element_type=jnp.float32
        )
        return ((carry[0] + grad_key, carry[1] + grad_value), grad_query)

    start_carry = (
        jnp.zeros((full_length, HD), jnp.float32),
        jnp.zeros((full_length, HD), jnp.float32),
    )
    (grad_keys, grad_values), grad_query_groups = lax.scan(
        backward_group, start_carry, (query_groups, grad_groups, lse_groups)
    )
    grad_pairs = lax.psum_scatter(
        jnp.concatenate([grad_keys, grad_values], 1), "ctx", scatter_dimension=0, tiled=True
    )
    grad_query = grad_query_groups.transpose(1, 0, 2, 3).reshape(tok_count, D)
    grad_projected = jnp.concatenate([grad_query, grad_pairs], 1).astype(jnp.bfloat16)
    grad_input_one = right_product(
        grad_projected, lax.all_gather(w_attn, ("dp", "ctx"), axis=0, tiled=True)
    )
    grad_tokens = grad_middle + norm_back(grad_input_one * gain_one, norm_one, factor_one)
    rows_in = input_one
    rows_grad = grad_branch
    attn_grads = lax.psum_scatter(
        jnp.concatenate(
            [token_product(rows_in, grad_projected), token_product(rows_grad, attended)], 1
        ),
        ("dp", "ctx"),
        scatter_dimension=0,
        tiled=True,
    )
    rows_in = input_two
    rows_grad = grad_two
    mlp_grads = lax.psum_scatter(
        jnp.concatenate([token_product(rows_in, grad_pre), token_product(rows_grad, hidden)], 1),
        ("dp", "ctx"),
        scatter_dimension=0,
        tiled=True,
    )
    projected_float = grad_projected.astype(jnp.float32)
    summed = (
        lax.psum_scatter(
            jnp.sum(grad_input_one * norm_one, 0), ("dp", "ctx"), scatter_dimension=0, tiled=True
        ),
        lax.psum_scatter(
            jnp.sum(grad_input_one, 0), ("dp", "ctx"), scatter_dimension=0, tiled=True
        ),
        lax.psum_scatter(
            jnp.sum(projected_float[:, :D], 0), ("dp", "ctx"), scatter_dimension=0, tiled=True
        ),
        lax.psum_scatter(
            jnp.sum(grad_branch.astype(jnp.float32), 0),
            ("dp", "ctx"),
            scatter_dimension=0,
            tiled=True,
        ),
        lax.psum_scatter(
            jnp.sum(grad_input_two * norm_two, 0), ("dp", "ctx"), scatter_dimension=0, tiled=True
        ),
        lax.psum_scatter(
            jnp.sum(grad_input_two, 0), ("dp", "ctx"), scatter_dimension=0, tiled=True
        ),
        lax.psum_scatter(
            jnp.sum(grad_pre.astype(jnp.float32), 0), ("dp", "ctx"), scatter_dimension=0, tiled=True
        ),
        lax.psum_scatter(
            jnp.sum(grad_two.astype(jnp.float32), 0), ("dp", "ctx"), scatter_dimension=0, tiled=True
        ),
    )
    value_grad = lax.psum(jnp.sum(projected_float[:, D + HD :], 0), ("dp", "ctx"))
    split_at = D + 2 * HD
    return (
        output[None],
        grad_tokens.astype(jnp.bfloat16)[None],
        summed[0],
        summed[1],
        attn_grads[:, :split_at],
        summed[2],
        value_grad,
        attn_grads[:, split_at:],
        summed[3],
        summed[4],
        summed[5],
        mlp_grads[:, :FF],
        summed[6],
        mlp_grads[:, FF:],
        summed[7],
    )


def solution(mesh):
    in_specs = (
        P("dp", "ctx", None),
        P("dp", "ctx", None),
        P("dp"),
        P("dp", None),
        P("dp", None),
        P(("dp", "ctx")),
        P(("dp", "ctx")),
        P(("dp", "ctx"), None),
        P(("dp", "ctx")),
        P(),
        P(("dp", "ctx"), None),
        P(("dp", "ctx")),
        P(("dp", "ctx")),
        P(("dp", "ctx")),
        P(("dp", "ctx"), None),
        P(("dp", "ctx")),
        P(("dp", "ctx"), None),
        P(("dp", "ctx")),
    )
    out_specs = (
        P("dp", "ctx", None),
        P("dp", "ctx", None),
        P(("dp", "ctx")),
        P(("dp", "ctx")),
        P(("dp", "ctx"), None),
        P(("dp", "ctx")),
        P(),
        P(("dp", "ctx"), None),
        P(("dp", "ctx")),
        P(("dp", "ctx")),
        P(("dp", "ctx")),
        P(("dp", "ctx"), None),
        P(("dp", "ctx")),
        P(("dp", "ctx"), None),
        P(("dp", "ctx")),
    )
    return jax.shard_map(local, mesh=mesh, in_specs=in_specs, out_specs=out_specs, check_vma=False)
```

profile of v0, /device:TPU:0, one launch (start us, length us, event | category | flops | bytes accessed | tf_op | source)
XLA Modules:
  0.0 1646.6 jit_solution(12228762255937724197)
XLA Ops:
  14.7 11.8 gather_fusion
  29.4 68.9 %all-reduce.19 = (f32[768]{0:T(1024)S(1)}, f32[768]{0:T(1024)S(1)}, f32[768]{0:T(1024)S(1)}, f32[768]{0:T(1024)}, f32[3072]{0:T(1024)}, /*index=5*/f32[768]{0:T(1024)}, f32[768]{0:T(1024)}) all-reduce(f32[768]{0:T(1024)S(1)} %dynamic-update-slice.2, f32[768]{0:T(1024)S(1)} %dynamic-update-slice.1, ...), channel_id=1, replica_groups=mesh['dp'=16,'ctx'=8] {'dp','ctx'}, use_global_device_ids=true, to_apply=%add.2 | all-reduce | flops 7680 | bytes 61440
  98.4 210.1 %all-gather.11.cloned.1.call-done = bf16[128,6,768]{2,1,0:T(8,128)(2,1)} async-done(((bf16[1,6,768]{2,1,0:T(8,128)(2,1)}), bf16[128,6,768]{2,1,0:T(8,128)(2,1)}) %all-gather.11.cloned.1.call-update) | async-done | bytes 1179664 | tf_op jit(solution)/shard_map/all_gather | solution.py:137
  308.5 3.2 reshape.224
  311.7 298.2 %all-gather.9.cloned.1.call-done = bf16[128,6,896]{2,1,0:T(8,128)(2,1)} async-done(((bf16[1,6,896]{2,1,0:T(8,128)(2,1)}), bf16[128,6,896]{2,1,0:T(8,128)(2,1)}) %all-gather.9.cloned.1.call-update) | async-done | bytes 1376272 | tf_op jit(solution)/shard_map/all_gather | solution.py:100
  613.5 35.4 %all_gather.49 = bf16[2048,128]{1,0:T(8,128)(2,1)S(1)} all-gather(bf16[256,128]{1,0:T(8,128)(2,1)S(1)} %slice.51), channel_id=1, replica_groups=mesh['dp'=16,'ctx'=8] {'ctx'}, dimensions={0}, use_global_device_ids=true | all-gather | bytes 589824 | tf_op jit(solution)/shard_map/all_gather | solution.py:109
  650.8 43.1 %while.28 = (s32[]{:T(128)}, bf16[6,256,2,64]{1,3,2,0:T(8,128)(2,1)}, f32[6,256,2]{1,2,0:T(2,128)}, bf16[6,256,2,64]{1,3,2,0:T(8,128)(2,1)S(1)}, bf16[2048,128]{...) while((s32[]{:T(128)}, ...), condition=%wide.region_5.6_spmd.clone, body=%wide.region_2.0_spmd.clone.sunk | while | flops 284196352 | bytes 17469596 | solution.py:134
  696.9 226.0 %all-gather.13.cloned.1.call-done = bf16[128,6,3072]{2,1,0:T(8,128)(2,1)} async-done(((bf16[1,6,3072]{2,1,0:T(8,128)(2,1)}), bf16[128,6,3072]{2,1,0:T(8,128)(2,1)}) %all-gather.13.cloned.1.call-update) | async-done | bytes 4718608 | tf_op jit(solution)/shard_map/all_gather | solution.py:147
  922.9 7.7 reshape.226
  930.6 5.5 convolution_add_fusion
  936.1 297.8 %all-gather.15.cloned.1.call-done = bf16[128,6,3072]{2,1,0:T(8,128)(2,1)} async-done(((bf16[1,6,3072]{2,1,0:T(8,128)(2,1)}), bf16[128,6,3072]{2,1,0:T(8,128)(2,1)}) %all-gather.15.cloned.1.call-update) | async-done | bytes 4718608 | tf_op jit(solution)/shard_map/all_gather | solution.py:152
  1233.9 7.8 reshape.228
  1241.6 7.2 convert_reduce_fusion
  1248.9 5.2 multiply_reduce_fusion.1
  1259.0 65.4 %while.29 = (s32[]{:T(128)}, f32[2048,64]{0,1:T(8,128)S(1)}, f32[2048,64]{0,1:T(8,128)S(1)}, bf16[6,256,2,64]{1,3,2,0:T(8,128)(2,1)}, bf16[6,256,2,64]{1,3,2,0:T...) while((s32[]{:T(128)}, f32[2048,64]{0,1:T(8,128)S(1)}, ...), condition=%wide.region_12.13_spmd.clone, body=%wide.region_10.12_spmd.clone.sunk | while | flops 684359168 | bytes 35813564 | solution.py:208
  1262.7 2.5 multiply_reduce_fusion.7
  1284.5 2.5 multiply_reduce_fusion.7
  1325.6 3.0 fusion.87
  1333.1 6.8 pad_maximum_fusion
  1339.9 59.5 %reduce-scatter.2.cloned.1.call-done = f32[256,128]{0,1:T(8,128)} async-done(((f32[2048,128]{0,1:T(8,128)}), f32[256,128]{0,1:T(8,128)}) %reduce-scatter.2.cloned.1.call-update) | async-done | bytes 131088 | tf_op jit(solution)/shard_map/reduce_scatter | solution.py:211
  1401.3 2.7 pad_maximum_fusion.1
  1407.4 66.1 %all-reduce.18 = (f32[768]{0:T(1024)S(1)}, f32[768]{0:T(1024)S(1)}, f32[768]{0:T(1024)S(1)}, f32[768]{0:T(1024)S(1)}, f32[64]{0:T(128)}, /*index=5*/f32[768]{0:T...) all-reduce(f32[768]{0:T(1024)S(1)} %dynamic-update-slice.7, ...), channel_id=1, replica_groups=mesh['dp'=16,'ctx'=8] {'dp','ctx'}, use_global_device_ids=true, to_apply=%add.7 | all-reduce | flops 9280 | bytes 74240
  1479.3 6.1 fusion.53
  1485.3 149.8 %all-reduce.23.cloned.1.call-done = (f32[768,1664]{1,0:T(8,128)}, f32[768,6144]{1,0:T(8,128)}) async-done(((f32[768,1664]{1,0:T(8,128)}, f32[768,6144]{1,0:T(8,128)}), (f32[768,1664]{1,0:T(8,128)}, f32[768,6144]{1,0:T(8,128)})) %all-reduce.23.cloned.1.call-update) | async-done | bytes 23986192
  (269 shorter events, 146.9 us)
Async XLA Ops:
  7.2 301.3 %all-gather.11.cloned.1.call-start = ((), (), s32[]{:S(2)}) async-start(), calls=%async_computation.3 | async-start | bytes 1585152 | tf_op jit(solution)/shard_map/all_gather | solution.py:137
  7.9 602.0 %all-gather.9.cloned.1.call-start = ((), (), s32[]{:S(2)}) async-start(), calls=%async_computation.2 | async-start | bytes 1849344 | tf_op jit(solution)/shard_map/all_gather | solution.py:100
  8.7 914.2 %all-gather.13.cloned.1.call-start = ((), (), s32[]{:S(2)}) async-start(), calls=%async_computation.4 | async-start | bytes 6340608 | tf_op jit(solution)/shard_map/all_gather | solution.py:147
  9.4 1224.5 %all-gather.15.cloned.1.call-start = ((), (), s32[]{:S(2)}) async-start(), calls=%async_computation.5 | async-start | bytes 6340608 | tf_op jit(solution)/shard_map/all_gather | solution.py:152
  10.0 1389.4 %reduce-scatter.2.cloned.1.call-start = ((), (), s32[]{:S(2)}) async-start(), calls=%async_computation.1 | async-start | bytes 1179648 | tf_op jit(solution)/shard_map/reduce_scatter | solution.py:211
  12.5 599.8 %copy-start.24 = (f32[256]{0:T(256)}, f32[256]{0:T(256)S(1)}, u32[]{:S(2)}) copy-start(f32[256]{0:T(256)S(1)} %broadcast_multiply_fusion.5) | copy-start | bytes 3076
  13.8 598.6 %copy-start.31 = (f32[256]{0:T(256)}, f32[256]{0:T(256)S(1)}, u32[]{:S(2)}) copy-start(f32[256]{0:T(256)S(1)} %add_rsqrt_fusion.1) | copy-start | bytes 3076
  14.7 83.6 %copy-start.38 = (f32[64]{0:T(128)S(1)}, f32[64]{0:T(128)}, u32[]{:S(2)}) copy-start(f32[64]{0:T(128)} %param.31) | copy-start | bytes 772
  26.5 585.9 %copy-start.3 = (bf16[1,256,768]{2,1,0:T(8,128)(2,1)S(1)}, bf16[1,256,768]{2,1,0:T(8,128)(2,1)}, u32[]{:S(2)}) copy-start(bf16[1,256,768]{2,1,0:T(8,128)(2,1)} %param.22) | copy-start | bytes 1179652
  98.3 514.8 %copy-start.22 = (f32[768]{0:T(1024)}, f32[768]{0:T(1024)S(1)}, u32[]{:S(2)}) copy-start(f32[768]{0:T(1024)S(1)} %get-tuple-element.326) | copy-start | bytes 9220
  98.3 514.8 %copy-start.33 = (f32[768]{0:T(1024)}, f32[768]{0:T(1024)S(1)}, u32[]{:S(2)}) copy-start(f32[768]{0:T(1024)S(1)} %get-tuple-element.325) | copy-start | bytes 9220
  696.6 552.3 %copy-start.20 = (f32[256]{0:T(256)}, f32[256]{0:T(256)S(1)}, u32[]{:S(2)}) copy-start(f32[256]{0:T(256)S(1)} %broadcast_multiply_fusion.4) | copy-start | bytes 3076
  696.8 552.0 %copy-start.28 = (f32[256]{0:T(256)}, f32[256]{0:T(256)S(1)}, u32[]{:S(2)}) copy-start(f32[256]{0:T(256)S(1)} %add_rsqrt_fusion) | copy-start | bytes 3076
  696.8 233.8 %copy-start.15 = (f32[768]{0:T(1024)S(1)}, f32[768]{0:T(1024)}, u32[]{:S(2)}) copy-start(f32[768]{0:T(1024)} %get-tuple-element.330) | copy-start | bytes 9220
  696.9 233.8 %copy-start.18 = (f32[768]{0:T(1024)S(1)}, f32[768]{0:T(1024)}, u32[]{:S(2)}) copy-start(f32[768]{0:T(1024)} %get-tuple-element.329) | copy-start | bytes 9220
  696.9 233.8 %copy-start.39 = (f32[3072]{0:T(1024)S(1)}, f32[3072]{0:T(1024)}, u32[]{:S(2)}) copy-start(f32[3072]{0:T(1024)} %get-tuple-element.328) | copy-start | bytes 36868
  936.1 305.5 %copy-start.10 = (bf16[1,256,768]{2,1,0:T(8,128)(2,1)S(1)}, bf16[1,256,768]{2,1,0:T(8,128)(2,1)}, u32[]{:S(2)}) copy-start(bf16[1,256,768]{2,1,0:T(8,128)(2,1)} %param.23) | copy-start | bytes 1179652
  1325.5 309.6 %all-reduce.23.cloned.1.call-start = ((), (), s32[]{:S(2)}) async-start(), calls=%async_computation.6 | async-start | bytes 47972352
  1333.0 67.5 %copy-start.8 = (bf16[6,256,2,64]{1,3,2,0:T(8,128)(2,1)S(1)}, bf16[6,256,2,64]{1,3,2,0:T(8,128)(2,1)}, u32[]{:S(2)}) copy-start(bf16[6,256,2,64]{1,3,2,0:T(8,128)(2,1)} %get-tuple-element.104) | copy-start | bytes 1179652
  1333.1 67.4 %copy-start.23 = (f32[768]{0:T(1024)S(1)}, f32[768]{0:T(1024)}, u32[]{:S(2)}) copy-start(f32[768]{0:T(1024)} %copy-done.22) | copy-start | bytes 9220
  1333.1 67.4 %copy-start.25 = (f32[256]{0:T(256)S(1)}, f32[256]{0:T(256)}, u32[]{:S(2)}) copy-start(f32[256]{0:T(256)} %copy-done.24) | copy-start | bytes 3076
  1333.1 67.4 %copy-start.32 = (f32[256]{0:T(256)S(1)}, f32[256]{0:T(256)}, u32[]{:S(2)}) copy-start(f32[256]{0:T(256)} %copy-done.31) | copy-start | bytes 3076
  1333.1 67.4 %copy-start.34 = (f32[768]{0:T(1024)S(1)}, f32[768]{0:T(1024)}, u32[]{:S(2)}) copy-start(f32[768]{0:T(1024)} %copy-done.33) | copy-start | bytes 9220
  1479.3 160.5 %copy-start.1 = (s32[1,2048]{1,0:T(1,128)S(1)}, s32[1,2048]{1,0:T(1,128)}, u32[]{:S(2)}) copy-start(s32[1,2048]{1,0:T(1,128)} %param.26) | copy-start | bytes 24580
  (35 other events, 203.9 us)
Sparse Core Ops, SparseCore 0:
  9.7 298.7 all-gather.10
  310.2 299.6 all-gather.8
  611.6 311.2 all-gather.12
  924.4 309.3 all-gather.14
  1325.6 73.7 reduce-scatter.1
  1406.1 228.8 all-reduce.22
where the time goes:
time: 1650 us
  waiting for transfers between devices  1240 us (75%)
  blocking collectives  170 us (10%)
  matrix products  110 us (7%)
  local copies, waits for them, and re-layouts  56 us (3%)
  other arithmetic  49.8 us (3%)
    all_gather x1, waiting for transfers between devices, local(): lax.all_gather(w_attn, ('dp', 'ctx'), axis=0, tiled=True)  298 us
    all_gather x1, waiting for transfers between devices, local(): lax.all_gather(w_proj, ('dp', 'ctx'), axis=0, tiled=True)  298 us
    all_gather x1, waiting for transfers between devices, expand_hidden(): lax.all_gather(w_fc, ('dp', 'ctx'), axis=0, tiled=True)  226 us
    all_gather x1, waiting for transfers between devices, local(): lax.all_gather(w_out, ('dp', 'ctx'), axis=0, tiled=True)  210 us
    unnamed x7, waiting for transfers between devices  152 us
    unnamed x2, blocking collectives  135 us
    reduce_scatter x1, waiting for transfers between devices, local(): lax.psum_scatter(jnp.concatenate([grad_keys, grad_values], 1), 'ctx', sca...  59.5 us
    all_gather x1, blocking collectives, gather_pairs(): return lax.all_gather(pairs_local, 'ctx', axis=0, tiled=True)  35.4 us
  transfers between devices with their start and end apart: 6, of which 6 were waited for; matrix products, arithmetic and copies ran while one was open for 7% of the time, Pallas kernels for 0%

commit v1 on v0

v1 whole, which is shorter than its diff:
```python
import functools

import jax
import jax.numpy as jnp
import numpy as np
from jax import lax
from jax.experimental import pallas as pl
from jax.experimental.pallas import tpu as pltpu
from jax.sharding import Mesh
from jax.sharding import PartitionSpec as P

D = 768
HEADS = 12
HD = 64
FF = 3072
TOK = 256
LENGTH = 2048
BLOCK = 128
BLOCKS = 16
PAIRS = 6
ROWS = 48
COLS = 384
NEG = -1e30

AXES = ("x", "zl", "core", "y", "zh")
SIZES = (4, 2, 2, 4, 2)
DP = ("x", "zl", "core")
CTX = ("y", "zh")

f32 = jnp.float32
bf16 = jnp.bfloat16


def route(dx=0, dy=0, dz=0, dc=0):
    pairs = []
    for device in range(128):
        x, zl, core, y, zh = (int(v) for v in np.unravel_index(device, SIZES))
        z = (zh * 2 + zl + dz) % 4
        target = ((x + dx) % 4, z % 2, core ^ dc, (y + dy) % 4, z // 2)
        pairs.append((device, int(np.ravel_multi_index(target, SIZES))))
    return pairs


def send(value, **shift):
    return lax.ppermute(value, AXES, route(**shift))


def mm(left, right):
    return lax.dot_general(left, right, (((1,), (0,)), ((), ())), preferred_element_type=f32)


def mm_nt(left, right):
    return lax.dot_general(left, right, (((1,), (1,)), ((), ())), preferred_element_type=f32)


def normalize(values):
    center = values - jnp.mean(values, -1, keepdims=True)
    spread = jnp.mean(center * center, -1, keepdims=True)
    factor = lax.rsqrt(spread + 1e-05)
    return center * factor, factor


def norm_back(grad_normed, normed, factor):
    return factor * (
        grad_normed
        - jnp.mean(grad_normed, -1, keepdims=True)
        - normed * jnp.mean(grad_normed * normed, -1, keepdims=True)
    )


def split_low(values):
    high = values.astype(bf16)
    return high, (values - high.astype(f32)).astype(bf16)


def first_kernel(x_ref, early_ref, vbias_ref, one_ref, kv_ref, vec_ref):
    turned = early_ref[:, BLOCK:].astype(f32).T
    vec = turned[0:16] + turned[16:32] + turned[32:48]
    vec_ref[...] = vec
    normed, _ = normalize(x_ref[...].astype(f32))
    one = (normed * vec[0:1] + vec[1:2]).astype(bf16)
    one_ref[...] = one
    bias = jnp.concatenate([jnp.zeros((1, HD), f32), vbias_ref[...]], 1)
    kv_ref[...] = (mm(one, early_ref[:, :BLOCK]) + bias).astype(bf16)


def block_plan(meta, b):
    place = meta[32 + b]
    length = meta[34]
    start = place * BLOCK
    first = jnp.int32(0)
    for f in range(3):
        bound = meta[35 + f]
        first = jnp.where(bound <= start, jnp.maximum(first, bound), first)
    low = first // BLOCK
    high = jnp.minimum(place - 1, (length - 1) // BLOCK)
    return place, low, jnp.maximum(high - low + 1, 0) + 1


def block_bias(meta, place, initial):
    lane = lax.broadcasted_iota(jnp.int32, (1, 2 * BLOCK), 1)
    query = place * BLOCK + (lane & (BLOCK - 1))
    first = jnp.zeros_like(query)
    for f in range(3):
        bound = meta[35 + f]
        first = jnp.where(bound <= query, jnp.maximum(first, bound), first)
    last = jnp.minimum(query, meta[34] - 1)
    key = initial * BLOCK + lax.broadcasted_iota(jnp.int32, (BLOCK, 2 * BLOCK), 0)
    allowed = ((key >= first) & (key <= last)) | (key == query)
    return jnp.where(allowed, 0.0, NEG)


def fold_heads(block):
    turned = block.T
    return jnp.concatenate([turned[:HD], turned[HD:]], 1)


def unfold_heads(wide):
    return jnp.concatenate([wide[:, :BLOCK], wide[:, BLOCK:]], 0).T


def forward_kernel(
    meta, one_ref, wq_ref, vec_ref, kv_ref, q_ref, att_ref, lse_ref, qt, vt, scores, mixed
):
    q = (mm(one_ref[...], wq_ref[...]) + vec_ref[2:3]).astype(bf16)
    q_ref[...] = q
    for b in range(2):
        for p in range(PAIRS):
            block = q[b * BLOCK : (b + 1) * BLOCK, p * BLOCK : (p + 1) * BLOCK].astype(f32) * 0.125
            qt[b, p, :HD] = fold_heads(block).astype(bf16)
            qt[b, p, HD:] = jnp.zeros((HD, 2 * BLOCK), bf16)
    for k in range(BLOCKS):
        vt[k] = kv_ref[k * BLOCK : (k + 1) * BLOCK].astype(f32).T[HD:].astype(bf16)

    for b in range(2):
        place, low, count = block_plan(meta, b)

        def initial_of(t):
            return jnp.where(t == count - 1, place, low + t)

        def score_step(t, tops):
            initial = initial_of(t)
            stored = meta[16 + initial]
            rows = kv_ref[pl.ds(pl.multiple_of(stored * BLOCK, BLOCK), BLOCK)]
            bias = block_bias(meta, place, initial)
            new = []
            for p in range(PAIRS):
                value = mm(rows, qt[b, p]) + bias
                scores[t, p] = value
                new.append(jnp.maximum(tops[p], jnp.max(value.reshape(16, 8, 2 * BLOCK), 0)))
            return tuple(new)

        tops = lax.fori_loop(
            0, count, score_step, tuple(jnp.full((8, 2 * BLOCK), NEG, f32) for _ in range(PAIRS))
        )
        tops = tuple(jnp.max(top, 0, keepdims=True) for top in tops)
        mixed[...] = jnp.zeros_like(mixed)

        def mix_step(t, sums):
            stored = meta[16 + initial_of(t)]
            values = vt[stored]
            new = []
            for p in range(PAIRS):
                weight = jnp.exp(scores[t, p] - tops[p])
                new.append(sums[p] + jnp.sum(weight.reshape(16, 8, 2 * BLOCK), 0))
                mixed[p] += mm(values, weight.astype(bf16))
            return tuple(new)

        sums = lax.fori_loop(
            0, count, mix_step, tuple(jnp.zeros((8, 2 * BLOCK), f32) for _ in range(PAIRS))
        )
        for p in range(PAIRS):
            total = jnp.sum(sums[p], 0, keepdims=True)
            lse_ref[b, p] = jnp.broadcast_to(tops[p] + jnp.log(total), (8, 2 * BLOCK))
            att_ref[b * BLOCK : (b + 1) * BLOCK, p * BLOCK : (p + 1) * BLOCK] = unfold_heads(
                mixed[p] / total
            ).astype(bf16)


def backward_kernel(
    meta,
    q_ref,
    do_ref,
    att_ref,
    lse_ref,
    kv_ref,
    one_ref,
    gq_ref,
    gwq_ref,
    dkv_ref,
    qt,
    dot_,
    qn,
    don,
    kt,
    delta,
    dq,
    dkv,
):
    zeros = jnp.zeros((BLOCK, HD), f32)
    for b in range(2):
        for p in range(PAIRS):
            span = (slice(b * BLOCK, (b + 1) * BLOCK), slice(p * BLOCK, (p + 1) * BLOCK))
            block = q_ref[span].astype(f32) * 0.125
            grad = do_ref[span].astype(f32)
            out = att_ref[span].astype(f32)
            qt[b, p, :HD] = fold_heads(block).astype(bf16)
            qt[b, p, HD:] = jnp.zeros((HD, 2 * BLOCK), bf16)
            wide = fold_heads(grad)
            dot_[b, p, :HD] = jnp.zeros((HD, 2 * BLOCK), bf16)
            dot_[b, p, HD:] = wide.astype(bf16)
            delta[b, p] = jnp.broadcast_to(
                jnp.sum(wide * fold_heads(out), 0, keepdims=True), (8, 2 * BLOCK)
            )
            qn[b, p, :BLOCK] = jnp.concatenate([block[:, :HD], zeros], 1).astype(bf16)
            qn[b, p, BLOCK:] = jnp.concatenate([block[:, HD:], zeros], 1).astype(bf16)
            don[b, p, :BLOCK] = jnp.concatenate([zeros, grad[:, :HD]], 1).astype(bf16)
            don[b, p, BLOCK:] = jnp.concatenate([zeros, grad[:, HD:]], 1).astype(bf16)
    for k in range(BLOCKS):
        kt[k] = kv_ref[k * BLOCK : (k + 1) * BLOCK].astype(f32).T[:HD].astype(bf16)
    dkv[...] = jnp.zeros_like(dkv)

    for b in range(2):
        place, low, count = block_plan(meta, b)
        dq[...] = jnp.zeros_like(dq)

        def step(t, carry):
            initial = jnp.where(t == count - 1, place, low + t)
            stored = meta[16 + initial]
            rows = kv_ref[pl.ds(pl.multiple_of(stored * BLOCK, BLOCK), BLOCK)]
            keys = kt[stored]
            bias = block_bias(meta, place, initial)
            total = dkv[stored]
            for p in range(PAIRS):
                value = mm(rows, qt[b, p]) + bias
                probs = jnp.exp(value - lse_ref[b, p, 0:1])
                grad = probs * (mm(rows, dot_[b, p]) - delta[b, p, 0:1])
                low_probs = probs.astype(bf16)
                low_grad = grad.astype(bf16)
                dq[p] += mm(keys, low_grad)
                total = total + mm(low_grad, qn[b, p]) + mm(low_probs, don[b, p])
            dkv[stored] = total
            return carry

        lax.fori_loop(0, count, step, 0)
        for p in range(PAIRS):
            gq_ref[b * BLOCK : (b + 1) * BLOCK, p * BLOCK : (p + 1) * BLOCK] = unfold_heads(
                dq[p] * 0.125
            ).astype(bf16)
    for k in range(BLOCKS):
        dkv_ref[k * BLOCK : (k + 1) * BLOCK] = dkv[k].astype(bf16)
    gwq_ref[...] = mm(one_ref[...].T, gq_ref[...]).astype(bf16)


def middle_kernel(meta, *refs):
    fc_parts = refs[0:8]
    proj_parts = refs[8:16]
    x_ref, ct_ref, att_ref, wout_ref, vec_ref, fcb_ref = refs[16:22]
    out_ref, gmid_ref, gatt_ref, gwout_ref, sums_ref, fcsum_ref = refs[22:28]
    keep_fc, send_fc, keep_proj, send_proj = refs[28:32]
    (wf, wg, gf, gg, in_sem, out_sem, x2, x2t, gtt, branch, gin, mid) = refs[32:]
    px, py, pz, pc = meta[38], meta[39], meta[40], meta[41]

    def places(dx, dc, zl, h):
        row = lax.rem(px + dx, 4) * 192 + zl * 96 + (pc if dc == 0 else 1 - pc) * ROWS
        return pl.ds(pl.multiple_of(row, 16), ROWS), lax.rem(2 * h + zl - pz + 4, 4)

    def fetch(c, slot):
        dy, h = c // 2, lax.rem(c, 2)
        for dx in range(4):
            for dc in range(2):
                for zl in range(2):
                    rows, dz = places(dx, dc, zl, h)
                    pltpu.make_async_copy(
                        fc_parts[dx * 2 + dc].at[dy, dz], wf.at[slot, rows], in_sem.at[slot, 0]
                    ).start()
        for k in range(4):

            @pl.when(dy == k)
            def _():
                for dx in range(4):
                    for dc in range(2):
                        for zl in range(2):
                            rows, dz = places(dx, dc, zl, h)
                            pltpu.make_async_copy(
                                proj_parts[k * 2 + dc].at[dx, dz],
                                wg.at[slot, rows],
                                in_sem.at[slot, 1],
                            ).start()

    def fetched(slot):
        pltpu.make_async_copy(wf.at[slot], wf.at[slot], in_sem.at[slot, 0]).wait()
        pltpu.make_async_copy(wg.at[slot], wg.at[slot], in_sem.at[slot, 1]).wait()

    def store(c, slot):
        dy, h = c // 2, lax.rem(c, 2)
        for dx in range(4):
            for dc in range(2):
                for zl in range(2):
                    rows, dz = places(dx, dc, zl, h)
                    fc_out = send_fc if dc else keep_fc
                    proj_out = send_proj if dc else keep_proj
                    pltpu.make_async_copy(
                        gf.at[slot, rows], fc_out.at[dx, dy, dz], out_sem.at[slot, 0]
                    ).start()
                    pltpu.make_async_copy(
                        gg.at[slot, rows], proj_out.at[dy, dx, dz], out_sem.at[slot, 1]
                    ).start()

    def stored(slot):
        pltpu.make_async_copy(gf.at[slot], gf.at[slot], out_sem.at[slot, 0]).wait()
        pltpu.make_async_copy(gg.at[slot], gg.at[slot], out_sem.at[slot, 1]).wait()

    fetch(0, 0)
    vec = vec_ref[...]
    att = att_ref[...]
    cot = ct_ref[...]
    middle = x_ref[...].astype(f32) + (mm_nt(att, wout_ref[...]) + vec[3:4])
    mid[...] = middle
    normed, factor = normalize(middle)
    two = (normed * vec[4:5] + vec[5:6]).astype(bf16)
    x2[...] = two
    x2t[...] = two.astype(f32).T.astype(bf16)
    gtt[...] = cot.astype(f32).T.astype(bf16)
    branch[...] = jnp.zeros_like(branch)
    gin[...] = jnp.zeros_like(gin)

    def chunk(c, carry):
        slot = lax.rem(c, 2)

        @pl.when(c + 1 < 8)
        def _():
            fetch(c + 1, 1 - slot)

        fetched(slot)
        col = (lax.rem(py + c // 2, 4) * 2 + lax.rem(c, 2)) * COLS
        span = pl.ds(pl.multiple_of(col, BLOCK), COLS)
        w_fc = wf[slot]
        w_proj = wg[slot]
        pre = mm(x2[...], w_fc) + fcb_ref[:, span]
        square = pre * pre
        tanh = jnp.tanh(0.7978845608028654 * (pre + 0.044715 * (pre * square)))
        half = 0.5 * (1.0 + tanh)
        hidden = (pre * half).astype(bf16)
        slope = half + (0.5 * pre) * (1.0 - tanh * tanh) * (
            0.7978845608028654 + (3 * 0.044715 * 0.7978845608028654) * square
        )
        branch[...] += mm_nt(hidden, w_proj)
        grad_pre = (mm(ct_ref[...], w_proj) * slope).astype(bf16)
        gin[...] += mm_nt(grad_pre, w_fc)
        fcsum_ref[:, span] = jnp.sum(grad_pre.astype(f32), 0, keepdims=True)

        @pl.when(c >= 2)
        def _():
            stored(slot)

        gf[slot] = mm(x2t[...], grad_pre).astype(bf16)
        gg[slot] = mm(gtt[...], hidden).astype(bf16)
        store(c, slot)
        return carry

    lax.fori_loop(0, 8, chunk, 0)
    middle = mid[...]
    cot = ct_ref[...].astype(f32)
    out_ref[...] = (middle + (branch[...] + vec[6:7])).astype(bf16)
    normed, factor = normalize(middle)
    grad_two = gin[...]
    grad_middle = cot + norm_back(grad_two * vec[4:5], normed, factor)
    gmid_ref[...] = grad_middle
    grad_branch = grad_middle.astype(bf16)
    gatt_ref[...] = mm(grad_branch, wout_ref[...]).astype(bf16)
    turned = grad_branch.astype(f32).T.astype(bf16)
    gwout_ref[...] = mm(turned, att).astype(bf16)
    sums_ref[...] = jnp.concatenate(
        [
            jnp.sum(grad_branch.astype(f32), 0, keepdims=True),
            jnp.sum(grad_two * normed, 0, keepdims=True),
            jnp.sum(grad_two, 0, keepdims=True),
            jnp.sum(cot, 0, keepdims=True),
            jnp.zeros((4, D), f32),
        ],
        0,
    )
    stored(0)
    stored(1)


def last_kernel(
    x_ref, one_ref, gq_ref, dkv_ref, gmid_ref, wq_ref, early_ref, vec_ref, sums_ref, fc4_ref,
    gx_ref, pack_ref,
):
    gkv = jnp.sum(dkv_ref[...].astype(f32), 0).astype(bf16)
    gq = gq_ref[...]
    vec = vec_ref[...]
    grad_one = mm_nt(gq, wq_ref[...]) + mm_nt(gkv, early_ref[:, :BLOCK])
    normed, factor = normalize(x_ref[...].astype(f32))
    gx_ref[...] = (gmid_ref[...] + norm_back(grad_one * vec[0:1], normed, factor)).astype(bf16)
    pack_ref[:, :BLOCK] = mm(one_ref[...].astype(f32).T.astype(bf16), gkv).astype(bf16)
    sums = sums_ref[...]
    rows = jnp.concatenate(
        [
            jnp.sum(grad_one * normed, 0, keepdims=True),
            jnp.sum(grad_one, 0, keepdims=True),
            jnp.sum(gq.astype(f32), 0, keepdims=True),
            sums[0:4],
            fc4_ref[0:4],
            jnp.zeros((5, D), f32),
        ],
        0,
    )
    high, low = split_low(rows)
    value = jnp.sum(gkv.astype(f32), 0, keepdims=True)[:, HD:]
    value_high, value_low = split_low(value)
    lane = lax.broadcasted_iota(jnp.int32, (16, HD), 1)
    mine = (lane & 15) == lax.broadcasted_iota(jnp.int32, (16, HD), 0)
    group = lax.broadcasted_iota(jnp.int32, (HD, D), 0) // 16
    spread = jnp.where(group == lax.broadcasted_iota(jnp.int32, (HD, D), 1) % 6, 1.0, 0.0).astype(bf16)
    put_high = mm(jnp.where(mine, value_high.astype(f32), 0.0).astype(bf16), spread)
    put_low = mm(jnp.where(mine, value_low.astype(f32), 0.0).astype(bf16), spread)
    packed = jnp.concatenate(
        [high.astype(f32), low.astype(f32), put_high, put_low, jnp.zeros((64, D), f32)], 0
    )
    pack_ref[:, BLOCK:] = packed.T.astype(bf16)


def whole(count):
    return [pl.BlockSpec(memory_space=pltpu.VMEM)] * count


def shape(*dims, dtype=bf16):
    return jax.ShapeDtypeStruct(dims, dtype)


def params(mib=56):
    return pltpu.CompilerParams(vmem_limit_bytes=mib * 1024 * 1024)


def cost(flops, moved, exps=0):
    return pl.CostEstimate(flops=flops, bytes_accessed=moved, transcendentals=exps)


SMEM = pl.BlockSpec(memory_space=pltpu.SMEM)
ANY = pl.BlockSpec(memory_space=pl.ANY)


def gather_rows(value):
    copies = jnp.broadcast_to(value[None], (128,) + value.shape)
    return lax.all_to_all(copies, AXES, 0, 0).reshape(D, value.shape[1])


def scatter_rows(value):
    pieces = lax.all_to_all(value.reshape(128, 6, value.shape[1]), AXES, 0, 0)
    return jnp.sum(pieces.astype(f32), 0)


def gather_mlp(w_fc, w_proj):
    both = jnp.concatenate(
        [w_fc.reshape(6, 8, COLS).transpose(1, 0, 2), w_proj.reshape(6, 8, COLS).transpose(1, 0, 2)],
        2,
    )
    block = lax.all_to_all(both, CTX, 0, 0).reshape(ROWS, 2 * COLS)
    ring = [block] + [send(block, dz=-k) for k in (1, 2, 3)]
    fc = jnp.stack([part[:, :COLS] for part in ring])
    proj = jnp.stack([part[:, COLS:] for part in ring])
    fc = jnp.stack([fc] + [send(fc, dy=-k) for k in (1, 2, 3)])
    proj = jnp.stack([proj] + [send(proj, dx=-k) for k in (1, 2, 3)])
    fc_parts = [fc] + [send(fc, dx=-k) for k in (1, 2, 3)]
    proj_parts = [proj] + [send(proj, dy=-k) for k in (1, 2, 3)]
    fc_all, proj_all = [], []
    for part in fc_parts:
        fc_all += [part, send(part, dc=1)]
    for part in proj_parts:
        proj_all += [part, send(part, dc=1)]
    return fc_all, proj_all


def add_all(parts, dtype=bf16):
    total = parts[0].astype(f32)
    for part in parts[1:]:
        total = total + part.astype(f32)
    return total.astype(dtype)


def scatter_mlp(keep_fc, send_fc, keep_proj, send_proj):
    got_fc = send(send_fc, dc=1)
    got_proj = send(send_proj, dc=1)
    fc = [add_all([keep_fc[k], got_fc[k]]) for k in range(4)]
    proj = [add_all([keep_proj[k], got_proj[k]]) for k in range(4)]
    fc = add_all([fc[0]] + [send(fc[k], dx=k) for k in (1, 2, 3)])
    proj = add_all([proj[0]] + [send(proj[k], dy=k) for k in (1, 2, 3)])
    fc = add_all([fc[0]] + [send(fc[k], dy=k) for k in (1, 2, 3)])
    proj = add_all([proj[0]] + [send(proj[k], dx=k) for k in (1, 2, 3)])
    both = [jnp.concatenate([fc[k], proj[k]], 1) for k in range(4)]
    block = add_all([both[0]] + [send(both[k], dz=k) for k in (1, 2, 3)], f32)
    mine = lax.all_to_all(block.reshape(8, 6, 2 * COLS), CTX, 0, 0).transpose(1, 0, 2)
    return mine[:, :, :COLS].reshape(6, FF), mine[:, :, COLS:].reshape(6, FF)


def local(
    layer_input,
    cotangent,
    lengths,
    order,
    files,
    ln1_gain,
    ln1_bias,
    w_attn,
    query_bias,
    value_bias,
    w_out,
    out_bias,
    ln2_gain,
    ln2_bias,
    w_fc,
    fc_bias,
    w_proj,
    proj_bias,
):
    x = layer_input[0]
    cot = cotangent[0]
    px, zl, pc, py, zh = (lax.axis_index(name) for name in AXES)
    own = py * 2 + zh
    order_row = order[0]
    slots = jnp.arange(BLOCKS, dtype=jnp.int32)
    inverse = jnp.sum(jnp.where(order_row[None, :] == slots[:, None], slots[None, :], 0), 1)
    bounds = [jnp.sum((files[0] < f).astype(jnp.int32)) for f in (1, 2, 3)]
    own_places = lax.dynamic_slice_in_dim(order_row, own * 2, 2)
    meta = jnp.concatenate(
        [
            order_row,
            inverse,
            own_places,
            lengths,
            jnp.stack(bounds + [px, py, zh * 2 + zl, pc]).astype(jnp.int32),
        ]
    )

    per_row = jnp.stack(
        [ln1_gain, ln1_bias, query_bias, out_bias, ln2_gain, ln2_bias, proj_bias], 1
    )
    per_row = jnp.concatenate([per_row, fc_bias.reshape(6, 4), jnp.zeros((6, 5), f32)], 1)
    high, rest = split_low(per_row)
    middle, low = split_low(per_row - high.astype(f32))
    early = jnp.concatenate(
        [w_attn[:, D:], high, middle, low, jnp.zeros((6, BLOCK - 48), bf16)], 1
    )
    early = gather_rows(early)
    wq = gather_rows(w_attn[:, :D])
    fc_all, proj_all = gather_mlp(w_fc, w_proj)
    wout = gather_rows(w_out)

    one, kv, vec = pl.pallas_call(
        first_kernel,
        out_shape=[shape(TOK, D), shape(TOK, BLOCK), shape(16, D, dtype=f32)],
        in_specs=whole(3),
        out_specs=whole(3),
        compiler_params=params(),
        cost_estimate=cost(2 * TOK * D * BLOCK, 1_000_000),
        name="first",
    )(x, early, value_bias[None])
    kv_all = lax.all_to_all(
        jnp.broadcast_to(kv[None], (8, TOK, BLOCK)), CTX, 0, 0
    ).reshape(LENGTH, BLOCK)
    fcb = vec[7:11].T.reshape(1, FF)

    wide = (2, PAIRS, BLOCK, 2 * BLOCK)
    q, att, lse = pl.pallas_call(
        forward_kernel,
        out_shape=[shape(TOK, D), shape(TOK, D), shape(2, PAIRS, 8, 2 * BLOCK, dtype=f32)],
        in_specs=[SMEM] + whole(4),
        out_specs=whole(3),
        scratch_shapes=[
            pltpu.VMEM(wide, bf16),
            pltpu.VMEM((BLOCKS, HD, BLOCK), bf16),
            pltpu.VMEM((BLOCKS, PAIRS, BLOCK, 2 * BLOCK), f32),
            pltpu.VMEM((PAIRS, HD, 2 * BLOCK), f32),
        ],
        compiler_params=params(),
        cost_estimate=cost(20_000_000_000, 4_000_000, 6_000_000),
        name="attend",
    )(meta, one, wq, vec, kv_all)

    block = shape(4, 4, 4, ROWS, COLS)
    results = pl.pallas_call(
        middle_kernel,
        out_shape=[
            shape(TOK, D),
            shape(TOK, D, dtype=f32),
            shape(TOK, D),
            shape(D, D),
            shape(8, D, dtype=f32),
            shape(1, FF, dtype=f32),
            block,
            block,
            block,
            block,
        ],
        in_specs=[SMEM] + [ANY] * 16 + whole(6),
        out_specs=whole(6) + [ANY] * 4,
        scratch_shapes=[
            pltpu.VMEM((2, D, COLS), bf16),
            pltpu.VMEM((2, D, COLS), bf16),
            pltpu.VMEM((2, D, COLS), bf16),
            pltpu.VMEM((2, D, COLS), bf16),
            pltpu.SemaphoreType.DMA((2, 2)),
            pltpu.SemaphoreType.DMA((2, 2)),
            pltpu.VMEM((TOK, D), bf16),
            pltpu.VMEM((D, TOK), bf16),
            pltpu.VMEM((D, TOK), bf16),
            pltpu.VMEM((TOK, D), f32),
            pltpu.VMEM((TOK, D), f32),
            pltpu.VMEM((TOK, D), f32),
        ],
        compiler_params=params(),
        cost_estimate=cost(8_000_000_000, 20_000_000, 1_000_000),
        name="feed",
    )(meta, *fc_all, *proj_all, x, cot, att, wout, vec, fcb)
    output, grad_middle, grad_att, gwout, sums, fcsum = results[:6]
    grad_w_fc, grad_w_proj = scatter_mlp(*results[6:])
    grad_w_out = scatter_rows(gwout)

    gq, gwq, dkv = pl.pallas_call(
        backward_kernel,
        out_shape=[shape(TOK, D), shape(D, D), shape(LENGTH, BLOCK)],
        in_specs=[SMEM] + whole(6),
        out_specs=whole(3),
        scratch_shapes=[
            pltpu.VMEM(wide, bf16),
            pltpu.VMEM(wide, bf16),
            pltpu.VMEM((2, PAIRS, 2 * BLOCK, BLOCK), bf16),
            pltpu.VMEM((2, PAIRS, 2 * BLOCK, BLOCK), bf16),
            pltpu.VMEM((BLOCKS, HD, BLOCK), bf16),
            pltpu.VMEM((2, PAIRS, 8, 2 * BLOCK), f32),
            pltpu.VMEM((PAIRS, HD, 2 * BLOCK), f32),
            pltpu.VMEM((BLOCKS, BLOCK, BLOCK), f32),
        ],
        compiler_params=params(),
        cost_estimate=cost(40_000_000_000, 6_000_000, 6_000_000),
        name="attend_back",
    )(meta, q, grad_att, att, lse, kv_all, one)
    got = lax.all_to_all(dkv.reshape(8, TOK, BLOCK), CTX, 0, 0)
    grad_wq = scatter_rows(gwq)

    fc4 = jnp.concatenate([fcsum.reshape(D, 4).T, jnp.zeros((4, D), f32)], 0)
    grad_x, pack = pl.pallas_call(
        last_kernel,
        out_shape=[shape(TOK, D), shape(D, 2 * BLOCK)],
        in_specs=whole(10),
        out_specs=whole(2),
        compiler_params=params(),
        cost_estimate=cost(1_000_000_000, 5_000_000),
        name="last",
    )(x, one, gq, got, grad_middle, wq, early, vec, sums, fc4)
    tail = scatter_rows(pack)
    rows = tail[:, BLOCK : BLOCK + 16] + tail[:, BLOCK + 16 : BLOCK + 32]
    value = tail[0:4, BLOCK + 32 : BLOCK + 48] + tail[0:4, BLOCK + 48 : BLOCK + 64]
    return (
        output[None],
        grad_x[None],
        rows[:, 0],
        rows[:, 1],
        jnp.concatenate([grad_wq, tail[:, :BLOCK]], 1),
        rows[:, 2],
        value.reshape(HD),
        grad_w_out,
        rows[:, 3],
        rows[:, 4],
        rows[:, 5],
        grad_w_fc,
        rows[:, 7:11].reshape(24),
        grad_w_proj,
        rows[:, 6],
    )


def solution(mesh):
    cells = Mesh(mesh.devices.reshape(SIZES), AXES)
    every = P(AXES)
    tall = P(AXES, None)
    tokens = P(DP, CTX, None)
    in_specs = (
        tokens,
        tokens,
        P(DP),
        P(DP, None),
        P(DP, None),
        every,
        every,
        tall,
        every,
        P(),
        tall,
        every,
        every,
        every,
        tall,
        every,
        tall,
        every,
    )
    out_specs = (
        tokens,
        tokens,
        every,
        every,
        tall,
        every,
        P(),
        tall,
        every,
        every,
        every,
        tall,
        every,
        tall,
        every,
    )
    return jax.shard_map(local, mesh=cells, in_specs=in_specs, out_specs=out_specs, check_vma=False)
```

time: 1650 us -> 373 us (0.23)
  waiting for transfers between devices: 1240 us -> 139 us
  blocking collectives: 170 us -> 0 us
  starting transfers between devices: 0.23 us -> 139 us
  matrix products: 110 us -> 0 us
  Pallas kernels: 0 us -> 41.3 us
  other arithmetic: 49.8 us -> 16 us
  local copies, waits for them, and re-layouts: 56 us -> 33 us
    all_gather x4 -> x0, waiting for transfers between devices: 1030 us -> none  [the longest x1 298 us: local(): lax.all_gather(w_attn, ('dp', 'ctx'), axis=0, tiled=True)]
    unnamed x7 -> x0, waiting for transfers between devices: 152 us -> none
    unnamed x2 -> x0, blocking collectives: 135 us -> none
    dot_general x54 -> x0, matrix products: 110 us -> none  [the longest x12 27.2 us: scores_for(): jnp.einsum('tgd,kd->tgk', query_block, key_rows, preferred_element_type=j...]
    ppermute x0 -> x40, waiting for transfers between devices: none -> 91.2 us  [send(): return lax.ppermute(value, AXES, route(**shift))]
    all_to_all x0 -> x10, starting transfers between devices: none -> 82.4 us  [the longest x1 25.5 us: local(): got = lax.all_to_all(dkv.reshape(8, TOK, BLOCK), CTX, 0, 0)]
    reduce_scatter x1 -> x0, waiting for transfers between devices: 59.5 us -> none  [local(): lax.psum_scatter(jnp.concatenate([grad_keys, grad_values], 1), 'ctx', sca...]
    ppermute x0 -> x40, starting transfers between devices: none -> 56.8 us  [send(): return lax.ppermute(value, AXES, route(**shift))]
  transfers between devices with their start and end apart: 6 -> 50, of which waited for: 6 -> 19; matrix products, arithmetic and copies ran while one was open for 7% -> 12% of each run, Pallas kernels for 0% -> 5%
where the time goes in v1:
time: 373 us; the launch traced here: 371 us
  starting transfers between devices  139 us (37%)
  waiting for transfers between devices  139 us (37%)
  Pallas kernels  41.3 us (11%)
  local copies, waits for them, and re-layouts  33 us (9%)
  other arithmetic  16 us (4%)
    ppermute x40, waiting for transfers between devices, send(): return lax.ppermute(value, AXES, route(**shift))  91.2 us
    ppermute x40, starting transfers between devices, send(): return lax.ppermute(value, AXES, route(**shift))  56.8 us
    all_to_all x1, starting transfers between devices, local(): got = lax.all_to_all(dkv.reshape(8, TOK, BLOCK), CTX, 0, 0)  25.5 us
    pallas_call x1, Pallas kernels, local(): pl.pallas_call(middle_kernel, out_shape=[shape(TOK, D), shape(TOK, D, dty...  21.4 us
    all_to_all x3, starting transfers between devices, gather_rows(): return lax.all_to_all(copies, AXES, 0, 0).reshape(D, value.shape[1])  21.1 us
    all_to_all x3, waiting for transfers between devices, gather_rows(): return lax.all_to_all(copies, AXES, 0, 0).reshape(D, value.shape[1])  18.8 us
    all_to_all x3, starting transfers between devices, scatter_rows(): pieces = lax.all_to_all(value.reshape(128, 6, value.shape[1]), AXES, 0, 0)  17.1 us
    convert_element_type x6, other arithmetic, add_all(): return total.astype(dtype)  10.4 us
  transfers between devices with their start and end apart: 50, of which 19 were waited for; matrix products, arithmetic and copies ran while one was open for 12% of the time, Pallas kernels for 5%

profile of v1, /device:TPU:0, one launch (start us, length us, event | category | flops | bytes accessed | tf_op | source)
XLA Modules:
  0.0 370.5 jit_solution(5681856807294472437)
XLA Ops:
  2.1 7.9 %all-to-all-start = ((bf16[8,6,768]{2,1,0:T(8,128)(2,1)}), bf16[8,6,768]{2,1,0:T(8,128)(2,1)S(1)}, u32[]{:S(2)}, u32[]{:S(2)}) async-start(bf16[8,6,768]{2,1,0:T(8,128)(2,1)} %pad_maximum_fusion.4), calls=%async_computation | async-start | bytes 196608 | tf_op jit(solution)/shard_map/all_to_all | solution.py:461
  18.6 9.5 %all-to-all-start.1 = ((bf16[128,6,256]{2,1,0:T(8,128)(2,1)}), bf16[128,6,256]{2,1,0:T(8,128)(2,1)S(1)}, u32[]{:S(2)}, u32[]{:S(2)}) async-start(bf16[128,6,256]{2,1,0:T(8,128)(2,1)} %broadcast_in_dim.54), calls=%async_computation.1 | async-start | bytes 1048576 | tf_op jit(solution)/shard_map/all_to_all | solution.py:448
  32.5 6.0 %collective-permute-done = bf16[48,768]{1,0:T(8,128)(2,1)S(1)} collective-permute-done((bf16[48,768]{1,0:T(8,128)(2,1)S(1)}, bf16[48,768]{1,0:T(8,128)(2,1)S(1)}, u32[]{:S(2)}, u32[]{:S(2)}) %collective-permute-start) | collective-permute-done | bytes 73760 | tf_op jit(solution)/shard_map/ppermute | solution.py:45
  42.7 6.6 %all-to-all-start.2 = ((bf16[128,6,768]{2,1,0:T(8,128)(2,1)}), bf16[128,6,768]{2,1,0:T(8,128)(2,1)S(1)}, u32[]{:S(2)}, u32[]{:S(2)}) async-start(bf16[128,6,768]{2,1,0:T(8,128)(2,1)} %broadcast_in_dim.56), calls=%async_computation.2 | async-start | bytes 3145728 | tf_op jit(solution)/shard_map/all_to_all | solution.py:448
  57.0 14.1 %collective-permute-done.13 = bf16[4,48,384]{2,1,0:T(8,128)(2,1)S(1)} collective-permute-done((bf16[4,48,384]{2,1,0:T(8,128)(2,1)S(1)}, bf16[4,48,384]{2,1,0:T(8,128)(2,1)S(1)}, u32[]{:S(2)}, u32[]{:S(2)}) %collective-permute-start.13) | collective-permute-done | bytes 147488 | tf_op jit(solution)/shard_map/ppermute | solution.py:45
  82.1 21.1 %collective-permute-done.17.refs_10_ = bf16[4,4,48,384]{3,2,1,0:T(8,128)(2,1)} collective-permute-done((bf16[4,4,48,384]{3,2,1,0:T(8,128)(2,1)S(1)}, bf16[4,4,48,384]{3,2,1,0:T(8,128)(2,1)}, u32[]{:S(2)}, u32[]{:S(2)}) %collective-permute-start.17) | collective-permute-done | bytes 589856 | tf_op jit(solution)/shard_map/ppermute | solution.py:45
  112.8 6.2 %all-to-all-start.3 = ((bf16[8,256,128]{2,1,0:T(8,128)(2,1)}), bf16[8,256,128]{2,1,0:T(8,128)(2,1)}, u32[]{:S(2)}, u32[]{:S(2)}) async-start(bf16[8,256,128]{2,1,0:T(8,128)(2,1)} %broadcast_in_dim.57), calls=%async_computation.3 | async-start | bytes 1048576 | tf_op jit(solution)/shard_map/all_to_all | solution.py:561
  131.3 5.0 %all-to-all-start.4 = ((bf16[128,6,768]{2,1,0:T(8,128)(2,1)}), bf16[128,6,768]{2,1,0:T(8,128)(2,1)S(1)}, u32[]{:S(2)}, u32[]{:S(2)}) async-start(bf16[128,6,768]{2,1,0:T(8,128)(2,1)} %broadcast_in_dim.58), calls=%async_computation.4 | async-start | bytes 3145728 | tf_op jit(solution)/shard_map/all_to_all | solution.py:448
  137.8 4.9 %attend.1 = (bf16[256,768]{1,0:T(8,128)(2,1)}, bf16[256,768]{1,0:T(8,128)(2,1)}, f32[2,6,8,256]{3,2,1,0:T(8,128)}) custom-call(s32[42]{0:T(128)} %concatenate.30.meta, bf16[256,768]{1,0:T(8,128)(2,1)} %get-tuple-element.36.one_ref, bf16[768,768]{1,0:T(8,128)(2,1)} %reshape.146.wq_ref, f32[16,768]{1,0:T(8,128)} %get-tuple-element.37.vec_ref.refs_20_, ...), custom_call_target="tpu_custom_call" | custom-call | flops 20000000000 | bytes 4000000 | tf_op jit(solution)/shard_map/attend/pallas_call | solution.py:567
  142.7 17.7 %all-to-all-done.4 = bf16[128,6,768]{2,1,0:T(8,128)(2,1)S(1)} async-done(((bf16[128,6,768]{2,1,0:T(8,128)(2,1)}), bf16[128,6,768]{2,1,0:T(8,128)(2,1)S(1)}, u32[]{:S(2)}, u32[]{:S(2)}) %all-to-all-start.4) | async-done | bytes 1179680 | tf_op jit(solution)/shard_map/all_to_all | solution.py:448
  162.6 21.4 %feed.1 = (bf16[256,768]{1,0:T(8,128)(2,1)}, f32[256,768]{1,0:T(8,128)}, bf16[256,768]{1,0:T(8,128)(2,1)}, bf16[768,768]{1,0:T(8,128)(2,1)}, f32[8,768]{1,0:T(8,...) custom-call(s32[42]{0:T(128)} %concatenate.30.meta, ...), custom_call_target="tpu_custom_call" | custom-call | flops 8000000000 | bytes 20000000 | tf_op jit(solution)/shard_map/feed/pallas_call | solution.py:584
  184.7 8.6 %attend_back.1 = (bf16[256,768]{1,0:T(8,128)(2,1)}, bf16[768,768]{1,0:T(8,128)(2,1)}, bf16[2048,128]{1,0:T(8,128)(2,1)}) custom-call(s32[42]{0:T(128)} %concatenate.30.meta, bf16[256,768]{1,0:T(8,128)(2,1)} %get-tuple-element.41.q_ref, bf16[256,768]{1,0:T(8,128)(2,1)} %get-tuple-element.42.do_ref, bf16[256,768]{1,0:T(8,128)(2,1)} %get-tuple-element.39.refs_18_.att_ref, ...), custom_call_target="tpu_custom_call" | custom-call | flops 40000000000 | bytes 6000000 | tf_op jit(solution)/shard_map/attend_back/pallas_call | solution.py:622
  193.3 25.5 %all-to-all-start.5 = ((bf16[8,256,128]{2,1,0:T(8,128)(2,1)}), bf16[8,256,128]{2,1,0:T(8,128)(2,1)S(1)}, u32[]{:S(2)}, u32[]{:S(2)}) async-start(bf16[8,256,128]{2,1,0:T(8,128)(2,1)} %bitcast.126), calls=%async_computation.5 | async-start | bytes 1048576 | tf_op jit(solution)/shard_map/all_to_all | solution.py:641
  221.1 7.3 %all-to-all-done.5.dkv_ref = bf16[8,256,128]{2,1,0:T(8,128)(2,1)S(1)} async-done(((bf16[8,256,128]{2,1,0:T(8,128)(2,1)}), bf16[8,256,128]{2,1,0:T(8,128)(2,1)S(1)}, u32[]{:S(2)}, u32[]{:S(2)}) %all-to-all-start.5) | async-done | bytes 524320 | tf_op jit(solution)/shard_map/all_to_all | solution.py:641
  235.2 6.4 %all-to-all-start.6 = ((bf16[128,6,256]{2,1,0:T(8,128)(2,1)}), bf16[128,6,256]{2,1,0:T(8,128)(2,1)S(1)}, u32[]{:S(2)}, u32[]{:S(2)}) async-start(bf16[128,6,256]{2,1,0:T(8,128)(2,1)} %reshape.152), calls=%async_computation.6 | async-start | bytes 1048576 | tf_op jit(solution)/shard_map/all_to_all | solution.py:452
  244.6 10.4 %all-to-all-done.6 = bf16[128,6,256]{2,1,0:T(8,128)(2,1)S(1)} async-done(((bf16[128,6,256]{2,1,0:T(8,128)(2,1)}), bf16[128,6,256]{2,1,0:T(8,128)(2,1)S(1)}, u32[]{:S(2)}, u32[]{:S(2)}) %all-to-all-start.6) | async-done | bytes 393248 | tf_op jit(solution)/shard_map/all_to_all | solution.py:452
  275.8 16.0 %collective-permute-done.24 = bf16[4,4,48,384]{3,2,1,0:T(8,128)(2,1)S(1)} collective-permute-done((bf16[4,4,48,384]{3,2,1,0:T(8,128)(2,1)S(1)}, bf16[4,4,48,384]{3,2,1,0:T(8,128)(2,1)S(1)}, u32[]{:S(2)}, u32[]{:S(2)}) %collective-permute-start.24) | collective-permute-done | bytes 589856 | tf_op jit(solution)/shard_map/ppermute | solution.py:45
  297.5 7.2 %collective-permute-done.25 = bf16[4,4,48,384]{3,2,1,0:T(8,128)(2,1)} collective-permute-done((bf16[4,4,48,384]{3,2,1,0:T(8,128)(2,1)}, bf16[4,4,48,384]{3,2,1,0:T(8,128)(2,1)}, u32[]{:S(2)}, u32[]{:S(2)}) %collective-permute-start.25) | collective-permute-done | bytes 589856 | tf_op jit(solution)/shard_map/ppermute | solution.py:45
  314.4 6.6 %collective-permute-start.35 = (bf16[4,48,384]{2,1,0:T(8,128)(2,1)S(1)}, bf16[4,48,384]{2,1,0:T(8,128)(2,1)S(1)}, u32[]{:S(2)}, u32[]{:S(2)}) collective-permute-start(bf16[4,48,384]{2,1,0:T(8,128)(2,1)S(1)} %get-tuple-element.78), channel_id=1, source_target_pairs={{0,64},{1,65},{2,66},{3,67},{4,68},{5,69},{6,70},{7,71},{8,72},{9,... | collective-permute-start | bytes 442376 | tf_op jit(solution)/shard_map/ppermute | solution.py:45
  326.3 6.0 %all-to-all-start.8 = ((bf16[128,6,768]{2,1,0:T(8,128)(2,1)}), bf16[128,6,768]{2,1,0:T(8,128)(2,1)S(1)}, u32[]{:S(2)}, u32[]{:S(2)}) async-start(bf16[128,6,768]{2,1,0:T(8,128)(2,1)} %reshape.155), calls=%async_computation.8 | async-start | bytes 3145728 | tf_op jit(solution)/shard_map/all_to_all | solution.py:452
  338.5 10.6 %collective-permute-done.37 = bf16[48,768]{1,0:T(8,128)(2,1)S(1)} collective-permute-done((bf16[48,768]{1,0:T(8,128)(2,1)S(1)}, bf16[48,768]{1,0:T(8,128)(2,1)S(1)}, u32[]{:S(2)}, u32[]{:S(2)}) %collective-permute-start.37) | collective-permute-done | bytes 73760 | tf_op jit(solution)/shard_map/ppermute | solution.py:45
  349.1 7.0 %collective-permute-done.38 = bf16[48,768]{1,0:T(8,128)(2,1)S(1)} collective-permute-done((bf16[48,768]{1,0:T(8,128)(2,1)S(1)}, bf16[48,768]{1,0:T(8,128)(2,1)S(1)}, u32[]{:S(2)}, u32[]{:S(2)}) %collective-permute-start.38) | collective-permute-done | bytes 73760 | tf_op jit(solution)/shard_map/ppermute | solution.py:45
  356.8 4.7 %all-to-all-start.9 = ((f32[8,6,768]{2,1,0:T(8,128)}), f32[8,6,768]{2,1,0:T(8,128)S(1)}, u32[]{:S(2)}, u32[]{:S(2)}) async-start(f32[8,6,768]{2,1,0:T(8,128)} %reshape.156), calls=%async_computation.9 | async-start | bytes 393216 | tf_op jit(solution)/shard_map/all_to_all | solution.py:495
  363.1 6.7 %all-to-all-done.9 = f32[8,6,768]{2,1,0:T(8,128)S(1)} async-done(((f32[8,6,768]{2,1,0:T(8,128)}), f32[8,6,768]{2,1,0:T(8,128)S(1)}, u32[]{:S(2)}, u32[]{:S(2)}) %all-to-all-start.9) | async-done | bytes 147488 | tf_op jit(solution)/shard_map/all_to_all | solution.py:495
  (193 shorter events, 125.5 us)
Async XLA Ops:
  42.7 68.3 %all-to-all-start.2 = ((bf16[128,6,768]{2,1,0:T(8,128)(2,1)}), bf16[128,6,768]{2,1,0:T(8,128)(2,1)S(1)}, u32[]{:S(2)}, u32[]{:S(2)}) async-start(bf16[128,6,768]{2,1,0:T(8,128)(2,1)} %broadcast_in_dim.56), calls=%async_computation.2 | async-start | bytes 3145728 | tf_op jit(solution)/shard_map/all_to_all | solution.py:448
  53.4 25.3 %collective-permute-start.3 = (bf16[4,48,384]{2,1,0:T(8,128)(2,1)S(1)}, bf16[4,48,384]{2,1,0:T(8,128)(2,1)S(1)}, u32[]{:S(2)}, u32[]{:S(2)}) collective-permute-start(bf16[4,48,384]{2,1,0:T(8,128)(2,1)S(1)} %get-tuple-element.92), channel_id=1, source_target_pairs={{0,6},{1,7},{2,0},{3,1},{4,2},{5,3},{6,4},{7,5},{8,14},{9,15},{10,... | collective-permute-start | bytes 442376 | tf_op jit(solution)/shard_map/ppermute | solution.py:45
  75.1 28.0 %collective-permute-start.17 = (bf16[4,4,48,384]{3,2,1,0:T(8,128)(2,1)S(1)}, bf16[4,4,48,384]{3,2,1,0:T(8,128)(2,1)}, u32[]{:S(2)}, u32[]{:S(2)}) collective-permute-start(bf16[4,4,48,384]{3,2,1,0:T(8,128)(2,1)S(1)} %pad_maximum_fusion.1.refs_8_), channel_id=1, source_target_pairs={{0,6},{1,7},{2,0},{3,1},{4,2},{5,3},{6,4},{7,5},{8,14},{9,15},{10,... | collective-permute-start | bytes 1769480 | tf_op jit(solution)/shard_map/ppermute | solution.py:45
  77.9 26.5 %collective-permute-start.19 = (bf16[4,4,48,384]{3,2,1,0:T(8,128)(2,1)S(1)}, bf16[4,4,48,384]{3,2,1,0:T(8,128)(2,1)S(1)}, u32[]{:S(2)}, u32[]{:S(2)}) collective-permute-start(bf16[4,4,48,384]{3,2,1,0:T(8,128)(2,1)S(1)} %pad_maximum_fusion.1.refs_8_), channel_id=1, source_target_pairs={{0,4},{1,5},{2,6},{3,7},{4,0},{5,1},{6,2},{7,3},{8,12},{9,13},{10,... | collective-permute-start | bytes 1769480 | tf_op jit(solution)/shard_map/ppermute | solution.py:45
  78.7 28.1 %collective-permute-start.21 = (bf16[4,4,48,384]{3,2,1,0:T(8,128)(2,1)S(1)}, bf16[4,4,48,384]{3,2,1,0:T(8,128)(2,1)S(1)}, u32[]{:S(2)}, u32[]{:S(2)}) collective-permute-start(bf16[4,4,48,384]{3,2,1,0:T(8,128)(2,1)S(1)} %pad_maximum_fusion.1.refs_8_), channel_id=1, source_target_pairs={{0,2},{1,3},{2,4},{3,5},{4,6},{5,7},{6,0},{7,1},{8,10},{9,11},{10,... | collective-permute-start | bytes 1769480 | tf_op jit(solution)/shard_map/ppermute | solution.py:45
  79.7 27.3 %collective-permute-start.9 = (bf16[4,4,48,384]{3,2,1,0:T(8,128)(2,1)S(1)}, bf16[4,4,48,384]{3,2,1,0:T(8,128)(2,1)S(1)}, u32[]{:S(2)}, u32[]{:S(2)}) collective-permute-start(bf16[4,4,48,384]{3,2,1,0:T(8,128)(2,1)S(1)} %pad_maximum_fusion.refs_0_), channel_id=1, source_target_pairs={{0,64},{1,65},{2,66},{3,67},{4,68},{5,69},{6,70},{7,71},{8,72},{9,... | collective-permute-start | bytes 1769480 | tf_op jit(solution)/shard_map/ppermute | solution.py:45
  80.6 55.8 %collective-permute-start.11 = (bf16[4,4,48,384]{3,2,1,0:T(8,128)(2,1)S(1)}, bf16[4,4,48,384]{3,2,1,0:T(8,128)(2,1)}, u32[]{:S(2)}, u32[]{:S(2)}) collective-permute-start(bf16[4,4,48,384]{3,2,1,0:T(8,128)(2,1)S(1)} %pad_maximum_fusion.refs_0_), channel_id=1, source_target_pairs={{0,32},{1,33},{2,34},{3,35},{4,36},{5,37},{6,38},{7,39},{8,40},{9,... | collective-permute-start | bytes 1769480 | tf_op jit(solution)/shard_map/ppermute | solution.py:45
  103.1 33.4 %collective-permute-start.7 = (bf16[4,4,48,384]{3,2,1,0:T(8,128)(2,1)S(1)}, bf16[4,4,48,384]{3,2,1,0:T(8,128)(2,1)}, u32[]{:S(2)}, u32[]{:S(2)}) collective-permute-start(bf16[4,4,48,384]{3,2,1,0:T(8,128)(2,1)S(1)} %pad_maximum_fusion.refs_0_), channel_id=1, source_target_pairs={{0,96},{1,97},{2,98},{3,99},{4,100},{5,101},{6,102},{7,103},{8,104... | collective-permute-start | bytes 1769480 | tf_op jit(solution)/shard_map/ppermute | solution.py:45
  104.4 32.5 %collective-permute-start.16 = (bf16[4,4,48,384]{3,2,1,0:T(8,128)(2,1)S(1)}, bf16[4,4,48,384]{3,2,1,0:T(8,128)(2,1)}, u32[]{:S(2)}, u32[]{:S(2)}) collective-permute-start(bf16[4,4,48,384]{3,2,1,0:T(8,128)(2,1)S(1)} %pad_maximum_fusion.1.refs_8_), channel_id=1, source_target_pairs={{0,8},{1,9},{2,10},{3,11},{4,12},{5,13},{6,14},{7,15},{8,0},{9,1},... | collective-permute-start | bytes 1769480 | tf_op jit(solution)/shard_map/ppermute | solution.py:45
  106.8 30.2 %collective-permute-start.6 = (bf16[4,4,48,384]{3,2,1,0:T(8,128)(2,1)S(1)}, bf16[4,4,48,384]{3,2,1,0:T(8,128)(2,1)}, u32[]{:S(2)}, u32[]{:S(2)}) collective-permute-start(bf16[4,4,48,384]{3,2,1,0:T(8,128)(2,1)S(1)} %pad_maximum_fusion.refs_0_), channel_id=1, source_target_pairs={{0,8},{1,9},{2,10},{3,11},{4,12},{5,13},{6,14},{7,15},{8,0},{9,1},... | collective-permute-start | bytes 1769480 | tf_op jit(solution)/shard_map/ppermute | solution.py:45
  107.0 30.5 %collective-permute-start.18 = (bf16[4,4,48,384]{3,2,1,0:T(8,128)(2,1)}, bf16[4,4,48,384]{3,2,1,0:T(8,128)(2,1)}, u32[]{:S(2)}, u32[]{:S(2)}) collective-permute-start(bf16[4,4,48,384]{3,2,1,0:T(8,128)(2,1)} %collective-permute-done.17.refs_10_), channel_id=1, source_target_pairs={{0,8},{1,9},{2,10},{3,11},{4,12},{5,13},{6,14},{7,15},{8,0},{9,1},... | collective-permute-start | bytes 1769480 | tf_op jit(solution)/shard_map/ppermute | solution.py:45
  131.3 29.0 %all-to-all-start.4 = ((bf16[128,6,768]{2,1,0:T(8,128)(2,1)}), bf16[128,6,768]{2,1,0:T(8,128)(2,1)S(1)}, u32[]{:S(2)}, u32[]{:S(2)}) async-start(bf16[128,6,768]{2,1,0:T(8,128)(2,1)} %broadcast_in_dim.58), calls=%async_computation.4 | async-start | bytes 3145728 | tf_op jit(solution)/shard_map/all_to_all | solution.py:448
  136.4 25.2 %collective-permute-start.20 = (bf16[4,4,48,384]{3,2,1,0:T(8,128)(2,1)S(1)}, bf16[4,4,48,384]{3,2,1,0:T(8,128)(2,1)}, u32[]{:S(2)}, u32[]{:S(2)}) collective-permute-start(bf16[4,4,48,384]{3,2,1,0:T(8,128)(2,1)S(1)} %copy-done.13), channel_id=1, source_target_pairs={{0,8},{1,9},{2,10},{3,11},{4,12},{5,13},{6,14},{7,15},{8,0},{9,1},... | collective-permute-start | bytes 1769480 | tf_op jit(solution)/shard_map/ppermute | solution.py:45
  136.5 25.1 %collective-permute-start.22 = (bf16[4,4,48,384]{3,2,1,0:T(8,128)(2,1)}, bf16[4,4,48,384]{3,2,1,0:T(8,128)(2,1)}, u32[]{:S(2)}, u32[]{:S(2)}) collective-permute-start(bf16[4,4,48,384]{3,2,1,0:T(8,128)(2,1)} %copy-done.14), channel_id=1, source_target_pairs={{0,8},{1,9},{2,10},{3,11},{4,12},{5,13},{6,14},{7,15},{8,0},{9,1},... | collective-permute-start | bytes 1769480 | tf_op jit(solution)/shard_map/ppermute | solution.py:45
  184.0 75.8 %collective-permute-start.23 = (bf16[4,4,4,48,384]{4,3,2,1,0:T(8,128)(2,1)}, bf16[4,4,4,48,384]{4,3,2,1,0:T(8,128)(2,1)}, u32[]{:S(2)}, u32[]{:S(2)}) collective-permute-start(bf16[4,4,4,48,384]{4,3,2,1,0:T(8,128)(2,1)} %get-tuple-element.54), channel_id=1, source_target_pairs={{0,8},{1,9},{2,10},{3,11},{4,12},{5,13},{6,14},{7,15},{8,0},{9,1},... | collective-permute-start | bytes 7077896 | tf_op jit(solution)/shard_map/ppermute | solution.py:45
  184.6 84.1 %collective-permute-start.30 = (bf16[4,4,4,48,384]{4,3,2,1,0:T(8,128)(2,1)}, bf16[4,4,4,48,384]{4,3,2,1,0:T(8,128)(2,1)}, u32[]{:S(2)}, u32[]{:S(2)}) collective-permute-start(bf16[4,4,4,48,384]{4,3,2,1,0:T(8,128)(2,1)} %get-tuple-element.56), channel_id=1, source_target_pairs={{0,8},{1,9},{2,10},{3,11},{4,12},{5,13},{6,14},{7,15},{8,0},{9,1},... | collective-permute-start | bytes 7077896 | tf_op jit(solution)/shard_map/ppermute | solution.py:45
  193.3 35.2 %all-to-all-start.5 = ((bf16[8,256,128]{2,1,0:T(8,128)(2,1)}), bf16[8,256,128]{2,1,0:T(8,128)(2,1)S(1)}, u32[]{:S(2)}, u32[]{:S(2)}) async-start(bf16[8,256,128]{2,1,0:T(8,128)(2,1)} %bitcast.126), calls=%async_computation.5 | async-start | bytes 1048576 | tf_op jit(solution)/shard_map/all_to_all | solution.py:641
  255.0 71.3 %all-to-all-start.7 = ((bf16[128,6,768]{2,1,0:T(8,128)(2,1)}), bf16[128,6,768]{2,1,0:T(8,128)(2,1)S(1)}, u32[]{:S(2)}, u32[]{:S(2)}) async-start(bf16[128,6,768]{2,1,0:T(8,128)(2,1)} %reshape.153), calls=%async_computation.7 | async-start | bytes 3145728 | tf_op jit(solution)/shard_map/all_to_all | solution.py:452
  263.4 28.4 %collective-permute-start.24 = (bf16[4,4,48,384]{3,2,1,0:T(8,128)(2,1)S(1)}, bf16[4,4,48,384]{3,2,1,0:T(8,128)(2,1)S(1)}, u32[]{:S(2)}, u32[]{:S(2)}) collective-permute-start(bf16[4,4,48,384]{3,2,1,0:T(8,128)(2,1)S(1)} %get-tuple-element.67), channel_id=1, source_target_pairs={{0,32},{1,33},{2,34},{3,35},{4,36},{5,37},{6,38},{7,39},{8,40},{9,... | collective-permute-start | bytes 1769480 | tf_op jit(solution)/shard_map/ppermute | solution.py:45
  264.4 40.2 %collective-permute-start.25 = (bf16[4,4,48,384]{3,2,1,0:T(8,128)(2,1)}, bf16[4,4,48,384]{3,2,1,0:T(8,128)(2,1)}, u32[]{:S(2)}, u32[]{:S(2)}) collective-permute-start(bf16[4,4,48,384]{3,2,1,0:T(8,128)(2,1)} %get-tuple-element.69), channel_id=1, source_target_pairs={{0,64},{1,65},{2,66},{3,67},{4,68},{5,69},{6,70},{7,71},{8,72},{9,... | collective-permute-start | bytes 1769480 | tf_op jit(solution)/shard_map/ppermute | solution.py:45
  267.1 37.6 %collective-permute-start.26 = (bf16[4,4,48,384]{3,2,1,0:T(8,128)(2,1)}, bf16[4,4,48,384]{3,2,1,0:T(8,128)(2,1)}, u32[]{:S(2)}, u32[]{:S(2)}) collective-permute-start(bf16[4,4,48,384]{3,2,1,0:T(8,128)(2,1)} %get-tuple-element.68), channel_id=1, source_target_pairs={{0,96},{1,97},{2,98},{3,99},{4,100},{5,101},{6,102},{7,103},{8,104... | collective-permute-start | bytes 1769480 | tf_op jit(solution)/shard_map/ppermute | solution.py:45
  271.6 39.6 %collective-permute-start.31 = (bf16[4,4,48,384]{3,2,1,0:T(8,128)(2,1)}, bf16[4,4,48,384]{3,2,1,0:T(8,128)(2,1)S(1)}, u32[]{:S(2)}, u32[]{:S(2)}) collective-permute-start(bf16[4,4,48,384]{3,2,1,0:T(8,128)(2,1)} %get-tuple-element.70), channel_id=1, source_target_pairs={{0,2},{1,3},{2,4},{3,5},{4,6},{5,7},{6,0},{7,1},{8,10},{9,11},{10,... | collective-permute-start | bytes 1769480 | tf_op jit(solution)/shard_map/ppermute | solution.py:45
  273.1 39.5 %collective-permute-start.32 = (bf16[4,4,48,384]{3,2,1,0:T(8,128)(2,1)}, bf16[4,4,48,384]{3,2,1,0:T(8,128)(2,1)S(1)}, u32[]{:S(2)}, u32[]{:S(2)}) collective-permute-start(bf16[4,4,48,384]{3,2,1,0:T(8,128)(2,1)} %get-tuple-element.72), channel_id=1, source_target_pairs={{0,4},{1,5},{2,6},{3,7},{4,0},{5,1},{6,2},{7,3},{8,12},{9,13},{10,... | collective-permute-start | bytes 1769480 | tf_op jit(solution)/shard_map/ppermute | solution.py:45
  326.3 30.5 %all-to-all-start.8 = ((bf16[128,6,768]{2,1,0:T(8,128)(2,1)}), bf16[128,6,768]{2,1,0:T(8,128)(2,1)S(1)}, u32[]{:S(2)}, u32[]{:S(2)}) async-start(bf16[128,6,768]{2,1,0:T(8,128)(2,1)} %reshape.155), calls=%async_computation.8 | async-start | bytes 3145728 | tf_op jit(solution)/shard_map/all_to_all | solution.py:452
  (46 other events, 678.1 us)

commit v2 on v1

v2 whole, which is shorter than its diff:
```python
import functools

import jax
import jax.numpy as jnp
import numpy as np
from jax import lax
from jax.experimental import pallas as pl
from jax.experimental.pallas import tpu as pltpu
from jax.sharding import Mesh
from jax.sharding import PartitionSpec as P

D = 768
HEADS = 12
HD = 64
FF = 3072
TOK = 256
LENGTH = 2048
BLOCK = 128
BLOCKS = 16
PAIRS = 6
ROWS = 48
COLS = 384
NEG = -1e30

AXES = ("x", "zl", "core", "y", "zh")
SIZES = (4, 2, 2, 4, 2)
DP = ("x", "zl", "core")
CTX = ("y", "zh")

f32 = jnp.float32
bf16 = jnp.bfloat16


def route(dx=0, dy=0, dz=0, dc=0, dl=0, dh=0):
    pairs = []
    for device in range(128):
        x, zl, core, y, zh = (int(v) for v in np.unravel_index(device, SIZES))
        z = (zh * 2 + zl + dz) % 4
        target = ((x + dx) % 4, z % 2 ^ dl, core ^ dc, (y + dy) % 4, z // 2 ^ dh)
        pairs.append((device, int(np.ravel_multi_index(target, SIZES))))
    return pairs


def send(value, **shift):
    return lax.ppermute(value, AXES, route(**shift))


def row_span(group, other):
    core = lax.axis_index("core")
    return pl.ds(pl.multiple_of(group * 96 + (1 - core if other else core) * ROWS, 16), ROWS)


def mm(left, right):
    return lax.dot_general(left, right, (((1,), (0,)), ((), ())), preferred_element_type=f32)


def mm_nt(left, right):
    return lax.dot_general(left, right, (((1,), (1,)), ((), ())), preferred_element_type=f32)


def normalize(values):
    center = values - jnp.mean(values, -1, keepdims=True)
    spread = jnp.mean(center * center, -1, keepdims=True)
    factor = lax.rsqrt(spread + 1e-05)
    return center * factor, factor


def norm_back(grad_normed, normed, factor):
    return factor * (
        grad_normed
        - jnp.mean(grad_normed, -1, keepdims=True)
        - normed * jnp.mean(grad_normed * normed, -1, keepdims=True)
    )


def split_low(values):
    high = values.astype(bf16)
    return high, (values - high.astype(f32)).astype(bf16)


SLICE = 768
KEYS, SMALL, QUERY, OUT, FC, PROJ, WIDE = 0, 128, 256, 1024, 1792, 4864, 7936
G_PROJ, G_QUERY, G_OUT, G_FC, G_WIDE = 256, 1024, 1792, 2560, 5632


def piece_kernel(*refs):
    vectors, fcb_ref, attn_ref, out_ref, fc_ref, proj_ref, piece_ref = (refs[:7],) + refs[7:]
    row = lax.broadcasted_iota(jnp.int32, (8, BLOCK), 0)
    lane = lax.broadcasted_iota(jnp.int32, (8, BLOCK), 1)
    small = jnp.zeros((8, BLOCK), f32)
    for i in range(6):
        values = [ref[i] for ref in vectors] + [fcb_ref[4 * i + j] for j in range(4)]
        for j, value in enumerate(values):
            small = jnp.where((row == i) & (lane < 48) & ((lane & 15) == j), value, small)
    high = small.astype(bf16).astype(f32)
    middle = (small - high).astype(bf16).astype(f32)
    low = small - high - middle
    small = jnp.where(lane < 16, high, jnp.where(lane < 32, middle, low)).astype(bf16)[:6]
    for k in range(8):
        piece_ref[k, :, KEYS:SMALL] = attn_ref[:, D:]
        piece_ref[k, :, SMALL:QUERY] = small
        piece_ref[k, :, QUERY:OUT] = attn_ref[:, :D]
        piece_ref[k, :, OUT:FC] = out_ref[...]
        piece_ref[k, :, FC:PROJ] = fc_ref[...]
        piece_ref[k, :, PROJ:] = proj_ref[...]


def block_kernel(piece_ref, attn_ref, feed_ref, rows):
    for j in range(8):
        rows[6 * j : 6 * j + 6] = piece_ref[j].astype(f32)
    for k in range(8):
        attn_ref[k] = rows[:, :FC].astype(bf16)
    feed_ref[...] = rows[:, FC:].astype(bf16)


def unblock_kernel(attn_ref, feed_ref, piece_ref, rows):
    rows[:, :G_OUT] = jnp.sum(attn_ref[...].astype(f32), 0)
    rows[:, G_OUT:] = feed_ref[...].astype(f32)
    for j in range(8):
        piece_ref[j] = rows[6 * j : 6 * j + 6].astype(bf16)


def finish_kernel(piece_ref, attn_ref, out_ref, fc_ref, proj_ref, *refs):
    vectors, fcb_ref, value_ref = refs[:7], refs[7], refs[8]
    total = jnp.sum(piece_ref[...].astype(f32), 0)
    attn_ref[:, :D] = total[:, G_QUERY:G_OUT]
    attn_ref[:, D:] = total[:, KEYS:SMALL]
    out_ref[...] = total[:, G_OUT:G_FC]
    fc_ref[...] = total[:, G_FC:]
    for j in range(4):
        proj_ref[:, j * SLICE : (j + 1) * SLICE] = (
            piece_ref[2 * j, :, G_PROJ:G_QUERY].astype(f32)
            + piece_ref[2 * j + 1, :, G_PROJ:G_QUERY].astype(f32)
        )
    small = total[:, SMALL:QUERY]
    small = jnp.concatenate([small, jnp.zeros((2, BLOCK), f32)], 0).T
    rows = small[:16] + small[16:32]
    for j, ref in enumerate(vectors):
        ref[...] = rows[j : j + 1, :6]
    spread = jnp.where(
        lax.broadcasted_iota(jnp.int32, (8, 24), 1) // 4
        == lax.broadcasted_iota(jnp.int32, (8, 24), 0),
        1.0,
        0.0,
    )
    wide = jnp.dot(rows[7:11], spread, precision=lax.Precision.HIGHEST)
    mine = lax.broadcasted_iota(jnp.int32, (4, 24), 1) % 4 == lax.broadcasted_iota(
        jnp.int32, (4, 24), 0
    )
    fcb_ref[...] = jnp.sum(jnp.where(mine, wide, 0.0), 0, keepdims=True)
    value_ref[...] = total[:4, SMALL + 32 : SMALL + 48] + total[:4, SMALL + 48 : SMALL + 64]


def four_apart(rows, columns, turned):
    return jnp.where(
        lax.broadcasted_iota(jnp.int32, (rows, columns), 1 - turned) // 4
        == lax.broadcasted_iota(jnp.int32, (rows, columns), turned),
        1.0,
        0.0,
    ).astype(bf16)


def first_kernel(
    x_ref, vbias_ref, mine_ref, other_ref, one_ref, kv_ref, vec_ref, fcb_ref, wq_ref, wout_ref, early_ref
):
    for k in range(8):
        for other, part in enumerate((mine_ref, other_ref)):
            span = row_span(k, other)
            early_ref[span, :] = part[k, :, :QUERY]
            wq_ref[span, :] = part[k, :, QUERY:OUT]
            wout_ref[span, :] = part[k, :, OUT:]
    turned = early_ref[:, BLOCK:].astype(f32).T
    vec = turned[0:16] + turned[16:32] + turned[32:48]
    vec_ref[...] = vec
    normed, _ = normalize(x_ref[...].astype(f32))
    one = (normed * vec[0:1] + vec[1:2]).astype(bf16)
    one_ref[...] = one
    bias = jnp.concatenate([jnp.zeros((1, HD), f32), vbias_ref[...]], 1)
    kv = (mm(one, early_ref[:, :BLOCK]) + bias).astype(bf16)
    for k in range(8):
        kv_ref[k] = kv
    spread = four_apart(BLOCK, 512, 0)
    terms = turned[0:48].astype(bf16)
    term = lax.broadcasted_iota(jnp.int32, (48, 512), 0) % 16 - 7
    mine = term == lax.broadcasted_iota(jnp.int32, (48, 512), 1) % 4
    for g in range(6):
        wide = mm(terms[:, g * BLOCK : (g + 1) * BLOCK], spread)
        fcb_ref[:, g * 512 : (g + 1) * 512] = jnp.sum(
            jnp.where(mine, wide, 0.0), 0, keepdims=True
        )


def read_plan(length_ref, order_ref, files_ref, inverse):
    for k in range(BLOCKS):
        inverse[order_ref[0, k]] = k
    files = files_ref[...]
    bounds = [jnp.sum(jnp.where(files < f, 1, 0)) for f in (1, 2, 3)]
    return length_ref[0], bounds


def block_plan(plan, order_ref, b):
    length, bounds = plan
    own = lax.axis_index("y") * 2 + lax.axis_index("zh")
    place = order_ref[0, own * 2 + b]
    start = place * BLOCK
    first = jnp.int32(0)
    for bound in bounds:
        first = jnp.where(bound <= start, jnp.maximum(first, bound), first)
    low = first // BLOCK
    high = jnp.minimum(place - 1, (length - 1) // BLOCK)
    return place, low, jnp.maximum(high - low + 1, 0) + 1


def block_bias(plan, place, initial):
    length, bounds = plan
    lane = lax.broadcasted_iota(jnp.int32, (1, 2 * BLOCK), 1)
    query = place * BLOCK + (lane & (BLOCK - 1))
    first = jnp.zeros_like(query)
    for bound in bounds:
        first = jnp.where(bound <= query, jnp.maximum(first, bound), first)
    last = jnp.minimum(query, length - 1)
    key = initial * BLOCK + lax.broadcasted_iota(jnp.int32, (BLOCK, 2 * BLOCK), 0)
    allowed = ((key >= first) & (key <= last)) | (key == query)
    return jnp.where(allowed, 0.0, NEG)


def fold_heads(block):
    turned = block.T
    return jnp.concatenate([turned[:HD], turned[HD:]], 1)


def unfold_heads(wide):
    return jnp.concatenate([wide[:, :BLOCK], wide[:, BLOCK:]], 0).T


def forward_kernel(
    length_ref,
    order_ref,
    files_ref,
    one_ref,
    wq_ref,
    vec_ref,
    kv_ref,
    q_ref,
    att_ref,
    lse_ref,
    inverse,
    qt,
    vt,
    scores,
    mixed,
):
    plan = read_plan(length_ref, order_ref, files_ref, inverse)
    q = (mm(one_ref[...], wq_ref[...]) + vec_ref[2:3]).astype(bf16)
    q_ref[...] = q
    for b in range(2):
        for p in range(PAIRS):
            block = q[b * BLOCK : (b + 1) * BLOCK, p * BLOCK : (p + 1) * BLOCK].astype(f32) * 0.125
            qt[b, p, :HD] = fold_heads(block).astype(bf16)
            qt[b, p, HD:] = jnp.zeros((HD, 2 * BLOCK), bf16)
    for k in range(BLOCKS):
        vt[k] = kv_ref[k * BLOCK : (k + 1) * BLOCK].astype(f32).T[HD:].astype(bf16)

    for b in range(2):
        place, low, count = block_plan(plan, order_ref, b)

        def initial_of(t):
            return jnp.where(t == count - 1, place, low + t)

        def score_step(t, tops):
            initial = initial_of(t)
            stored = inverse[initial]
            rows = kv_ref[pl.ds(pl.multiple_of(stored * BLOCK, BLOCK), BLOCK)]
            bias = block_bias(plan, place, initial)
            new = []
            for p in range(PAIRS):
                value = mm(rows, qt[b, p]) + bias
                scores[t, p] = value
                new.append(jnp.maximum(tops[p], jnp.max(value.reshape(16, 8, 2 * BLOCK), 0)))
            return tuple(new)

        tops = lax.fori_loop(
            0, count, score_step, tuple(jnp.full((8, 2 * BLOCK), NEG, f32) for _ in range(PAIRS))
        )
        tops = tuple(jnp.max(top, 0, keepdims=True) for top in tops)
        mixed[...] = jnp.zeros_like(mixed)

        def mix_step(t, sums):
            stored = inverse[initial_of(t)]
            values = vt[stored]
            new = []
            for p in range(PAIRS):
                weight = jnp.exp(scores[t, p] - tops[p])
                new.append(sums[p] + jnp.sum(weight.reshape(16, 8, 2 * BLOCK), 0))
                mixed[p] += mm(values, weight.astype(bf16))
            return tuple(new)

        sums = lax.fori_loop(
            0, count, mix_step, tuple(jnp.zeros((8, 2 * BLOCK), f32) for _ in range(PAIRS))
        )
        for p in range(PAIRS):
            total = jnp.sum(sums[p], 0, keepdims=True)
            lse_ref[b, p] = jnp.broadcast_to(tops[p] + jnp.log(total), (8, 2 * BLOCK))
            att_ref[b * BLOCK : (b + 1) * BLOCK, p * BLOCK : (p + 1) * BLOCK] = unfold_heads(
                mixed[p] / total
            ).astype(bf16)


def backward_kernel(
    length_ref, order_ref, files_ref, q_ref, do_ref, att_ref, lse_ref, one_ref, kv_ref, *refs
):
    gq_ref, keep_ref, send_ref, grad_ref = refs[:4]
    inverse, qt, dot_, qn, don, kt, delta, dq, dkv, gwq = refs[4:]
    plan = read_plan(length_ref, order_ref, files_ref, inverse)
    zeros = jnp.zeros((BLOCK, HD), f32)
    for b in range(2):
        for p in range(PAIRS):
            span = (slice(b * BLOCK, (b + 1) * BLOCK), slice(p * BLOCK, (p + 1) * BLOCK))
            block = q_ref[span].astype(f32) * 0.125
            grad = do_ref[span].astype(f32)
            out = att_ref[span].astype(f32)
            qt[b, p, :HD] = fold_heads(block).astype(bf16)
            qt[b, p, HD:] = jnp.zeros((HD, 2 * BLOCK), bf16)
            wide = fold_heads(grad)
            dot_[b, p, :HD] = jnp.zeros((HD, 2 * BLOCK), bf16)
            dot_[b, p, HD:] = wide.astype(bf16)
            delta[b, p] = jnp.broadcast_to(
                jnp.sum(wide * fold_heads(out), 0, keepdims=True), (8, 2 * BLOCK)
            )
            qn[b, p, :BLOCK] = jnp.concatenate([block[:, :HD], zeros], 1).astype(bf16)
            qn[b, p, BLOCK:] = jnp.concatenate([block[:, HD:], zeros], 1).astype(bf16)
            don[b, p, :BLOCK] = jnp.concatenate([zeros, grad[:, :HD]], 1).astype(bf16)
            don[b, p, BLOCK:] = jnp.concatenate([zeros, grad[:, HD:]], 1).astype(bf16)
    for k in range(BLOCKS):
        kt[k] = kv_ref[k * BLOCK : (k + 1) * BLOCK].astype(f32).T[:HD].astype(bf16)
    dkv[...] = jnp.zeros_like(dkv)

    for b in range(2):
        place, low, count = block_plan(plan, order_ref, b)
        dq[...] = jnp.zeros_like(dq)

        def step(t, carry):
            initial = jnp.where(t == count - 1, place, low + t)
            stored = inverse[initial]
            rows = kv_ref[pl.ds(pl.multiple_of(stored * BLOCK, BLOCK), BLOCK)]
            keys = kt[stored]
            bias = block_bias(plan, place, initial)
            total = dkv[stored]
            for p in range(PAIRS):
                value = mm(rows, qt[b, p]) + bias
                probs = jnp.exp(value - lse_ref[b, p, 0:1])
                grad = probs * (mm(rows, dot_[b, p]) - delta[b, p, 0:1])
                low_probs = probs.astype(bf16)
                low_grad = grad.astype(bf16)
                dq[p] += mm(keys, low_grad)
                total = total + mm(low_grad, qn[b, p]) + mm(low_probs, don[b, p])
            dkv[stored] = total
            return carry

        lax.fori_loop(0, count, step, 0)
        for p in range(PAIRS):
            gq_ref[b * BLOCK : (b + 1) * BLOCK, p * BLOCK : (p + 1) * BLOCK] = unfold_heads(
                dq[p] * 0.125
            ).astype(bf16)
    for k in range(BLOCKS):
        grad_ref[k] = dkv[k].astype(bf16)
    gwq[...] = mm(one_ref[...].astype(f32).T.astype(bf16), gq_ref[...]).astype(bf16)
    deal_rows(gwq, keep_ref, send_ref)


def deal_rows(source, keep_ref, send_ref):
    for k in range(8):
        keep_ref[k] = source[row_span(k, 0), :]
        send_ref[k] = source[row_span(k, 1), :]


def middle_kernel(
    feed_ref,
    wout_ref,
    x_ref,
    ct_ref,
    att_ref,
    vec_ref,
    fcb_ref,
    out_ref,
    gmid_ref,
    gatt_ref,
    sums_ref,
    hidden_ref,
    grad_ref,
    wf,
    wg,
    gf,
    in_sem,
    out_sem,
    last_sem,
    gout,
    x2,
    x2t,
    branch,
    gin,
    mid,
    fcsum,
):
    def columns(c, start=0):
        return pl.ds(pl.multiple_of(start + c * COLS, BLOCK), COLS)

    def loads(c, slot):
        return (
            pltpu.make_async_copy(feed_ref.at[:, columns(c)], wf.at[slot], in_sem.at[slot, 0]),
            pltpu.make_async_copy(feed_ref.at[:, columns(c, FF)], wg.at[slot], in_sem.at[slot, 1]),
        )

    def store(c, slot):
        return pltpu.make_async_copy(gf.at[slot], grad_ref.at[:, columns(c, D)], out_sem.at[slot])

    def start(copies):
        for copy in copies:
            copy.start()

    start(loads(0, 0))
    vec = vec_ref[...]
    att = att_ref[...]
    middle = x_ref[...].astype(f32) + (mm_nt(att, wout_ref[...]) + vec[3:4])
    mid[...] = middle
    normed, factor = normalize(middle)
    two = (normed * vec[4:5] + vec[5:6]).astype(bf16)
    x2[...] = two
    x2t[...] = two.astype(f32).T.astype(bf16)
    branch[...] = jnp.zeros_like(branch)
    gin[...] = jnp.zeros_like(gin)

    def chunk(c, carry):
        slot = lax.rem(c, 2)

        @pl.when(c + 1 < 8)
        def _():
            start(loads(c + 1, 1 - slot))

        for copy in loads(c, slot):
            copy.wait()
        span = columns(c)
        w_fc = wf[slot]
        w_proj = wg[slot]
        pre = mm(x2[...], w_fc) + fcb_ref[:, span]
        square = pre * pre
        tanh = jnp.tanh(0.7978845608028654 * (pre + 0.044715 * (pre * square)))
        half = 0.5 * (1.0 + tanh)
        hidden = (pre * half).astype(bf16)
        slope = half + (0.5 * pre) * (1.0 - tanh * tanh) * (
            0.7978845608028654 + (3 * 0.044715 * 0.7978845608028654) * square
        )
        hidden_ref[:, span] = hidden
        branch[...] += mm_nt(hidden, w_proj)
        grad_pre = (mm(ct_ref[...], w_proj) * slope).astype(bf16)
        gin[...] += mm_nt(grad_pre, w_fc)
        fcsum[:, span] = jnp.sum(grad_pre.astype(f32), 0, keepdims=True)

        @pl.when(c >= 2)
        def _():
            store(c - 2, slot).wait()

        gf[slot] = mm(x2t[...], grad_pre).astype(bf16)
        store(c, slot).start()
        return carry

    lax.fori_loop(0, 8, chunk, 0)
    middle = mid[...]
    cot = ct_ref[...].astype(f32)
    out_ref[...] = (middle + (branch[...] + vec[6:7])).astype(bf16)
    normed, factor = normalize(middle)
    grad_two = gin[...]
    grad_middle = cot + norm_back(grad_two * vec[4:5], normed, factor)
    gmid_ref[...] = grad_middle
    grad_branch = grad_middle.astype(bf16)
    gatt_ref[...] = mm(grad_branch, wout_ref[...]).astype(bf16)
    gout[...] = mm(grad_branch.astype(f32).T.astype(bf16), att).astype(bf16)
    out = pltpu.make_async_copy(gout, grad_ref.at[:, :D], last_sem)
    out.start()
    sums_ref[0:4] = jnp.concatenate(
        [
            jnp.sum(grad_branch.astype(f32), 0, keepdims=True),
            jnp.sum(grad_two * normed, 0, keepdims=True),
            jnp.sum(grad_two, 0, keepdims=True),
            jnp.sum(cot, 0, keepdims=True),
        ],
        0,
    )
    gather = four_apart(512, BLOCK, 1)
    mine = lax.broadcasted_iota(jnp.int32, (4, 512), 0) == (
        lax.broadcasted_iota(jnp.int32, (4, 512), 1) % 4
    )
    for g in range(6):
        high, low = split_low(jnp.where(mine, fcsum[:, g * 512 : (g + 1) * 512], 0.0))
        sums_ref[4:8, g * BLOCK : (g + 1) * BLOCK] = mm(high, gather) + mm(low, gather)
    store(6, 0).wait()
    store(7, 1).wait()
    out.wait()


def rest_kernel(ct_ref, hidden_ref, keep_ref, send_ref, turned, grad):
    turned[...] = ct_ref[...].astype(f32).T.astype(bf16)
    for j in range(4):
        grad[...] = mm(turned[...], hidden_ref[:, j * SLICE : (j + 1) * SLICE]).astype(bf16)
        deal_rows(grad, keep_ref.at[j], send_ref.at[j])


def last_kernel(
    x_ref,
    one_ref,
    gq_ref,
    gmid_ref,
    wq_ref,
    early_ref,
    vec_ref,
    sums_ref,
    dkv_ref,
    gx_ref,
    keep_ref,
    send_ref,
    pack_ref,
):
    gkv = jnp.sum(dkv_ref[...].astype(f32), 0).astype(bf16)
    gq = gq_ref[...]
    vec = vec_ref[...]
    grad_one = mm_nt(gq, wq_ref[...]) + mm_nt(gkv, early_ref[:, :BLOCK])
    normed, factor = normalize(x_ref[...].astype(f32))
    gx_ref[...] = (gmid_ref[...] + norm_back(grad_one * vec[0:1], normed, factor)).astype(bf16)
    pack_ref[:, :BLOCK] = mm(one_ref[...].astype(f32).T.astype(bf16), gkv).astype(bf16)
    sums = sums_ref[...]
    rows = jnp.concatenate(
        [
            jnp.sum(grad_one * normed, 0, keepdims=True),
            jnp.sum(grad_one, 0, keepdims=True),
            jnp.sum(gq.astype(f32), 0, keepdims=True),
            sums,
            jnp.zeros((5, D), f32),
        ],
        0,
    )
    high, low = split_low(rows)
    value = jnp.sum(gkv.astype(f32), 0, keepdims=True)[:, HD:]
    value_high, value_low = split_low(value)
    lane = lax.broadcasted_iota(jnp.int32, (16, HD), 1)
    mine = (lane & 15) == lax.broadcasted_iota(jnp.int32, (16, HD), 0)
    group = lax.broadcasted_iota(jnp.int32, (HD, D), 0) // 16
    spread = jnp.where(group == lax.broadcasted_iota(jnp.int32, (HD, D), 1) % 6, 1.0, 0.0).astype(bf16)
    put_high = mm(jnp.where(mine, value_high.astype(f32), 0.0).astype(bf16), spread)
    put_low = mm(jnp.where(mine, value_low.astype(f32), 0.0).astype(bf16), spread)
    packed = jnp.concatenate(
        [high.astype(f32), low.astype(f32), put_high, put_low, jnp.zeros((64, D), f32)], 0
    )
    pack_ref[:, BLOCK:] = packed.T.astype(bf16)
    deal_rows(pack_ref, keep_ref, send_ref)


SMEM = pl.BlockSpec(memory_space=pltpu.SMEM)
VMEM = pl.BlockSpec(memory_space=pltpu.VMEM)
ANY = pl.BlockSpec(memory_space=pl.ANY)


def shape(*dims, dtype=bf16):
    return jax.ShapeDtypeStruct(dims, dtype)


def add_all(parts, dtype=bf16):
    total = parts[0].astype(f32)
    for part in parts[1:]:
        total = total + part.astype(f32)
    return total.astype(dtype)


def call(kernel, name, outs, args, scratch=(), smem=0, hbm=(), hbm_out=0, flops=0, moved=0, exps=0):
    places = [SMEM if i < smem else ANY if i in hbm else VMEM for i in range(len(args))]
    return pl.pallas_call(
        kernel,
        out_shape=outs,
        in_specs=places,
        out_specs=[VMEM] * (len(outs) - hbm_out) + [ANY] * hbm_out,
        scratch_shapes=list(scratch),
        compiler_params=pltpu.CompilerParams(vmem_limit_bytes=56 * 1024 * 1024),
        cost_estimate=pl.CostEstimate(flops=flops, bytes_accessed=moved, transcendentals=exps),
        name=name,
    )(*args)


def tie(value, after):
    return lax.optimization_barrier((value, after))[0]


def local(
    layer_input,
    cotangent,
    lengths,
    order,
    files,
    ln1_gain,
    ln1_bias,
    w_attn,
    query_bias,
    value_bias,
    w_out,
    out_bias,
    ln2_gain,
    ln2_bias,
    w_fc,
    fc_bias,
    w_proj,
    proj_bias,
):
    x = layer_input[0]
    cot = cotangent[0]
    vectors = [ln1_gain, ln1_bias, query_bias, out_bias, ln2_gain, ln2_bias, proj_bias, fc_bias]
    (pieces,) = call(
        piece_kernel,
        "pieces",
        [shape(8, 6, WIDE)],
        [*vectors, w_attn, w_out, w_fc, w_proj],
        smem=8,
        moved=2_000_000,
    )
    attn_block, feed_block = call(
        block_kernel,
        "blocks",
        [shape(8, ROWS, FC), shape(ROWS, 2 * FF)],
        [lax.all_to_all(pieces, CTX, 0, 0)],
        [pltpu.VMEM((ROWS, WIDE), f32)],
        moved=4_000_000,
    )
    feed = lax.all_gather(feed_block, DP, axis=0, tiled=True)
    attn = lax.all_to_all(attn_block, ("x", "zl"), 0, 0)
    one, kv, vec, fcb, wq, wout, early = call(
        first_kernel,
        "first",
        [
            shape(TOK, D),
            shape(8, TOK, BLOCK),
            shape(16, D, dtype=f32),
            shape(1, FF, dtype=f32),
            shape(D, D),
            shape(D, D),
            shape(D, 2 * BLOCK),
        ],
        [x, value_bias[None], attn, send(attn, dc=1)],
        flops=100_000_000,
        moved=8_000_000,
    )
    kv = lax.all_to_all(kv, CTX, 0, 0).reshape(LENGTH, BLOCK)

    wide = (2, PAIRS, BLOCK, 2 * BLOCK)
    plan = [lengths, order, files]
    q, att, lse = call(
        forward_kernel,
        "attend",
        [shape(TOK, D), shape(TOK, D), shape(2, PAIRS, 8, 2 * BLOCK, dtype=f32)],
        [*plan, one, wq, vec, kv],
        [
            pltpu.SMEM((BLOCKS,), jnp.int32),
            pltpu.VMEM(wide, bf16),
            pltpu.VMEM((BLOCKS, HD, BLOCK), bf16),
            pltpu.VMEM((BLOCKS, PAIRS, BLOCK, 2 * BLOCK), f32),
            pltpu.VMEM((PAIRS, HD, 2 * BLOCK), f32),
        ],
        smem=2,
        flops=10_000_000_000,
        moved=4_000_000,
        exps=6_000_000,
    )
    output, grad_middle, grad_att, sums, hidden, grad_feed = call(
        middle_kernel,
        "feed",
        [
            shape(TOK, D),
            shape(TOK, D, dtype=f32),
            shape(TOK, D),
            shape(8, D, dtype=f32),
            shape(TOK, FF),
            shape(D, D + FF),
        ],
        [feed, wout, x, cot, att, vec, fcb],
        [
            pltpu.VMEM((2, D, COLS), bf16),
            pltpu.VMEM((2, D, COLS), bf16),
            pltpu.VMEM((2, D, COLS), bf16),
            pltpu.SemaphoreType.DMA((2, 2)),
            pltpu.SemaphoreType.DMA((2,)),
            pltpu.SemaphoreType.DMA,
            pltpu.VMEM((D, D), bf16),
            pltpu.VMEM((TOK, D), bf16),
            pltpu.VMEM((D, TOK), bf16),
            pltpu.VMEM((TOK, D), f32),
            pltpu.VMEM((TOK, D), f32),
            pltpu.VMEM((TOK, D), f32),
            pltpu.VMEM((1, FF), f32),
        ],
        hbm=(0,),
        hbm_out=1,
        flops=8_000_000_000,
        moved=30_000_000,
        exps=1_000_000,
    )
    grad_feed = lax.psum_scatter(grad_feed, DP, scatter_dimension=0, tiled=True)
    half = shape(8, ROWS, D)
    sliced = shape(4, 8, ROWS, SLICE)
    keep_proj, send_proj = call(
        rest_kernel,
        "rest",
        [sliced, sliced],
        [cot, hidden],
        [pltpu.VMEM((D, TOK), bf16), pltpu.VMEM((D, D), bf16)],
        flops=1_500_000_000,
        moved=8_000_000,
    )
    got_proj = send(send_proj, dc=1)
    grad_proj = add_all([keep_proj, got_proj])
    grad_att = tie(grad_att, grad_proj)
    grad_proj = add_all(list(lax.all_to_all(grad_proj, "y", 0, 0)))

    gq, keep_q, send_q, grad_kv = call(
        backward_kernel,
        "attend_back",
        [shape(TOK, D), half, half, shape(BLOCKS, BLOCK, BLOCK)],
        [*plan, q, grad_att, att, lse, one, kv],
        [
            pltpu.SMEM((BLOCKS,), jnp.int32),
            pltpu.VMEM(wide, bf16),
            pltpu.VMEM(wide, bf16),
            pltpu.VMEM((2, PAIRS, 2 * BLOCK, BLOCK), bf16),
            pltpu.VMEM((2, PAIRS, 2 * BLOCK, BLOCK), bf16),
            pltpu.VMEM((BLOCKS, HD, BLOCK), bf16),
            pltpu.VMEM((2, PAIRS, 8, 2 * BLOCK), f32),
            pltpu.VMEM((PAIRS, HD, 2 * BLOCK), f32),
            pltpu.VMEM((BLOCKS, BLOCK, BLOCK), f32),
            pltpu.VMEM((D, D), bf16),
        ],
        smem=2,
        flops=20_000_000_000,
        moved=6_000_000,
        exps=6_000_000,
    )
    grad_kv = tie(grad_kv.reshape(8, TOK, BLOCK), grad_proj)
    grad_kv = lax.all_to_all(grad_kv, CTX, 0, 0)
    grad_q = add_all([keep_q, send(send_q, dc=1)])

    thin = shape(8, ROWS, 2 * BLOCK)
    grad_x, keep_pack, send_pack = call(
        last_kernel,
        "last",
        [shape(TOK, D), thin, thin],
        [x, one, gq, grad_middle, wq, early, vec, sums, grad_kv],
        [pltpu.VMEM((D, 2 * BLOCK), bf16)],
        flops=1_000_000_000,
        moved=5_000_000,
    )
    grad_pack = add_all([keep_pack, send(send_pack, dc=1)])
    parts = [grad_pack, grad_proj, grad_q]
    both = lax.all_to_all(jnp.concatenate(parts, 2), ("x", "zl"), 0, 0)
    (pieces,) = call(
        unblock_kernel,
        "unblock",
        [shape(8, 6, G_WIDE)],
        [both, grad_feed],
        [pltpu.VMEM((ROWS, G_WIDE), f32)],
    )
    results = call(
        finish_kernel,
        "finish",
        [
            shape(6, D + BLOCK, dtype=f32),
            shape(6, D, dtype=f32),
            shape(6, FF, dtype=f32),
            shape(6, FF, dtype=f32),
        ]
        + [shape(1, 6, dtype=f32)] * 7
        + [shape(1, 24, dtype=f32), shape(4, 16, dtype=f32)],
        [lax.all_to_all(pieces, CTX, 0, 0)],
    )
    grad_w_attn, grad_w_out, grad_w_fc, grad_w_proj = results[:4]
    gain_one, bias_one, bias_query, bias_out, gain_two, bias_two, bias_proj, bias_fc = (
        value.reshape(-1) for value in results[4:12]
    )
    return (
        output[None],
        grad_x[None],
        gain_one,
        bias_one,
        grad_w_attn,
        bias_query,
        results[12].reshape(HD),
        grad_w_out,
        bias_out,
        gain_two,
        bias_two,
        grad_w_fc,
        bias_fc,
        grad_w_proj,
        bias_proj,
    )


def solution(mesh):
    cells = Mesh(mesh.devices.reshape(SIZES), AXES)
    every = P(AXES)
    tall = P(AXES, None)
    tokens = P(DP, CTX, None)
    in_specs = (
        tokens,
        tokens,
        P(DP),
        P(DP, None),
        P(DP, None),
        every,
        every,
        tall,
        every,
        P(),
        tall,
        every,
        every,
        every,
        tall,
        every,
        tall,
        every,
    )
    out_specs = (
        tokens,
        tokens,
        every,
        every,
        tall,
        every,
        P(),
        tall,
        every,
        every,
        every,
        tall,
        every,
        tall,
        every,
    )
    return jax.shard_map(local, mesh=cells, in_specs=in_specs, out_specs=out_specs, check_vma=False)
```

time: 373 us -> 262 us (0.70); the launches traced: 371 us -> 267 us
  blocking collectives: 0 us -> 132 us
  starting transfers between devices: 139 us -> 8.07 us
  waiting for transfers between devices: 139 us -> 31.5 us
  Pallas kernels: 41.3 us -> 73.6 us
  local copies, waits for them, and re-layouts: 33 us -> 3.15 us
  between operations: 1.73 us -> 14.8 us
  other arithmetic: 16 us -> 4.24 us
    all_to_all x0 -> x5, blocking collectives: none -> 132 us  [the longest x2 41.6 us: local(): lax.all_to_all(pieces, CTX, 0, 0)]
    ppermute x40 -> x4, waiting for transfers between devices: 91.2 us -> 9.4 us  [send(): return lax.ppermute(value, AXES, route(**shift))]
    all_to_all x10 -> x2, starting transfers between devices: 82.4 us -> 7.61 us  [the longest x1 4.12 us: local(): grad_proj = add_all(list(lax.all_to_all(grad_proj, 'y', 0, 0)))]
    ppermute x40 -> x4, starting transfers between devices: 56.8 us -> 0.38 us  [send(): return lax.ppermute(value, AXES, route(**shift))]
    pallas_call x5 -> x10, Pallas kernels: 41.3 us -> 73.6 us  [call(): pl.pallas_call(kernel, out_shape=outs, in_specs=places, out_specs=[VMEM]...]
    all_to_all x10 -> x2, waiting for transfers between devices: 48.1 us -> 20.4 us  [the longest x1 11.2 us: local(): kv = lax.all_to_all(kv, CTX, 0, 0).reshape(LENGTH, BLOCK)]
    reshape x14 -> x1, local copies, waits for them, and re-layouts: 12.2 us -> 1.26 us  [local(): results[12].reshape(HD)]
    convert_element_type x6 -> x3, other arithmetic: 10.4 us -> 3.86 us  [add_all(): return total.astype(dtype)]
  transfers between devices with their start and end apart: 50 -> 8, of which waited for: 19 -> 6; matrix products, arithmetic and copies ran while one was open for 12% -> 2% of each run, Pallas kernels for 5% -> 16%
where the time goes in v2:
time: 262 us; the launch traced here: 267 us
  blocking collectives  132 us (50%)
  Pallas kernels  73.6 us (28%)
  waiting for transfers between devices  31.5 us (12%)
  between operations  14.8 us (6%)
  starting transfers between devices  8.07 us (3%)
  other arithmetic  4.24 us (2%)
  local copies, waits for them, and re-layouts  3.15 us (1%)
    pallas_call x10, Pallas kernels, call(): pl.pallas_call(kernel, out_shape=outs, in_specs=places, out_specs=[VMEM]...  73.6 us
    all_to_all x2, blocking collectives, local(): lax.all_to_all(pieces, CTX, 0, 0)  41.6 us
    all_to_all x1, blocking collectives, local(): attn = lax.all_to_all(attn_block, ('x', 'zl'), 0, 0)  35.9 us
    all_to_all x1, blocking collectives, local(): grad_kv = lax.all_to_all(grad_kv, CTX, 0, 0)  31.2 us
    all_to_all x1, blocking collectives, local(): both = lax.all_to_all(jnp.concatenate(parts, 2), ('x', 'zl'), 0, 0)  23 us
    all_to_all x1, waiting for transfers between devices, local(): kv = lax.all_to_all(kv, CTX, 0, 0).reshape(LENGTH, BLOCK)  11.2 us
    ppermute x4, waiting for transfers between devices, send(): return lax.ppermute(value, AXES, route(**shift))  9.4 us
    all_to_all x1, waiting for transfers between devices, local(): grad_proj = add_all(list(lax.all_to_all(grad_proj, 'y', 0, 0)))  9.28 us
  transfers between devices with their start and end apart: 8, of which 6 were waited for; matrix products, arithmetic and copies ran while one was open for 2% of the time, Pallas kernels for 16%

profile of v2, /device:TPU:0, one launch (start us, length us, event | category | flops | bytes accessed | tf_op | source)
XLA Modules:
  0.0 267.0 jit_solution(1966290541466293076)
XLA Ops:
  7.2 2.0 pieces.1
  9.2 24.5 %all_to_all.35.piece_ref = bf16[8,6,7936]{2,1,0:T(8,128)(2,1)} all-to-all(bf16[8,6,7936]{2,1,0:T(8,128)(2,1)} %pieces.1), channel_id=1, replica_groups=mesh['x'=4,'zl'=2,'core'=2,'y'=4,'zh'=2] {'y','zh'}, dimensions={0} | all-to-all | bytes 1523712 | tf_op jit(solution)/shard_map/all_to_all | solution.py:626
  33.7 2.8 %blocks.1 = (bf16[8,48,1792]{2,1,0:T(8,128)(2,1)}, bf16[48,6144]{1,0:T(8,128)(2,1)}) custom-call(bf16[8,6,7936]{2,1,0:T(8,128)(2,1)} %all_to_all.35.piece_ref), custom_call_target="tpu_custom_call" | custom-call | bytes 4000000 | tf_op jit(solution)/shard_map/blocks/pallas_call | solution.py:575
  36.5 35.9 %all_to_all.36.mine_ref = bf16[8,48,1792]{2,1,0:T(8,128)(2,1)S(1)} all-to-all(bf16[8,48,1792]{2,1,0:T(8,128)(2,1)} %get-tuple-element.58), channel_id=1, replica_groups=mesh['x'=4,'zl'=2,'core'=2,'y'=4,'zh'=2] {'x','zl'}, dimensions={0} | all-to-all | bytes 2752512 | tf_op jit(solution)/shard_map/all_to_all | solution.py:631
  72.5 3.5 %collective-permute-done.other_ref = bf16[8,48,1792]{2,1,0:T(8,128)(2,1)S(1)} collective-permute-done((bf16[8,48,1792]{2,1,0:T(8,128)(2,1)S(1)}, bf16[8,48,1792]{2,1,0:T(8,128)(2,1)S(1)}, u32[]{:S(2)}, u32[]{:S(2)}) %collective-permute-start) | collective-permute-done | bytes 1376288 | tf_op jit(solution)/shard_map/ppermute | solution.py:45
  77.1 4.2 %first.1 = (bf16[256,768]{1,0:T(8,128)(2,1)}, bf16[8,256,128]{2,1,0:T(8,128)(2,1)}, f32[16,768]{1,0:T(8,128)}, f32[1,3072]{1,0:T(1,128)}, bf16[768,768]{1,0:T(8,...) custom-call(bf16[256,768]{1,0:T(8,128)(2,1)} %bitcast.17, f32[1,64]{1,0:T(1,128)} %bitcast.23, ...), custom_call_target="tpu_custom_call" | custom-call | flops 100000000 | bytes 8000000 | tf_op jit(solution)/shard_map/first/pallas_call | solution.py:575
  81.3 3.5 %all-to-all-start.2 = ((bf16[8,256,128]{2,1,0:T(8,128)(2,1)}), bf16[8,256,128]{2,1,0:T(8,128)(2,1)S(1)}, u32[]{:S(2)}, u32[]{:S(2)}) async-start(bf16[8,256,128]{2,1,0:T(8,128)(2,1)} %get-tuple-element.63), calls=%async_computation.2 | async-start | bytes 1048576 | tf_op jit(solution)/shard_map/all_to_all | solution.py:648
  85.5 11.2 %all-to-all-done.2 = bf16[8,256,128]{2,1,0:T(8,128)(2,1)S(1)} async-done(((bf16[8,256,128]{2,1,0:T(8,128)(2,1)}), bf16[8,256,128]{2,1,0:T(8,128)(2,1)S(1)}, u32[]{:S(2)}, u32[]{:S(2)}) %all-to-all-start.2) | async-done | bytes 524320 | tf_op jit(solution)/shard_map/all_to_all | solution.py:648
  97.4 9.4 %attend.1 = (bf16[256,768]{1,0:T(8,128)(2,1)}, bf16[256,768]{1,0:T(8,128)(2,1)}, f32[2,6,8,256]{3,2,1,0:T(8,128)}) custom-call(s32[1]{0:T(128)S(6)} %copy.33.length_ref, s32[1,16]{1,0:T(1,128)} %order_ref.3, s32[1,2048]{1,0:T(1,128)} %files_ref.3, bf16[256,768]{1,0:T(8,128)(2,1)} %get-tuple-element.60.one_ref, bf16[768,768]{1,0:T(8,128)(2,1)} %get-tuple-element.61.wq_ref, ...), custom_call_target="tpu_custom_call" | custom-call | flops 10000000000 | bytes 4000000 | tf_op jit(solution)/shard_map/attend/pallas_call | solution.py:575
  106.8 1.6 all-gather.2.cloned.1.call-done.feed_ref
  108.4 20.1 %feed.1 = (bf16[256,768]{1,0:T(8,128)(2,1)}, f32[256,768]{1,0:T(8,128)}, bf16[256,768]{1,0:T(8,128)(2,1)}, f32[8,768]{1,0:T(8,128)}, bf16[256,3072]{1,0:T(8,128)(2,1)}, /*index=5*/bf16[768,3840]{1,0:T(8,128)(2,1)}) custom-call(bf16[768,6144]{1,0:T(8,128)(2,1)} %all-gather.2.cloned.1.call-done.feed_ref, bf16[768,768]{1,0:T(8,128)(2,1)} %get-tuple-element.59.wout_ref, ...), custom_call_target="tpu_custom_call" | custom-call | flops 8000000000 | bytes 30000000 | tf_op jit(solution)/shard_map/feed/pallas_call | solution.py:575
  128.6 5.9 %rest.1 = (bf16[4,8,48,768]{3,2,1,0:T(8,128)(2,1)}, bf16[4,8,48,768]{3,2,1,0:T(8,128)(2,1)}) custom-call(bf16[256,768]{1,0:T(8,128)(2,1)} %bitcast.25, bf16[256,3072]{1,0:T(8,128)(2,1)} %get-tuple-element.69.hidden_ref), custom_call_target="tpu_custom_call" | custom-call | flops 1500000000 | bytes 8000000 | tf_op jit(solution)/shard_map/rest/pallas_call | solution.py:575
  134.8 4.4 %collective-permute-done.1 = bf16[4,8,48,768]{3,2,1,0:T(8,128)(2,1)S(1)} collective-permute-done((bf16[4,8,48,768]{3,2,1,0:T(8,128)(2,1)}, bf16[4,8,48,768]{3,2,1,0:T(8,128)(2,1)S(1)}, u32[]{:S(2)}, u32[]{:S(2)}) %collective-permute-start.1) | collective-permute-done | bytes 2359328 | tf_op jit(solution)/shard_map/ppermute | solution.py:45
  139.2 3.7 %add_convert_fusion = bf16[4,8,48,768]{3,2,1,0:T(8,128)(2,1)} fusion(bf16[4,8,48,768]{3,2,1,0:T(8,128)(2,1)S(1)} %collective-permute-done.1, bf16[4,8,48,768]{3,2,1,0:T(8,128)(2,1)} %get-tuple-element.70), kind=kLoop, calls=%fused_computation | loop fusion | flops 4718592 | bytes 7077888 | tf_op jit(solution)/shard_map/convert_element_type | solution.py:570
  142.8 4.1 %all-to-all-start.3 = ((bf16[4,8,48,768]{3,2,1,0:T(8,128)(2,1)}), bf16[4,8,48,768]{3,2,1,0:T(8,128)(2,1)S(1)}, u32[]{:S(2)}, u32[]{:S(2)}) async-start(bf16[4,8,48,768]{3,2,1,0:T(8,128)(2,1)} %add_convert_fusion), calls=%async_computation.3 | async-start | bytes 4718592 | tf_op jit(solution)/shard_map/all_to_all | solution.py:717
  147.0 20.4 %attend_back.1 = (bf16[256,768]{1,0:T(8,128)(2,1)}, bf16[8,48,768]{2,1,0:T(8,128)(2,1)}, bf16[8,48,768]{2,1,0:T(8,128)(2,1)}, bf16[16,128,128]{2,1,0:T(8,128)(2,1)}) custom-call(s32[1]{0:T(128)S(6)} %copy.33.length_ref, s32[1,16]{1,0:T(1,128)} %order_ref.3, s32[1,2048]{1,0:T(1,128)} %files_ref.3, bf16[256,768]{1,0:T(8,128)(2,1)} %get-tuple-element.67.q_ref, ...), custom_call_target="tpu_custom_call" | custom-call | flops 20000000000 | bytes 6000000 | tf_op jit(solution)/shard_map/attend_back/pallas_call | solution.py:575
  167.4 9.3 %all-to-all-done.3 = bf16[4,8,48,768]{3,2,1,0:T(8,128)(2,1)S(1)} async-done(((bf16[4,8,48,768]{3,2,1,0:T(8,128)(2,1)}), bf16[4,8,48,768]{3,2,1,0:T(8,128)(2,1)S(1)}, u32[]{:S(2)}, u32[]{:S(2)}) %all-to-all-start.3) | async-done | bytes 2359328 | tf_op jit(solution)/shard_map/all_to_all | solution.py:717
  176.9 31.2 %all_to_all.37.dkv_ref = bf16[8,256,128]{2,1,0:T(8,128)(2,1)} all-to-all(bf16[8,256,128]{2,1,0:T(8,128)(2,1)S(1)} %bitcast.22), channel_id=1, replica_groups=mesh['x'=4,'zl'=2,'core'=2,'y'=4,'zh'=2] {'y','zh'}, dimensions={0} | all-to-all | bytes 1048576 | tf_op jit(solution)/shard_map/all_to_all | solution.py:742
  208.2 4.2 %last.1 = (bf16[256,768]{1,0:T(8,128)(2,1)}, bf16[8,48,256]{2,1,0:T(8,128)(2,1)}, bf16[8,48,256]{2,1,0:T(8,128)(2,1)}) custom-call(bf16[256,768]{1,0:T(8,128)(2,1)} %bitcast.19, bf16[256,768]{1,0:T(8,128)(2,1)} %get-tuple-element.60.one_ref, bf16[256,768]{1,0:T(8,128)(2,1)} %get-tuple-element.74.gq_ref, f32[256,768]{1,0:T(8,128)} %get-tuple-element.75.gmid_ref, ...), custom_call_target="tpu_custom_call" | custom-call | flops 1000000000 | bytes 5000000 | tf_op jit(solution)/shard_map/last/pallas_call | solution.py:575
  212.5 1.5 collective-permute-done.2
  214.1 23.0 %all_to_all.38.attn_ref = bf16[8,48,1792]{2,1,0:T(8,128)(2,1)} all-to-all(bf16[8,48,1792]{2,1,0:T(8,128)(2,1)S(1)} %pad_maximum_fusion), channel_id=1, replica_groups=mesh['x'=4,'zl'=2,'core'=2,'y'=4,'zh'=2] {'x','zl'}, dimensions={0} | all-to-all | bytes 2752512 | tf_op jit(solution)/shard_map/all_to_all | solution.py:757
  237.1 2.7 %unblock.1 = bf16[8,6,5632]{2,1,0:T(8,128)(2,1)} custom-call(bf16[8,48,1792]{2,1,0:T(8,128)(2,1)} %all_to_all.38.attn_ref, bf16[48,3840]{1,0:T(8,128)(2,1)} %reduce-scatter.2.cloned.1.call-done.feed_ref), custom_call_target="tpu_custom_call" | custom-call | tf_op jit(solution)/shard_map/unblock/pallas_call | solution.py:575
  239.8 17.1 %all_to_all.39.piece_ref = bf16[8,6,5632]{2,1,0:T(8,128)(2,1)} all-to-all(bf16[8,6,5632]{2,1,0:T(8,128)(2,1)} %unblock.1), channel_id=1, replica_groups=mesh['x'=4,'zl'=2,'core'=2,'y'=4,'zh'=2] {'y','zh'}, dimensions={0} | all-to-all | bytes 1081344 | tf_op jit(solution)/shard_map/all_to_all | solution.py:776
  256.9 2.1 finish.1
  (27 shorter events, 4.2 us)
Async XLA Ops:
  7.2 101.2 %all-gather.2.cloned.1.call-start = ((), (), s32[]{:S(2)}) async-start(), calls=%async_computation.8 | async-start | bytes 10027008 | tf_op jit(solution)/shard_map/all_gather | solution.py:630
  72.5 3.6 %copy-start = (bf16[8,48,1792]{2,1,0:T(8,128)(2,1)}, bf16[8,48,1792]{2,1,0:T(8,128)(2,1)S(1)}, u32[]{:S(2)}) copy-start(bf16[8,48,1792]{2,1,0:T(8,128)(2,1)S(1)} %all_to_all.36.mine_ref) | copy-start | bytes 4128772
  72.5 3.6 %collective-permute-start = (bf16[8,48,1792]{2,1,0:T(8,128)(2,1)S(1)}, bf16[8,48,1792]{2,1,0:T(8,128)(2,1)S(1)}, u32[]{:S(2)}, u32[]{:S(2)}) collective-permute-start(bf16[8,48,1792]{2,1,0:T(8,128)(2,1)S(1)} %all_to_all.36.mine_ref), channel_id=1, source_target_pairs={{0,8},{1,9},{2,10},{3,11},{4,12},{5,13},{6,14},{7,15},{8,0},{9,1},... | collective-permute-start | bytes 4128776 | tf_op jit(solution)/shard_map/ppermute | solution.py:45
  76.0 1.1 copy-start.1
  81.3 15.4 %all-to-all-start.2 = ((bf16[8,256,128]{2,1,0:T(8,128)(2,1)}), bf16[8,256,128]{2,1,0:T(8,128)(2,1)S(1)}, u32[]{:S(2)}, u32[]{:S(2)}) async-start(bf16[8,256,128]{2,1,0:T(8,128)(2,1)} %get-tuple-element.63), calls=%async_computation.2 | async-start | bytes 1048576 | tf_op jit(solution)/shard_map/all_to_all | solution.py:648
  84.8 152.3 %reduce-scatter.2.cloned.1.call-start = ((), (), s32[]{:S(2)}) async-start(), calls=%async_computation.9 | async-start | bytes 6266880 | tf_op jit(solution)/shard_map/reduce_scatter | solution.py:702
  96.6 0.8 copy-start.3
  134.4 4.7 %collective-permute-start.1 = (bf16[4,8,48,768]{3,2,1,0:T(8,128)(2,1)}, bf16[4,8,48,768]{3,2,1,0:T(8,128)(2,1)S(1)}, u32[]{:S(2)}, u32[]{:S(2)}) collective-permute-start(bf16[4,8,48,768]{3,2,1,0:T(8,128)(2,1)} %get-tuple-element.71), channel_id=1, source_target_pairs={{0,8},{1,9},{2,10},{3,11},{4,12},{5,13},{6,14},{7,15},{8,0},{9,1},... | collective-permute-start | bytes 7077896 | tf_op jit(solution)/shard_map/ppermute | solution.py:45
  142.8 33.8 %all-to-all-start.3 = ((bf16[4,8,48,768]{3,2,1,0:T(8,128)(2,1)}), bf16[4,8,48,768]{3,2,1,0:T(8,128)(2,1)S(1)}, u32[]{:S(2)}, u32[]{:S(2)}) async-start(bf16[4,8,48,768]{3,2,1,0:T(8,128)(2,1)} %add_convert_fusion), calls=%async_computation.3 | async-start | bytes 4718592 | tf_op jit(solution)/shard_map/all_to_all | solution.py:717
  167.3 9.6 %copy-start.4 = (bf16[16,128,128]{2,1,0:T(8,128)(2,1)S(1)}, bf16[16,128,128]{2,1,0:T(8,128)(2,1)}, u32[]{:S(2)}) copy-start(bf16[16,128,128]{2,1,0:T(8,128)(2,1)} %get-tuple-element.78) | copy-start | bytes 1572868
  167.3 45.0 %collective-permute-start.3 = (bf16[8,48,768]{2,1,0:T(8,128)(2,1)}, bf16[8,48,768]{2,1,0:T(8,128)(2,1)S(1)}, u32[]{:S(2)}, u32[]{:S(2)}) collective-permute-start(bf16[8,48,768]{2,1,0:T(8,128)(2,1)} %get-tuple-element.84), channel_id=1, source_target_pairs={{0,8},{1,9},{2,10},{3,11},{4,12},{5,13},{6,14},{7,15},{8,0},{9,1},... | collective-permute-start | bytes 1769480 | tf_op jit(solution)/shard_map/ppermute | solution.py:45
  208.2 4.2 %copy-start.2 = (bf16[8,48,768]{2,1,0:T(8,128)(2,1)S(1)}, bf16[8,48,768]{2,1,0:T(8,128)(2,1)}, u32[]{:S(2)}) copy-start(bf16[8,48,768]{2,1,0:T(8,128)(2,1)} %get-tuple-element.83) | copy-start | bytes 1769476
  212.3 1.7 copy-start.5
  212.3 1.7 collective-permute-start.2
Sparse Core Ops, SparseCore 0:
  36.7 71.7 all-gather.1
  128.7 80.3 reduce-scatter.1

commit v3 on v2

v3 whole, which is shorter than its diff:
```python
import functools

import jax
import jax.numpy as jnp
import numpy as np
from jax import lax
from jax.experimental import pallas as pl
from jax.experimental.pallas import tpu as pltpu
from jax.sharding import Mesh
from jax.sharding import PartitionSpec as P

D = 768
HEADS = 12
HD = 64
FF = 3072
TOK = 256
LENGTH = 2048
BLOCK = 128
BLOCKS = 16
PAIRS = 6
ROWS = 48
COLS = 384
NEG = -1e30

AXES = ("x", "zl", "core", "y", "zh")
SIZES = (4, 2, 2, 4, 2)
DP = ("x", "zl", "core")
CTX = ("y", "zh")

f32 = jnp.float32
bf16 = jnp.bfloat16


def route(dx=0, dy=0, dz=0, dc=0, dl=0, dh=0):
    pairs = []
    for device in range(128):
        x, zl, core, y, zh = (int(v) for v in np.unravel_index(device, SIZES))
        z = (zh * 2 + zl + dz) % 4
        target = ((x + dx) % 4, z % 2 ^ dl, core ^ dc, (y + dy) % 4, z // 2 ^ dh)
        pairs.append((device, int(np.ravel_multi_index(target, SIZES))))
    return pairs


def send(value, **shift):
    return lax.ppermute(value, AXES, route(**shift))


def row_span(group, other):
    core = lax.axis_index("core")
    return pl.ds(pl.multiple_of(group * 96 + (1 - core if other else core) * ROWS, 16), ROWS)


def row_copies(parts, lanes, target, sem):
    return [
        pltpu.make_async_copy(part.at[k, :, lanes], target.at[row_span(k, other)], sem)
        for k in range(8)
        for other, part in enumerate(parts)
    ]


def start(copies):
    for copy in copies:
        copy.start()


def finish(copies):
    for copy in copies:
        copy.wait()


def mm(left, right):
    return lax.dot_general(left, right, (((1,), (0,)), ((), ())), preferred_element_type=f32)


def mm_nt(left, right):
    return lax.dot_general(left, right, (((1,), (1,)), ((), ())), preferred_element_type=f32)


def normalize(values):
    center = values - jnp.mean(values, -1, keepdims=True)
    spread = jnp.mean(center * center, -1, keepdims=True)
    factor = lax.rsqrt(spread + 1e-05)
    return center * factor, factor


def norm_back(grad_normed, normed, factor):
    return factor * (
        grad_normed
        - jnp.mean(grad_normed, -1, keepdims=True)
        - normed * jnp.mean(grad_normed * normed, -1, keepdims=True)
    )


def split_low(values):
    high = values.astype(bf16)
    return high, (values - high.astype(f32)).astype(bf16)


SLICE = 768
KEYS, SMALL, QUERY, OUT, FC, PROJ, WIDE = 0, 128, 256, 1024, 1792, 4864, 7936
SENT = 512
REST = SLICE - SENT
G_PROJ, G_QUERY, G_FC, G_OUT, G_REST, G_WIDE = 256, 768, 1536, 4608, 5376, 6400
REDUCED = G_WIDE - G_FC


def piece_kernel(*refs):
    vectors, fcb_ref, attn_ref, out_ref, fc_ref, proj_ref, piece_ref = (refs[:7],) + refs[7:]
    row = lax.broadcasted_iota(jnp.int32, (8, BLOCK), 0)
    lane = lax.broadcasted_iota(jnp.int32, (8, BLOCK), 1)
    small = jnp.zeros((8, BLOCK), f32)
    for i in range(6):
        values = [ref[i] for ref in vectors] + [fcb_ref[4 * i + j] for j in range(4)]
        for j, value in enumerate(values):
            small = jnp.where((row == i) & (lane < 48) & ((lane & 15) == j), value, small)
    high = small.astype(bf16).astype(f32)
    middle = (small - high).astype(bf16).astype(f32)
    low = small - high - middle
    small = jnp.where(lane < 16, high, jnp.where(lane < 32, middle, low)).astype(bf16)[:6]
    for k in range(8):
        piece_ref[k, :, KEYS:SMALL] = attn_ref[:, D:]
        piece_ref[k, :, SMALL:QUERY] = small
        piece_ref[k, :, QUERY:OUT] = attn_ref[:, :D]
        piece_ref[k, :, OUT:FC] = out_ref[...]
        piece_ref[k, :, FC:PROJ] = fc_ref[...]
        piece_ref[k, :, PROJ:] = proj_ref[...]


def block_kernel(piece_ref, attn_ref, feed_ref, rows):
    for j in range(8):
        rows[6 * j : 6 * j + 6] = piece_ref[j].astype(f32)
    for k in range(8):
        attn_ref[k] = rows[:, :FC].astype(bf16)
    feed_ref[...] = rows[:, FC:].astype(bf16)


def unblock_kernel(attn_ref, mine_ref, other_ref, piece_ref, rows):
    rows[:, :G_FC] = jnp.sum(attn_ref[...].astype(f32), 0)
    rows[:, G_FC:] = mine_ref[lax.axis_index("zl")].astype(f32) + other_ref[...].astype(f32)
    for j in range(8):
        piece_ref[j] = rows[6 * j : 6 * j + 6].astype(bf16)


def finish_kernel(piece_ref, attn_ref, out_ref, fc_ref, proj_ref, *refs):
    vectors, fcb_ref, value_ref = refs[:7], refs[7], refs[8]
    total = jnp.sum(piece_ref[...].astype(f32), 0)
    attn_ref[:, :D] = total[:, G_QUERY:G_FC]
    attn_ref[:, D:] = total[:, KEYS:SMALL]
    out_ref[...] = total[:, G_OUT:G_REST]
    fc_ref[...] = total[:, G_FC:G_OUT]
    for j in range(4):
        proj_ref[:, j * SLICE + SENT : (j + 1) * SLICE] = total[
            :, G_REST + j * REST : G_REST + (j + 1) * REST
        ]
        proj_ref[:, j * SLICE : j * SLICE + SENT] = (
            piece_ref[2 * j, :, G_PROJ:G_QUERY].astype(f32)
            + piece_ref[2 * j + 1, :, G_PROJ:G_QUERY].astype(f32)
        )
    small = total[:, SMALL:QUERY]
    small = jnp.concatenate([small, jnp.zeros((2, BLOCK), f32)], 0).T
    rows = small[:16] + small[16:32]
    for j, ref in enumerate(vectors):
        ref[...] = rows[j : j + 1, :6]
    spread = jnp.where(
        lax.broadcasted_iota(jnp.int32, (8, 24), 1) // 4
        == lax.broadcasted_iota(jnp.int32, (8, 24), 0),
        1.0,
        0.0,
    )
    wide = jnp.dot(rows[7:11], spread, precision=lax.Precision.HIGHEST)
    mine = lax.broadcasted_iota(jnp.int32, (4, 24), 1) % 4 == lax.broadcasted_iota(
        jnp.int32, (4, 24), 0
    )
    fcb_ref[...] = jnp.sum(jnp.where(mine, wide, 0.0), 0, keepdims=True)
    value = total[:4, SMALL + 32 : SMALL + 48] + total[:4, SMALL + 48 : SMALL + 64]
    value_ref[...] = jnp.concatenate([value[j : j + 1] for j in range(4)], 1)


def four_apart(rows, columns, turned):
    return jnp.where(
        lax.broadcasted_iota(jnp.int32, (rows, columns), 1 - turned) // 4
        == lax.broadcasted_iota(jnp.int32, (rows, columns), turned),
        1.0,
        0.0,
    ).astype(bf16)


def first_kernel(
    x_ref, vbias_ref, mine_ref, other_ref, one_ref, kv_ref, vec_ref, fcb_ref, early_ref, sem
):
    copies = row_copies((mine_ref, other_ref), pl.ds(0, QUERY), early_ref, sem)
    start(copies)
    normed, _ = normalize(x_ref[...].astype(f32))
    finish(copies)
    turned = early_ref[:, BLOCK:].astype(f32).T
    vec = turned[0:16] + turned[16:32] + turned[32:48]
    vec_ref[...] = vec
    one = (normed * vec[0:1] + vec[1:2]).astype(bf16)
    one_ref[...] = one
    bias = jnp.concatenate([jnp.zeros((1, HD), f32), vbias_ref[...]], 1)
    kv = (mm(one, early_ref[:, :BLOCK]) + bias).astype(bf16)
    for k in range(8):
        kv_ref[k] = kv
    spread = four_apart(BLOCK, 512, 0)
    terms = turned[0:48].astype(bf16)
    term = lax.broadcasted_iota(jnp.int32, (48, 512), 0) % 16 - 7
    mine = term == lax.broadcasted_iota(jnp.int32, (48, 512), 1) % 4
    for g in range(6):
        wide = mm(terms[:, g * BLOCK : (g + 1) * BLOCK], spread)
        fcb_ref[:, g * 512 : (g + 1) * 512] = jnp.sum(
            jnp.where(mine, wide, 0.0), 0, keepdims=True
        )


def read_plan(length_ref, order_ref, files_ref):
    files = files_ref[...]
    bounds = [jnp.sum(jnp.where(files < f, 1, 0)) for f in (1, 2, 3)]
    return length_ref[0], bounds


def block_plan(plan, order_ref, b):
    length, bounds = plan
    own = lax.axis_index("y") * 2 + lax.axis_index("zh")
    place = order_ref[0, own * 2 + b]
    start = place * BLOCK
    first = jnp.int32(0)
    for bound in bounds:
        first = jnp.where(bound <= start, jnp.maximum(first, bound), first)
    low = first // BLOCK
    high = jnp.minimum(place - 1, (length - 1) // BLOCK)
    return place, low, jnp.maximum(high - low + 1, 0)


def own_bias(plan, place):
    length, bounds = plan
    lane = lax.broadcasted_iota(jnp.int32, (1, 2 * BLOCK), 1)
    query = place * BLOCK + (lane & (BLOCK - 1))
    first = jnp.zeros_like(query)
    for bound in bounds:
        first = jnp.where(bound <= query, jnp.maximum(first, bound), first)
    last = jnp.minimum(query, length - 1)
    key = place * BLOCK + lax.broadcasted_iota(jnp.int32, (BLOCK, 2 * BLOCK), 0)
    allowed = ((key >= first) & (key <= last)) | (key == query)
    return jnp.where(allowed, 0.0, NEG)


def file_of(plan, position):
    number = jnp.zeros_like(position)
    for bound in plan[1]:
        number = number + jnp.where(bound <= position, 1, 0)
    return number


def place_keys(plan, order_ref, kv_ref, keys):
    lane = lax.broadcasted_iota(jnp.int32, (BLOCK, BLOCK), 1)

    def place(k, carry):
        start = pl.multiple_of(order_ref[0, k] * BLOCK, BLOCK)
        position = start + lax.broadcasted_iota(jnp.int32, (BLOCK, BLOCK), 0)
        mark = (file_of(plan, position) == lane) | ((position >= plan[0]) & (lane == 4))
        mark = mark | ((lane >= 5) & (lane < 8))
        keys[pl.ds(start, BLOCK), :BLOCK] = kv_ref[pl.ds(pl.multiple_of(k * BLOCK, BLOCK), BLOCK)]
        keys[pl.ds(start, BLOCK), BLOCK:] = jnp.where(mark, 1.0, 0.0).astype(bf16)
        return carry

    lax.fori_loop(0, BLOCKS, place, 0)


def own_keys(keys, place):
    rows = keys[pl.ds(pl.multiple_of(place * BLOCK, BLOCK), BLOCK)]
    lane = lax.broadcasted_iota(jnp.int32, rows.shape, 1)
    return jnp.where((lane >= BLOCK) & (lane < BLOCK + 5), jnp.zeros_like(rows), rows)


def query_marks(plan, place):
    lane = lax.broadcasted_iota(jnp.int32, (8, 2 * BLOCK), 1)
    number = file_of(plan, place * BLOCK + (lane & (BLOCK - 1)))
    mark = lax.broadcasted_iota(jnp.int32, (8, 2 * BLOCK), 0)
    return jnp.where(((mark < 4) & (mark != number)) | (mark == 4), NEG, 0.0)


def minus_terms(row):
    high = row.astype(bf16).astype(f32)
    middle = (row - high).astype(bf16).astype(f32)
    low = row - high - middle
    mark = lax.broadcasted_iota(jnp.int32, (8, row.shape[1]), 0)
    return jnp.where(
        mark == 5, -high, jnp.where(mark == 6, -middle, jnp.where(mark == 7, -low, 0.0))
    )


def fill(target, top, marks):
    target[:BLOCK] = top
    zeros = jnp.zeros((BLOCK - 8, 2 * BLOCK), f32)
    target[BLOCK:] = jnp.concatenate([marks, zeros], 0).astype(bf16)


def sweep(low, count, step):
    def four(t, carry):
        step(low + 4 * t, 4)
        return carry

    lax.fori_loop(0, count // 4, four, 0)

    @pl.when(lax.rem(count, 4) >= 2)
    def _():
        step(low + count // 4 * 4, 2)

    @pl.when(lax.rem(count, 2) == 1)
    def _():
        step(low + count - 1, 1)


def fold_heads(block):
    turned = block.T
    return jnp.concatenate([turned[:HD], turned[HD:]], 1)


def unfold_heads(wide):
    return jnp.concatenate([wide[:, :BLOCK], wide[:, BLOCK:]], 0).T


def eights(values):
    return values.reshape(values.shape[0] // 8, 8, values.shape[1])


def forward_kernel(
    length_ref,
    order_ref,
    files_ref,
    one_ref,
    vec_ref,
    kv_ref,
    mine_ref,
    other_ref,
    q_ref,
    att_ref,
    lse_ref,
    wq_ref,
    keys,
    qt,
    vt,
    scores,
    tops,
    sums,
    mixed,
    sem,
):
    copies = row_copies((mine_ref, other_ref), pl.ds(QUERY, D), wq_ref, sem)
    start(copies)
    plan = read_plan(length_ref, order_ref, files_ref)
    place_keys(plan, order_ref, kv_ref, keys)
    for k in range(BLOCKS):
        vt[:, k * BLOCK : (k + 1) * BLOCK] = (
            keys[k * BLOCK : (k + 1) * BLOCK, :BLOCK].T[HD:]
        )
    finish(copies)
    q = (mm(one_ref[...], wq_ref[...]) + vec_ref[2:3]).astype(bf16)
    q_ref[...] = q
    empty = jnp.zeros((HD, 2 * BLOCK), bf16)
    for b in range(2):
        place, low, count = block_plan(plan, order_ref, b)
        marks = query_marks(plan, place)
        for p in range(PAIRS):
            block = q[b * BLOCK : (b + 1) * BLOCK, p * BLOCK : (p + 1) * BLOCK] * 0.125
            fill(qt.at[p], jnp.concatenate([fold_heads(block), empty], 0), marks)
        own = own_keys(keys, place)
        bias = own_bias(plan, place)
        for p in range(PAIRS):
            value = mm(own, qt[p]) + bias
            scores[p, 0:BLOCK] = value
            tops[p] = jnp.max(eights(value), 0)

        def score_step(first, blocks):
            rows = keys[pl.ds(pl.multiple_of(first * BLOCK, BLOCK), blocks * BLOCK)]
            at = pl.ds(pl.multiple_of((first - low + 1) * BLOCK, BLOCK), blocks * BLOCK)
            for p in range(PAIRS):
                value = mm(rows, qt[p])
                scores[p, at] = value
                tops[p] = jnp.maximum(tops[p], jnp.max(eights(value), 0))

        sweep(low, count, score_step)
        peaks = [jnp.max(tops[p], 0, keepdims=True) for p in range(PAIRS)]
        for p in range(PAIRS):
            tops[p] = jnp.broadcast_to(peaks[p], (8, 2 * BLOCK))
            weight = jnp.exp(scores[p, 0:BLOCK] - peaks[p])
            sums[p] = jnp.sum(eights(weight), 0)
            span = pl.ds(pl.multiple_of(place * BLOCK, BLOCK), BLOCK)
            mixed[p] = mm(vt[:, span], weight.astype(bf16))

        def mix_step(first, blocks):
            span = pl.ds(pl.multiple_of(first * BLOCK, BLOCK), blocks * BLOCK)
            at = pl.ds(pl.multiple_of((first - low + 1) * BLOCK, BLOCK), blocks * BLOCK)
            values = vt[:, span]
            for p in range(PAIRS):
                weight = jnp.exp(scores[p, at] - tops[p, 0:1])
                sums[p] += jnp.sum(eights(weight), 0)
                mixed[p] += mm(values, weight.astype(bf16))

        sweep(low, count, mix_step)
        for p in range(PAIRS):
            total = jnp.sum(sums[p], 0, keepdims=True)
            lse_ref[b, p] = tops[p] + jnp.log(total)
            att_ref[b * BLOCK : (b + 1) * BLOCK, p * BLOCK : (p + 1) * BLOCK] = unfold_heads(
                (mixed[p] / total).astype(bf16)
            )


def backward_kernel(
    length_ref,
    order_ref,
    files_ref,
    q_ref,
    do_ref,
    att_ref,
    lse_ref,
    one_ref,
    kv_ref,
    gq_ref,
    keep_ref,
    send_ref,
    grad_ref,
    keys,
    qt,
    dot_,
    qd,
    both,
    kt,
    dq,
    dkv,
    gwq,
):
    plan = read_plan(length_ref, order_ref, files_ref)
    place_keys(plan, order_ref, kv_ref, keys)
    for k in range(BLOCKS):
        kt[:, k * BLOCK : (k + 1) * BLOCK] = (
            keys[k * BLOCK : (k + 1) * BLOCK, :BLOCK].T[:HD]
        )
    dkv[...] = jnp.zeros_like(dkv)
    zeros = jnp.zeros((BLOCK, HD), bf16)
    empty = jnp.zeros((HD, 2 * BLOCK), bf16)
    for b in range(2):
        place, low, count = block_plan(plan, order_ref, b)
        marks = query_marks(plan, place)
        for p in range(PAIRS):
            span = (slice(b * BLOCK, (b + 1) * BLOCK), slice(p * BLOCK, (p + 1) * BLOCK))
            block = q_ref[span] * 0.125
            grad = do_ref[span]
            wide = fold_heads(grad)
            out = fold_heads(att_ref[span]).astype(f32)
            delta = jnp.sum(wide.astype(f32) * out, 0, keepdims=True)
            top = jnp.concatenate([fold_heads(block), empty], 0)
            fill(qt.at[p], top, marks + minus_terms(lse_ref[b, p, 0:1]))
            fill(dot_.at[p], jnp.concatenate([empty, wide], 0), minus_terms(delta))
            factors = [
                jnp.concatenate([block[:, :HD], zeros], 1),
                jnp.concatenate([block[:, HD:], zeros], 1),
                jnp.concatenate([zeros, grad[:, :HD]], 1),
                jnp.concatenate([zeros, grad[:, HD:]], 1),
            ]
            qd[512 * p : 512 * (p + 1)] = jnp.concatenate(factors, 0)
        dq[...] = jnp.zeros_like(dq)

        def step(first, blocks, rows=None, bias=None):
            span = pl.ds(pl.multiple_of(first * BLOCK, BLOCK), blocks * BLOCK)
            rows = keys[span] if rows is None else rows
            turned = kt[:, span]
            size = blocks * BLOCK
            for p in range(PAIRS):
                value = mm(rows, qt[p])
                probs = jnp.exp(value if bias is None else value + bias)
                grad = (probs * mm(rows, dot_[p])).astype(bf16)
                dq[p] += mm(turned, grad)
                both[:size, 512 * p : 512 * p + 256] = grad
                both[:size, 512 * p + 256 : 512 * p + 512] = probs.astype(bf16)
            dkv[span] += mm(both[:size], qd[...])

        step(place, 1, own_keys(keys, place), own_bias(plan, place))
        sweep(low, count, step)
        for p in range(PAIRS):
            gq_ref[b * BLOCK : (b + 1) * BLOCK, p * BLOCK : (p + 1) * BLOCK] = unfold_heads(
                (dq[p] * 0.125).astype(bf16)
            )

    def give(k, carry):
        initial = order_ref[0, k]
        grad_ref[k] = dkv[pl.ds(pl.multiple_of(initial * BLOCK, BLOCK), BLOCK)].astype(bf16)
        return carry

    lax.fori_loop(0, BLOCKS, give, 0)
    gwq[...] = mm(one_ref[...].T, gq_ref[...]).astype(bf16)
    deal_rows(gwq, keep_ref, send_ref)


def deal_rows(source, keep_ref, send_ref):
    for k in range(8):
        keep_ref[k] = source[row_span(k, 0), :]
        send_ref[k] = source[row_span(k, 1), :]


def columns(c, first=0):
    return pl.ds(pl.multiple_of(first + c * SLICE, BLOCK), SLICE)


def middle_kernel(
    feed_ref,
    mine_ref,
    other_ref,
    x_ref,
    ct_ref,
    att_ref,
    vec_ref,
    fcb_ref,
    out_ref,
    gmid_ref,
    gatt_ref,
    sums_ref,
    keep_ref,
    send_ref,
    grad_ref,
    wf,
    wg,
    gf,
    gg,
    in_sem,
    out_sem,
    last_sem,
    wout,
    gout,
    x2,
    x2t,
    ctt,
    branch,
    gin,
    mid,
    fcsum,
):
    def loads(c, slot):
        return (
            pltpu.make_async_copy(feed_ref.at[:, columns(c)], wf.at[slot], in_sem.at[slot, 0]),
            pltpu.make_async_copy(feed_ref.at[:, columns(c, FF)], wg.at[slot], in_sem.at[slot, 1]),
        )

    def store(c, slot):
        for k in range(16):
            pltpu.make_async_copy(
                gf.at[slot, pl.ds(k * ROWS, ROWS)],
                grad_ref.at[k // 4, k % 2, k // 2 % 2, :, columns(c)],
                out_sem.at[slot, 0],
            ).start()
            pltpu.make_async_copy(
                gg.at[slot, pl.ds(k * ROWS, ROWS), pl.ds(SENT, REST)],
                grad_ref.at[
                    k // 4,
                    k % 2,
                    k // 2 % 2,
                    :,
                    pl.ds(pl.multiple_of(FF + D + c * REST, BLOCK), REST),
                ],
                out_sem.at[slot, 1],
            ).start()
        for k in range(8):
            for other, ref in enumerate((keep_ref, send_ref)):
                pltpu.make_async_copy(
                    gg.at[slot, row_span(k, other), pl.ds(0, SENT)],
                    ref.at[c, k],
                    out_sem.at[slot, 1],
                ).start()

    def stored(slot):
        pltpu.make_async_copy(gf.at[slot], gf.at[slot], out_sem.at[slot, 0]).wait()
        pltpu.make_async_copy(gg.at[slot], gg.at[slot], out_sem.at[slot, 1]).wait()

    copies = row_copies((mine_ref, other_ref), pl.ds(OUT, D), wout, last_sem)
    start(copies)
    start(loads(0, 0))
    ctt[...] = ct_ref[...].T
    branch[...] = jnp.zeros_like(branch)
    gin[...] = jnp.zeros_like(gin)
    vec = vec_ref[...]
    finish(copies)
    middle = x_ref[...].astype(f32) + (mm_nt(att_ref[...], wout[...]) + vec[3:4])
    mid[...] = middle
    normed, factor = normalize(middle)
    two = (normed * vec[4:5] + vec[5:6]).astype(bf16)
    x2[...] = two
    x2t[...] = two.T

    def chunk(c, carry):
        slot = lax.rem(c, 2)

        @pl.when(c < 3)
        def _():
            start(loads(c + 1, 1 - slot))

        finish(loads(c, slot))
        span = columns(c)
        pre = mm(x2[...], wf[slot]) + fcb_ref[:, span]
        grad_hidden = mm(ct_ref[...], wg[slot])
        square = pre * pre
        tanh = jnp.tanh(0.7978845608028654 * (pre + 0.044715 * (pre * square)))
        half = 0.5 * (1.0 + tanh)
        hidden = (pre * half).astype(bf16)
        slope = half + (0.5 * pre) * (1.0 - tanh * tanh) * (
            0.7978845608028654 + (3 * 0.044715 * 0.7978845608028654) * square
        )
        grad_pre = (grad_hidden * slope).astype(bf16)
        branch[...] += mm_nt(hidden, wg[slot])
        gin[...] += mm_nt(grad_pre, wf[slot])
        fcsum[:, span] = jnp.sum(grad_pre.astype(f32), 0, keepdims=True)

        @pl.when(c >= 2)
        def _():
            stored(slot)

        gf[slot] = mm(x2t[...], grad_pre).astype(bf16)
        gg[slot] = mm(ctt[...], hidden).astype(bf16)
        store(c, slot)
        return carry

    lax.fori_loop(0, 4, chunk, 0)
    middle = mid[...]
    cot = ct_ref[...].astype(f32)
    out_ref[...] = (middle + (branch[...] + vec[6:7])).astype(bf16)
    normed, factor = normalize(middle)
    grad_two = gin[...]
    grad_middle = cot + norm_back(grad_two * vec[4:5], normed, factor)
    gmid_ref[...] = grad_middle
    grad_branch = grad_middle.astype(bf16)
    gout[...] = mm(grad_branch.T, att_ref[...]).astype(bf16)
    outs = [
        pltpu.make_async_copy(
            gout.at[pl.ds(k * ROWS, ROWS)],
            grad_ref.at[k // 4, k % 2, k // 2 % 2, :, pl.ds(FF, D)],
            last_sem,
        )
        for k in range(16)
    ]
    start(outs)
    gatt_ref[...] = mm(grad_branch, wout[...]).astype(bf16)
    sums_ref[0:4] = jnp.concatenate(
        [
            jnp.sum(grad_branch.astype(f32), 0, keepdims=True),
            jnp.sum(grad_two * normed, 0, keepdims=True),
            jnp.sum(grad_two, 0, keepdims=True),
            jnp.sum(cot, 0, keepdims=True),
        ],
        0,
    )
    gather = four_apart(512, BLOCK, 1)
    mine = lax.broadcasted_iota(jnp.int32, (4, 512), 0) == (
        lax.broadcasted_iota(jnp.int32, (4, 512), 1) % 4
    )
    for g in range(6):
        high, low = split_low(jnp.where(mine, fcsum[:, g * 512 : (g + 1) * 512], 0.0))
        sums_ref[4:8, g * BLOCK : (g + 1) * BLOCK] = mm(high, gather) + mm(low, gather)
    stored(0)
    stored(1)
    finish(outs)


def last_kernel(
    x_ref,
    one_ref,
    gq_ref,
    gmid_ref,
    wq_ref,
    early_ref,
    vec_ref,
    sums_ref,
    dkv_ref,
    gx_ref,
    keep_ref,
    send_ref,
    pack_ref,
):
    gkv = jnp.sum(dkv_ref[...].astype(f32), 0).astype(bf16)
    gq = gq_ref[...]
    vec = vec_ref[...]
    grad_one = mm_nt(gq, wq_ref[...]) + mm_nt(gkv, early_ref[:, :BLOCK])
    normed, factor = normalize(x_ref[...].astype(f32))
    gx_ref[...] = (gmid_ref[...] + norm_back(grad_one * vec[0:1], normed, factor)).astype(bf16)
    pack_ref[:, :BLOCK] = mm(one_ref[...].astype(f32).T.astype(bf16), gkv).astype(bf16)
    sums = sums_ref[...]
    rows = jnp.concatenate(
        [
            jnp.sum(grad_one * normed, 0, keepdims=True),
            jnp.sum(grad_one, 0, keepdims=True),
            jnp.sum(gq.astype(f32), 0, keepdims=True),
            sums,
            jnp.zeros((5, D), f32),
        ],
        0,
    )
    high, low = split_low(rows)
    value = jnp.sum(gkv.astype(f32), 0, keepdims=True)[:, HD:]
    value_high, value_low = split_low(value)
    lane = lax.broadcasted_iota(jnp.int32, (16, HD), 1)
    mine = (lane & 15) == lax.broadcasted_iota(jnp.int32, (16, HD), 0)
    group = lax.broadcasted_iota(jnp.int32, (HD, D), 0) // 16
    spread = jnp.where(group == lax.broadcasted_iota(jnp.int32, (HD, D), 1) % 6, 1.0, 0.0).astype(bf16)
    put_high = mm(jnp.where(mine, value_high.astype(f32), 0.0).astype(bf16), spread)
    put_low = mm(jnp.where(mine, value_low.astype(f32), 0.0).astype(bf16), spread)
    packed = jnp.concatenate(
        [high.astype(f32), low.astype(f32), put_high, put_low, jnp.zeros((64, D), f32)], 0
    )
    pack_ref[:, BLOCK:] = packed.T.astype(bf16)
    deal_rows(pack_ref, keep_ref, send_ref)


SMEM = pl.BlockSpec(memory_space=pltpu.SMEM)
VMEM = pl.BlockSpec(memory_space=pltpu.VMEM)
ANY = pl.BlockSpec(memory_space=pl.ANY)


def shape(*dims, dtype=bf16):
    return jax.ShapeDtypeStruct(dims, dtype)


def add_all(parts, dtype=bf16):
    total = parts[0].astype(f32)
    for part in parts[1:]:
        total = total + part.astype(f32)
    return total.astype(dtype)


def call(kernel, name, outs, args, scratch=(), smem=0, hbm=(), hbm_out=0, flops=0, moved=0, exps=0):
    places = [SMEM if i < smem else ANY if i in hbm else VMEM for i in range(len(args))]
    return pl.pallas_call(
        kernel,
        out_shape=outs,
        in_specs=places,
        out_specs=[VMEM] * (len(outs) - hbm_out) + [ANY] * hbm_out,
        scratch_shapes=list(scratch),
        compiler_params=pltpu.CompilerParams(vmem_limit_bytes=56 * 1024 * 1024),
        cost_estimate=pl.CostEstimate(flops=flops, bytes_accessed=moved, transcendentals=exps),
        name=name,
    )(*args)


def tie(value, after):
    return lax.optimization_barrier((value, after))[0]


def local(
    layer_input,
    cotangent,
    lengths,
    order,
    files,
    ln1_gain,
    ln1_bias,
    w_attn,
    query_bias,
    value_bias,
    w_out,
    out_bias,
    ln2_gain,
    ln2_bias,
    w_fc,
    fc_bias,
    w_proj,
    proj_bias,
):
    x = layer_input[0]
    cot = cotangent[0]
    vectors = [ln1_gain, ln1_bias, query_bias, out_bias, ln2_gain, ln2_bias, proj_bias, fc_bias]
    (pieces,) = call(
        piece_kernel,
        "pieces",
        [shape(8, 6, WIDE)],
        [*vectors, w_attn, w_out, w_fc, w_proj],
        smem=8,
        moved=2_000_000,
    )
    attn_block, feed_block = call(
        block_kernel,
        "blocks",
        [shape(8, ROWS, FC), shape(ROWS, 2 * FF)],
        [lax.all_to_all(pieces, CTX, 0, 0)],
        [pltpu.VMEM((ROWS, WIDE), f32)],
        moved=4_000_000,
    )
    feed = lax.all_gather(feed_block, DP, axis=0, tiled=True)
    attn = lax.all_to_all(attn_block, ("x", "zl"), 0, 0)
    parts = [attn, send(attn, dc=1)]
    one, kv, vec, fcb, early = call(
        first_kernel,
        "first",
        [
            shape(TOK, D),
            shape(8, TOK, BLOCK),
            shape(16, D, dtype=f32),
            shape(1, FF, dtype=f32),
            shape(D, 2 * BLOCK),
        ],
        [x, value_bias[None], *parts],
        [pltpu.SemaphoreType.DMA],
        hbm=(2, 3),
        flops=100_000_000,
        moved=4_000_000,
    )
    kv = lax.all_to_all(kv, CTX, 0, 0).reshape(LENGTH, BLOCK)

    wide = (PAIRS, 2 * BLOCK, 2 * BLOCK)
    plan = [lengths, order, files]
    q, att, lse, wq = call(
        forward_kernel,
        "attend",
        [
            shape(TOK, D),
            shape(TOK, D),
            shape(2, PAIRS, 8, 2 * BLOCK, dtype=f32),
            shape(D, D),
        ],
        [*plan, one, vec, kv, *parts],
        [
            pltpu.VMEM((LENGTH, 2 * BLOCK), bf16),
            pltpu.VMEM(wide, bf16),
            pltpu.VMEM((HD, LENGTH), bf16),
            pltpu.VMEM((PAIRS, LENGTH, 2 * BLOCK), f32),
            pltpu.VMEM((PAIRS, 8, 2 * BLOCK), f32),
            pltpu.VMEM((PAIRS, 8, 2 * BLOCK), f32),
            pltpu.VMEM((PAIRS, HD, 2 * BLOCK), f32),
            pltpu.SemaphoreType.DMA,
        ],
        smem=2,
        hbm=(6, 7),
        flops=10_000_000_000,
        moved=4_000_000,
        exps=6_000_000,
    )
    half = shape(8, ROWS, D)
    sliced = shape(4, 8, ROWS, SENT)
    output, grad_middle, grad_att, sums, keep_proj, send_proj, grad_fc = call(
        middle_kernel,
        "feed",
        [
            shape(TOK, D),
            shape(TOK, D, dtype=f32),
            shape(TOK, D),
            shape(8, D, dtype=f32),
            sliced,
            sliced,
            shape(4, 2, 2, ROWS, REDUCED),
        ],
        [feed, *parts, x, cot, att, vec, fcb],
        [
            pltpu.VMEM((2, D, SLICE), bf16),
            pltpu.VMEM((2, D, SLICE), bf16),
            pltpu.VMEM((2, D, SLICE), bf16),
            pltpu.VMEM((2, D, SLICE), bf16),
            pltpu.SemaphoreType.DMA((2, 2)),
            pltpu.SemaphoreType.DMA((2, 2)),
            pltpu.SemaphoreType.DMA,
            pltpu.VMEM((D, D), bf16),
            pltpu.VMEM((D, D), bf16),
            pltpu.VMEM((TOK, D), bf16),
            pltpu.VMEM((D, TOK), bf16),
            pltpu.VMEM((D, TOK), bf16),
            pltpu.VMEM((TOK, D), f32),
            pltpu.VMEM((TOK, D), f32),
            pltpu.VMEM((TOK, D), f32),
            pltpu.VMEM((1, FF), f32),
        ],
        hbm=(0, 1, 2),
        hbm_out=3,
        flops=8_000_000_000,
        moved=30_000_000,
        exps=1_000_000,
    )
    grad_fc = grad_fc.reshape(8, 2, ROWS, REDUCED)
    grad_fc = lax.psum_scatter(grad_fc, ("x", "core"), scatter_dimension=0, tiled=True)[0]
    grad_proj = add_all([keep_proj, send(send_proj, dc=1)])
    grad_att = tie(grad_att, grad_proj)
    grad_proj = add_all(list(lax.all_to_all(grad_proj, "y", 0, 0)))

    gq, keep_q, send_q, grad_kv = call(
        backward_kernel,
        "attend_back",
        [shape(TOK, D), half, half, shape(BLOCKS, BLOCK, BLOCK)],
        [*plan, q, grad_att, att, lse, one, kv],
        [
            pltpu.VMEM((LENGTH, 2 * BLOCK), bf16),
            pltpu.VMEM(wide, bf16),
            pltpu.VMEM(wide, bf16),
            pltpu.VMEM((PAIRS * 4 * BLOCK, BLOCK), bf16),
            pltpu.VMEM((4 * BLOCK, PAIRS * 4 * BLOCK), bf16),
            pltpu.VMEM((HD, LENGTH), bf16),
            pltpu.VMEM((PAIRS, HD, 2 * BLOCK), f32),
            pltpu.VMEM((LENGTH, BLOCK), f32),
            pltpu.VMEM((D, D), bf16),
        ],
        smem=2,
        flops=20_000_000_000,
        moved=6_000_000,
        exps=6_000_000,
    )
    grad_q = add_all([keep_q, send(send_q, dc=1)])
    grad_kv = tie(grad_kv.reshape(8, TOK, BLOCK), grad_proj)
    grad_kv = lax.all_to_all(grad_kv, CTX, 0, 0)

    grad_fc = tie(grad_fc, grad_kv)
    other_fc = lax.dynamic_index_in_dim(grad_fc, 1 - lax.axis_index("zl"), 0, False)
    other_fc = send(other_fc, dl=1)
    small = shape(8, ROWS, 2 * BLOCK)
    grad_x, keep_pack, send_pack = call(
        last_kernel,
        "last",
        [shape(TOK, D), small, small],
        [x, one, gq, grad_middle, wq, early, vec, sums, grad_kv],
        [pltpu.VMEM((D, 2 * BLOCK), bf16)],
        flops=1_000_000_000,
        moved=5_000_000,
    )
    grad_pack = add_all([keep_pack, send(send_pack, dc=1)])
    both = jnp.concatenate([tie(grad_pack, other_fc), grad_proj, grad_q], 2)
    both = lax.all_to_all(both, ("x", "zl"), 0, 0)
    (pieces,) = call(
        unblock_kernel,
        "unblock",
        [shape(8, 6, G_WIDE)],
        [both, grad_fc, other_fc],
        [pltpu.VMEM((ROWS, G_WIDE), f32)],
    )
    results = call(
        finish_kernel,
        "finish",
        [
            shape(6, D + BLOCK, dtype=f32),
            shape(6, D, dtype=f32),
            shape(6, FF, dtype=f32),
            shape(6, FF, dtype=f32),
        ]
        + [shape(1, 6, dtype=f32)] * 7
        + [shape(1, 24, dtype=f32), shape(1, HD, dtype=f32)],
        [lax.all_to_all(pieces, CTX, 0, 0)],
    )
    grad_w_attn, grad_w_out, grad_w_fc, grad_w_proj = results[:4]
    gain_one, bias_one, bias_query, bias_out, gain_two, bias_two, bias_proj, bias_fc = (
        value.reshape(-1) for value in results[4:12]
    )
    return (
        output[None],
        grad_x[None],
        gain_one,
        bias_one,
        grad_w_attn,
        bias_query,
        results[12].reshape(HD),
        grad_w_out,
        bias_out,
        gain_two,
        bias_two,
        grad_w_fc,
        bias_fc,
        grad_w_proj,
        bias_proj,
    )


def solution(mesh):
    cells = Mesh(mesh.devices.reshape(SIZES), AXES)
    every = P(AXES)
    tall = P(AXES, None)
    tokens = P(DP, CTX, None)
    in_specs = (
        tokens,
        tokens,
        P(DP),
        P(DP, None),
        P(DP, None),
        every,
        every,
        tall,
        every,
        P(),
        tall,
        every,
        every,
        every,
        tall,
        every,
        tall,
        every,
    )
    out_specs = (
        tokens,
        tokens,
        every,
        every,
        tall,
        every,
        P(),
        tall,
        every,
        every,
        every,
        tall,
        every,
        tall,
        every,
    )
    return jax.shard_map(local, mesh=cells, in_specs=in_specs, out_specs=out_specs, check_vma=False)
```

time: 262 us -> 244 us (0.931); the launches traced: 267 us -> 243 us
  blocking collectives: 132 us -> 100 us
  waiting for transfers between devices: 31.5 us -> 48.7 us
  Pallas kernels: 73.6 us -> 58.7 us
  starting transfers between devices: 8.07 us -> 12.9 us
    all_to_all x2 -> x1, blocking collectives: 54.2 us -> 22.1 us  [local(): both = lax.all_to_all(both, ('x', 'zl'), 0, 0)]
    pallas_call x10 -> x9, Pallas kernels: 73.6 us -> 58.7 us  [call(): pl.pallas_call(kernel, out_shape=outs, in_specs=places, out_specs=[VMEM]...]
    all_to_all x0 -> x1, waiting for transfers between devices: none -> 10.4 us  [local(): grad_kv = lax.all_to_all(grad_kv, CTX, 0, 0)]
    ppermute x4 -> x5, waiting for transfers between devices: 9.4 us -> 18.6 us  [send(): return lax.ppermute(value, AXES, route(**shift))]
    all_to_all x0 -> x1, starting transfers between devices: none -> 4.4 us  [local(): grad_kv = lax.all_to_all(grad_kv, CTX, 0, 0)]
    all_to_all x1, waiting for transfers between devices: 9.28 us -> 5.76 us  [local(): grad_proj = add_all(list(lax.all_to_all(grad_proj, 'y', 0, 0)))]
  transfers between devices with their start and end apart: 8 -> 10, of which waited for: 6 -> 7; matrix products, arithmetic and copies ran while one was open for 2% -> 1% of each run, Pallas kernels for 16% -> 13%
where the time goes in v3:
time: 244 us; the launch traced here: 243 us
  blocking collectives  100 us (41%)
  Pallas kernels  58.7 us (24%)
  waiting for transfers between devices  48.7 us (20%)
  between operations  14.9 us (6%)
  starting transfers between devices  12.9 us (5%)
  local copies, waits for them, and re-layouts  5.27 us (2%)
    pallas_call x9, Pallas kernels, call(): pl.pallas_call(kernel, out_shape=outs, in_specs=places, out_specs=[VMEM]...  58.7 us
    all_to_all x2, blocking collectives, local(): lax.all_to_all(pieces, CTX, 0, 0)  42 us
    all_to_all x1, blocking collectives, local(): attn = lax.all_to_all(attn_block, ('x', 'zl'), 0, 0)  35.9 us
    all_to_all x1, blocking collectives, local(): both = lax.all_to_all(both, ('x', 'zl'), 0, 0)  22.1 us
    ppermute x5, waiting for transfers between devices, send(): return lax.ppermute(value, AXES, route(**shift))  18.6 us
    all_to_all x1, waiting for transfers between devices, local(): kv = lax.all_to_all(kv, CTX, 0, 0).reshape(LENGTH, BLOCK)  11.2 us
    all_to_all x1, waiting for transfers between devices, local(): grad_kv = lax.all_to_all(grad_kv, CTX, 0, 0)  10.4 us
    all_to_all x1, waiting for transfers between devices, local(): grad_proj = add_all(list(lax.all_to_all(grad_proj, 'y', 0, 0)))  5.76 us
  transfers between devices with their start and end apart: 10, of which 7 were waited for; matrix products, arithmetic and copies ran while one was open for 1% of the time, Pallas kernels for 13%

profile of v3, /device:TPU:0, one launch (start us, length us, event | category | flops | bytes accessed | tf_op | source)
XLA Modules:
  0.0 242.8 jit_solution(2794651549056348693)
XLA Ops:
  7.2 1.9 pieces.1
  9.2 24.5 %all_to_all.35.piece_ref = bf16[8,6,7936]{2,1,0:T(8,128)(2,1)} all-to-all(bf16[8,6,7936]{2,1,0:T(8,128)(2,1)} %pieces.1), channel_id=1, replica_groups=mesh['x'=4,'zl'=2,'core'=2,'y'=4,'zh'=2] {'y','zh'}, dimensions={0} | all-to-all | bytes 1523712 | tf_op jit(solution)/shard_map/all_to_all | solution.py:780
  33.7 2.8 %blocks.1 = (bf16[8,48,1792]{2,1,0:T(8,128)(2,1)}, bf16[48,6144]{1,0:T(8,128)(2,1)}) custom-call(bf16[8,6,7936]{2,1,0:T(8,128)(2,1)} %all_to_all.35.piece_ref), custom_call_target="tpu_custom_call" | custom-call | bytes 4000000 | tf_op jit(solution)/shard_map/blocks/pallas_call | solution.py:729
  36.5 35.9 %all_to_all.36.mine_ref = bf16[8,48,1792]{2,1,0:T(8,128)(2,1)S(1)} all-to-all(bf16[8,48,1792]{2,1,0:T(8,128)(2,1)} %get-tuple-element.58), channel_id=1, replica_groups=mesh['x'=4,'zl'=2,'core'=2,'y'=4,'zh'=2] {'x','zl'}, dimensions={0} | all-to-all | bytes 2752512 | tf_op jit(solution)/shard_map/all_to_all | solution.py:785
  72.4 3.5 %collective-permute-done.other_ref = bf16[8,48,1792]{2,1,0:T(8,128)(2,1)S(1)} collective-permute-done((bf16[8,48,1792]{2,1,0:T(8,128)(2,1)S(1)}, bf16[8,48,1792]{2,1,0:T(8,128)(2,1)S(1)}, u32[]{:S(2)}, u32[]{:S(2)}) %collective-permute-start) | collective-permute-done | bytes 1376288 | tf_op jit(solution)/shard_map/ppermute | solution.py:45
  77.1 3.3 %first.1 = (bf16[256,768]{1,0:T(8,128)(2,1)}, bf16[8,256,128]{2,1,0:T(8,128)(2,1)}, f32[16,768]{1,0:T(8,128)}, f32[1,3072]{1,0:T(1,128)}, bf16[768,256]{1,0:T(8,128)(2,1)}) custom-call(bf16[256,768]{1,0:T(8,128)(2,1)} %bitcast.25, f32[1,64]{1,0:T(1,128)} %bitcast.30, bf16[8,48,1792]{2,1,0:T(8,128)(2,1)} %copy-done, bf16[8,48,1792]{2,1,0:T(8,128)(2,1)} %copy-done.3), custom_call_target="tpu_custom_call" | custom-call | flops 100000000 | bytes 4000000 | tf_op jit(solution)/shard_map/first/pallas_call | solution.py:729
  80.4 3.5 %all-to-all-start.2 = ((bf16[8,256,128]{2,1,0:T(8,128)(2,1)}), bf16[8,256,128]{2,1,0:T(8,128)(2,1)S(1)}, u32[]{:S(2)}, u32[]{:S(2)}) async-start(bf16[8,256,128]{2,1,0:T(8,128)(2,1)} %get-tuple-element.61), calls=%async_computation.2 | async-start | bytes 1048576 | tf_op jit(solution)/shard_map/all_to_all | solution.py:803
  84.6 11.2 %all-to-all-done.2 = bf16[8,256,128]{2,1,0:T(8,128)(2,1)S(1)} async-done(((bf16[8,256,128]{2,1,0:T(8,128)(2,1)}), bf16[8,256,128]{2,1,0:T(8,128)(2,1)S(1)}, u32[]{:S(2)}, u32[]{:S(2)}) %all-to-all-start.2) | async-done | bytes 524320 | tf_op jit(solution)/shard_map/all_to_all | solution.py:803
  96.6 9.0 %attend.1 = (bf16[256,768]{1,0:T(8,128)(2,1)}, bf16[256,768]{1,0:T(8,128)(2,1)}, f32[2,6,8,256]{3,2,1,0:T(8,128)}, bf16[768,768]{1,0:T(8,128)(2,1)}) custom-call(s32[1]{0:T(128)S(6)} %copy.33.length_ref, s32[1,16]{1,0:T(1,128)} %order_ref.3, s32[1,2048]{1,0:T(1,128)} %files_ref.3, bf16[256,768]{1,0:T(8,128)(2,1)} %get-tuple-element.59.one_ref, ...), custom_call_target="tpu_custom_call" | custom-call | flops 10000000000 | bytes 4000000 | tf_op jit(solution)/shard_map/attend/pallas_call | solution.py:729
  105.6 2.8 %all-gather.2.cloned.1.call-done.feed_ref = bf16[768,6144]{1,0:T(8,128)(2,1)} async-done(((bf16[48,6144]{1,0:T(8,128)(2,1)}), bf16[768,6144]{1,0:T(8,128)(2,1)}) %all-gather.2.cloned.1.call-update) | async-done | bytes 9437200 | tf_op jit(solution)/shard_map/all_gather | solution.py:784
  108.4 16.9 %feed.1 = (bf16[256,768]{1,0:T(8,128)(2,1)}, f32[256,768]{1,0:T(8,128)}, bf16[256,768]{1,0:T(8,128)(2,1)}, f32[8,768]{1,0:T(8,128)}, bf16[4,8,48,512]{3,2,1,0:T(...) custom-call(bf16[768,6144]{1,0:T(8,128)(2,1)} %all-gather.2.cloned.1.call-done.feed_ref, ...), custom_call_target="tpu_custom_call" | custom-call | flops 8000000000 | bytes 30000000 | tf_op jit(solution)/shard_map/feed/pallas_call | solution.py:729
  126.9 3.2 %collective-permute-done.1 = bf16[4,8,48,512]{3,2,1,0:T(8,128)(2,1)S(1)} collective-permute-done((bf16[4,8,48,512]{3,2,1,0:T(8,128)(2,1)S(1)}, bf16[4,8,48,512]{3,2,1,0:T(8,128)(2,1)S(1)}, u32[]{:S(2)}, u32[]{:S(2)}) %collective-permute-start.1) | collective-permute-done | bytes 1572896 | tf_op jit(solution)/shard_map/ppermute | solution.py:45
  130.0 1.8 add_convert_fusion
  131.8 3.6 %all-to-all-start.3 = ((bf16[4,8,48,512]{3,2,1,0:T(8,128)(2,1)}), bf16[4,8,48,512]{3,2,1,0:T(8,128)(2,1)S(1)}, u32[]{:S(2)}, u32[]{:S(2)}) async-start(bf16[4,8,48,512]{3,2,1,0:T(8,128)(2,1)} %add_convert_fusion), calls=%async_computation.3 | async-start | bytes 3145728 | tf_op jit(solution)/shard_map/all_to_all | solution.py:876
  135.4 15.6 %attend_back.1 = (bf16[256,768]{1,0:T(8,128)(2,1)}, bf16[8,48,768]{2,1,0:T(8,128)(2,1)}, bf16[8,48,768]{2,1,0:T(8,128)(2,1)}, bf16[16,128,128]{2,1,0:T(8,128)(2,1)}) custom-call(s32[1]{0:T(128)S(6)} %copy.33.length_ref, s32[1,16]{1,0:T(1,128)} %order_ref.3, s32[1,2048]{1,0:T(1,128)} %files_ref.3, bf16[256,768]{1,0:T(8,128)(2,1)} %get-tuple-element.65.q_ref, ...), custom_call_target="tpu_custom_call" | custom-call | flops 20000000000 | bytes 6000000 | tf_op jit(solution)/shard_map/attend_back/pallas_call | solution.py:729
  151.0 5.8 %all-to-all-done.3 = bf16[4,8,48,512]{3,2,1,0:T(8,128)(2,1)S(1)} async-done(((bf16[4,8,48,512]{3,2,1,0:T(8,128)(2,1)}), bf16[4,8,48,512]{3,2,1,0:T(8,128)(2,1)S(1)}, u32[]{:S(2)}, u32[]{:S(2)}) %all-to-all-start.3) | async-done | bytes 1572896 | tf_op jit(solution)/shard_map/all_to_all | solution.py:876
  157.0 4.4 %all-to-all-start.4 = ((bf16[8,256,128]{2,1,0:T(8,128)(2,1)}), bf16[8,256,128]{2,1,0:T(8,128)(2,1)S(1)}, u32[]{:S(2)}, u32[]{:S(2)}) async-start(bf16[8,256,128]{2,1,0:T(8,128)(2,1)} %bitcast.5), calls=%async_computation.4 | async-start | bytes 1048576 | tf_op jit(solution)/shard_map/all_to_all | solution.py:901
  161.5 10.4 %all-to-all-done.4.dkv_ref = bf16[8,256,128]{2,1,0:T(8,128)(2,1)S(1)} async-done(((bf16[8,256,128]{2,1,0:T(8,128)(2,1)}), bf16[8,256,128]{2,1,0:T(8,128)(2,1)S(1)}, u32[]{:S(2)}, u32[]{:S(2)}) %all-to-all-start.4) | async-done | bytes 524320 | tf_op jit(solution)/shard_map/all_to_all | solution.py:901
  172.7 4.1 %last.1 = (bf16[256,768]{1,0:T(8,128)(2,1)}, bf16[8,48,256]{2,1,0:T(8,128)(2,1)}, bf16[8,48,256]{2,1,0:T(8,128)(2,1)}) custom-call(bf16[256,768]{1,0:T(8,128)(2,1)} %bitcast.27, bf16[256,768]{1,0:T(8,128)(2,1)} %get-tuple-element.59.one_ref, bf16[256,768]{1,0:T(8,128)(2,1)} %get-tuple-element.71.gq_ref, f32[256,768]{1,0:T(8,128)} %get-tuple-element.72.gmid_ref, ...), custom_call_target="tpu_custom_call" | custom-call | flops 1000000000 | bytes 5000000 | tf_op jit(solution)/shard_map/last/pallas_call | solution.py:729
  179.2 11.9 %collective-permute-done.3.other_ref = bf16[48,4864]{1,0:T(8,128)(2,1)S(1)} collective-permute-done((bf16[48,4864]{1,0:T(8,128)(2,1)S(1)}, bf16[48,4864]{1,0:T(8,128)(2,1)S(1)}, u32[]{:S(2)}, u32[]{:S(2)}) %collective-permute-start.3) | collective-permute-done | bytes 466976 | tf_op jit(solution)/shard_map/ppermute | solution.py:45
  191.2 22.1 %all_to_all.37.attn_ref = bf16[8,48,1536]{2,1,0:T(8,128)(2,1)} all-to-all(bf16[8,48,1536]{2,1,0:T(8,128)(2,1)S(1)} %pad_maximum_fusion), channel_id=1, replica_groups=mesh['x'=4,'zl'=2,'core'=2,'y'=4,'zh'=2] {'x','zl'}, dimensions={0} | all-to-all | bytes 2359296 | tf_op jit(solution)/shard_map/all_to_all | solution.py:918
  213.3 3.1 %unblock.1 = bf16[8,6,6400]{2,1,0:T(8,128)(2,1)} custom-call(bf16[8,48,1536]{2,1,0:T(8,128)(2,1)} %all_to_all.37.attn_ref, bf16[2,48,4864]{2,1,0:T(8,128)(2,1)} %bitcast.24, bf16[48,4864]{1,0:T(8,128)(2,1)} %copy-done.6), custom_call_target="tpu_custom_call" | custom-call | tf_op jit(solution)/shard_map/unblock/pallas_call | solution.py:729
  216.4 17.5 %all_to_all.38.piece_ref = bf16[8,6,6400]{2,1,0:T(8,128)(2,1)} all-to-all(bf16[8,6,6400]{2,1,0:T(8,128)(2,1)} %unblock.1), channel_id=1, replica_groups=mesh['x'=4,'zl'=2,'core'=2,'y'=4,'zh'=2] {'y','zh'}, dimensions={0} | all-to-all | bytes 1228800 | tf_op jit(solution)/shard_map/all_to_all | solution.py:937
  233.9 2.1 finish.1
  (37 shorter events, 7.3 us)
Async XLA Ops:
  7.2 101.2 %all-gather.2.cloned.1.call-start = ((), (), s32[]{:S(2)}) async-start(), calls=%async_computation.8 | async-start | bytes 10027008 | tf_op jit(solution)/shard_map/all_gather | solution.py:784
  72.4 3.6 %copy-start = (bf16[8,48,1792]{2,1,0:T(8,128)(2,1)}, bf16[8,48,1792]{2,1,0:T(8,128)(2,1)S(1)}, u32[]{:S(2)}) copy-start(bf16[8,48,1792]{2,1,0:T(8,128)(2,1)S(1)} %all_to_all.36.mine_ref) | copy-start | bytes 4128772
  72.4 3.6 %collective-permute-start = (bf16[8,48,1792]{2,1,0:T(8,128)(2,1)S(1)}, bf16[8,48,1792]{2,1,0:T(8,128)(2,1)S(1)}, u32[]{:S(2)}, u32[]{:S(2)}) collective-permute-start(bf16[8,48,1792]{2,1,0:T(8,128)(2,1)S(1)} %all_to_all.36.mine_ref), channel_id=1, source_target_pairs={{0,8},{1,9},{2,10},{3,11},{4,12},{5,13},{6,14},{7,15},{8,0},{9,1},... | collective-permute-start | bytes 4128776 | tf_op jit(solution)/shard_map/ppermute | solution.py:45
  76.0 1.1 copy-start.3
  80.4 15.4 %all-to-all-start.2 = ((bf16[8,256,128]{2,1,0:T(8,128)(2,1)}), bf16[8,256,128]{2,1,0:T(8,128)(2,1)S(1)}, u32[]{:S(2)}, u32[]{:S(2)}) async-start(bf16[8,256,128]{2,1,0:T(8,128)(2,1)} %get-tuple-element.61), calls=%async_computation.2 | async-start | bytes 1048576 | tf_op jit(solution)/shard_map/all_to_all | solution.py:803
  83.9 92.9 %reduce-scatter.2.cloned.1.call-start = ((), (), s32[]{:S(2)}) async-start(), calls=%async_computation.9 | async-start | bytes 8404992 | tf_op jit(solution)/shard_map/reduce_scatter | solution.py:873
  95.8 0.8 copy-start.5
  125.2 1.4 copy-start.8
  125.2 4.8 %copy-start.2 = (bf16[4,8,48,512]{3,2,1,0:T(8,128)(2,1)S(1)}, bf16[4,8,48,512]{3,2,1,0:T(8,128)(2,1)}, u32[]{:S(2)}) copy-start(bf16[4,8,48,512]{3,2,1,0:T(8,128)(2,1)} %get-tuple-element.67) | copy-start | bytes 4718596
  126.6 3.4 %collective-permute-start.1 = (bf16[4,8,48,512]{3,2,1,0:T(8,128)(2,1)S(1)}, bf16[4,8,48,512]{3,2,1,0:T(8,128)(2,1)S(1)}, u32[]{:S(2)}, u32[]{:S(2)}) collective-permute-start(bf16[4,8,48,512]{3,2,1,0:T(8,128)(2,1)S(1)} %copy-done.8), channel_id=1, source_target_pairs={{0,8},{1,9},{2,10},{3,11},{4,12},{5,13},{6,14},{7,15},{8,0},{9,1},... | collective-permute-start | bytes 4718600 | tf_op jit(solution)/shard_map/ppermute | solution.py:45
  131.8 24.9 %all-to-all-start.3 = ((bf16[4,8,48,512]{3,2,1,0:T(8,128)(2,1)}), bf16[4,8,48,512]{3,2,1,0:T(8,128)(2,1)S(1)}, u32[]{:S(2)}, u32[]{:S(2)}) async-start(bf16[4,8,48,512]{3,2,1,0:T(8,128)(2,1)} %add_convert_fusion), calls=%async_computation.3 | async-start | bytes 3145728 | tf_op jit(solution)/shard_map/all_to_all | solution.py:876
  151.0 10.4 %copy-start.9 = (bf16[8,48,768]{2,1,0:T(8,128)(2,1)S(1)}, bf16[8,48,768]{2,1,0:T(8,128)(2,1)}, u32[]{:S(2)}) copy-start(bf16[8,48,768]{2,1,0:T(8,128)(2,1)} %get-tuple-element.85) | copy-start | bytes 1769476
  157.0 14.9 %all-to-all-start.4 = ((bf16[8,256,128]{2,1,0:T(8,128)(2,1)}), bf16[8,256,128]{2,1,0:T(8,128)(2,1)S(1)}, u32[]{:S(2)}, u32[]{:S(2)}) async-start(bf16[8,256,128]{2,1,0:T(8,128)(2,1)} %bitcast.5), calls=%async_computation.4 | async-start | bytes 1048576 | tf_op jit(solution)/shard_map/all_to_all | solution.py:901
  161.4 17.6 %collective-permute-start.4 = (bf16[8,48,768]{2,1,0:T(8,128)(2,1)S(1)}, bf16[8,48,768]{2,1,0:T(8,128)(2,1)S(1)}, u32[]{:S(2)}, u32[]{:S(2)}) collective-permute-start(bf16[8,48,768]{2,1,0:T(8,128)(2,1)S(1)} %copy-done.9), channel_id=1, source_target_pairs={{0,8},{1,9},{2,10},{3,11},{4,12},{5,13},{6,14},{7,15},{8,0},{9,1},... | collective-permute-start | bytes 1769480 | tf_op jit(solution)/shard_map/ppermute | solution.py:45
  171.9 0.8 copy-start.1
  172.7 6.3 %copy-start.4 = (bf16[8,48,768]{2,1,0:T(8,128)(2,1)S(1)}, bf16[8,48,768]{2,1,0:T(8,128)(2,1)}, u32[]{:S(2)}) copy-start(bf16[8,48,768]{2,1,0:T(8,128)(2,1)} %get-tuple-element.84) | copy-start | bytes 1769476
  176.8 2.3 copy-start.7
  176.8 2.3 collective-permute-start.2
  177.9 13.1 %collective-permute-start.3 = (bf16[48,4864]{1,0:T(8,128)(2,1)S(1)}, bf16[48,4864]{1,0:T(8,128)(2,1)S(1)}, u32[]{:S(2)}, u32[]{:S(2)}) collective-permute-start(bf16[48,4864]{1,0:T(8,128)(2,1)S(1)} %dynamic-slice_bitcast_fusion), channel_id=1, source_target_pairs={{0,16},{1,17},{2,18},{3,19},{4,20},{5,21},{6,22},{7,23},{8,24},{9,... | collective-permute-start | bytes 1400840 | tf_op jit(solution)/shard_map/ppermute | solution.py:45
  191.1 22.2 %copy-start.6 = (bf16[48,4864]{1,0:T(8,128)(2,1)}, bf16[48,4864]{1,0:T(8,128)(2,1)S(1)}, u32[]{:S(2)}) copy-start(bf16[48,4864]{1,0:T(8,128)(2,1)S(1)} %collective-permute-done.3.other_ref) | copy-start | bytes 1400836
Sparse Core Ops, SparseCore 0:
  36.6 71.7 all-gather.1
  125.4 46.1 reduce-scatter.1

commit v4 on v3

--- a/solution.py
+++ b/solution.py
@@ -97,65 +97,88 @@
 
 
 SLICE = 768
-KEYS, SMALL, QUERY, OUT, FC, PROJ, WIDE = 0, 128, 256, 1024, 1792, 4864, 7936
-SENT = 512
+KEYS, SMALL, QUERY, OUT, FC, PROJ, WIDE = 0, 128, 256, 1024, 1792, 4864, 8192
+FOLD = WIDE // 4
+SENT = 128
 REST = SLICE - SENT
-G_PROJ, G_QUERY, G_FC, G_OUT, G_REST, G_WIDE = 256, 768, 1536, 4608, 5376, 6400
+G_PROJ, G_QUERY, G_FC, G_OUT, G_REST, G_WIDE = 256, 384, 1152, 4224, 4992, 7552
+G_FOLD = (G_WIDE + 511) // 512 * BLOCK
 REDUCED = G_WIDE - G_FC
 
 
 def piece_kernel(*refs):
-    vectors, fcb_ref, attn_ref, out_ref, fc_ref, proj_ref, piece_ref = (refs[:7],) + refs[7:]
-    row = lax.broadcasted_iota(jnp.int32, (8, BLOCK), 0)
+    vectors, fcb_ref, attn_ref, out_ref, fc_ref, proj_ref, piece_ref, row = (
+        refs[:7],
+    ) + refs[7:]
+    line = lax.broadcasted_iota(jnp.int32, (8, BLOCK), 0)
     lane = lax.broadcasted_iota(jnp.int32, (8, BLOCK), 1)
     small = jnp.zeros((8, BLOCK), f32)
     for i in range(6):
         values = [ref[i] for ref in vectors] + [fcb_ref[4 * i + j] for j in range(4)]
         for j, value in enumerate(values):
-            small = jnp.where((row == i) & (lane < 48) & ((lane & 15) == j), value, small)
+            small = jnp.where((line == i) & (lane < 48) & ((lane & 15) == j), value, small)
     high = small.astype(bf16).astype(f32)
     middle = (small - high).astype(bf16).astype(f32)
     low = small - high - middle
-    small = jnp.where(lane < 16, high, jnp.where(lane < 32, middle, low)).astype(bf16)[:6]
-    for k in range(8):
-        piece_ref[k, :, KEYS:SMALL] = attn_ref[:, D:]
-        piece_ref[k, :, SMALL:QUERY] = small
-        piece_ref[k, :, QUERY:OUT] = attn_ref[:, :D]
-        piece_ref[k, :, OUT:FC] = out_ref[...]
-        piece_ref[k, :, FC:PROJ] = fc_ref[...]
-        piece_ref[k, :, PROJ:] = proj_ref[...]
+    small = jnp.where(lane < 16, high, jnp.where(lane < 32, middle, low))[:6]
+    row[:, KEYS:SMALL] = attn_ref[:, D:].astype(f32)
+    row[:, SMALL:QUERY] = small
+    row[:, QUERY:OUT] = attn_ref[:, :D].astype(f32)
+    row[:, OUT:FC] = out_ref[...].astype(f32)
+    row[:, FC:PROJ] = fc_ref[...].astype(f32)
+    row[:, PROJ : PROJ + FF] = proj_ref[...].astype(f32)
+    row[:, PROJ + FF :] = jnp.zeros((6, WIDE - PROJ - FF), f32)
+    quarters = [row[:, k * FOLD : (k + 1) * FOLD] for k in range(4)]
+    piece = jnp.concatenate(quarters, 0).astype(bf16)
+
+    def copy(k, carry):
+        piece_ref[k] = piece
+        return carry
+
+    lax.fori_loop(0, 16, copy, 0)
 
 
 def block_kernel(piece_ref, attn_ref, feed_ref, rows):
-    for j in range(8):
-        rows[6 * j : 6 * j + 6] = piece_ref[j].astype(f32)
-    for k in range(8):
+    for j in range(16):
+        piece = piece_ref[j].astype(f32)
+        for k in range(4):
+            rows[6 * j : 6 * j + 6, k * FOLD : (k + 1) * FOLD] = piece[6 * k : 6 * k + 6]
+    for k in range(4):
         attn_ref[k] = rows[:, :FC].astype(bf16)
-    feed_ref[...] = rows[:, FC:].astype(bf16)
-
-
-def unblock_kernel(attn_ref, mine_ref, other_ref, piece_ref, rows):
+    feed_ref[...] = rows[:, FC : FC + 2 * FF].astype(bf16)
+
+
+def fold_lanes(rows):
+    width = rows.shape[1] // 4
+    return jnp.concatenate([rows[:, k * width : (k + 1) * width] for k in range(4)], 0)
+
+
+def unblock_kernel(attn_ref, feed_ref, piece_ref, rows):
     rows[:, :G_FC] = jnp.sum(attn_ref[...].astype(f32), 0)
-    rows[:, G_FC:] = mine_ref[lax.axis_index("zl")].astype(f32) + other_ref[...].astype(f32)
-    for j in range(8):
-        piece_ref[j] = rows[6 * j : 6 * j + 6].astype(bf16)
+    for zl in range(2):
+        rows[zl * ROWS : (zl + 1) * ROWS, G_FC:G_WIDE] = feed_ref[zl].astype(f32)
+    if G_WIDE < 4 * G_FOLD:
+        rows[:, G_WIDE:] = jnp.zeros((2 * ROWS, 4 * G_FOLD - G_WIDE), f32)
+    for j in range(16):
+        piece_ref[j] = fold_lanes(rows[6 * j : 6 * j + 6]).astype(bf16)
 
 
 def finish_kernel(piece_ref, attn_ref, out_ref, fc_ref, proj_ref, *refs):
-    vectors, fcb_ref, value_ref = refs[:7], refs[7], refs[8]
+    vectors, fcb_ref, value_ref, rows = refs[:7], refs[7], refs[8], refs[9]
     total = jnp.sum(piece_ref[...].astype(f32), 0)
+    for k in range(4):
+        rows[:, k * G_FOLD : (k + 1) * G_FOLD] = total[6 * k : 6 * k + 6]
+    total = rows[...]
     attn_ref[:, :D] = total[:, G_QUERY:G_FC]
     attn_ref[:, D:] = total[:, KEYS:SMALL]
+    fc_ref[...] = total[:, G_FC:G_OUT]
     out_ref[...] = total[:, G_OUT:G_REST]
-    fc_ref[...] = total[:, G_FC:G_OUT]
     for j in range(4):
+        sent = [piece_ref[k, :6, G_PROJ:G_QUERY].astype(f32) for k in (2 * j, 2 * j + 1, 2 * j + 8, 2 * j + 9)]
+        proj_ref[:, j * SLICE : j * SLICE + SENT] = sent[0] + sent[1] + sent[2] + sent[3]
         proj_ref[:, j * SLICE + SENT : (j + 1) * SLICE] = total[
             :, G_REST + j * REST : G_REST + (j + 1) * REST
         ]
-        proj_ref[:, j * SLICE : j * SLICE + SENT] = (
-            piece_ref[2 * j, :, G_PROJ:G_QUERY].astype(f32)
-            + piece_ref[2 * j + 1, :, G_PROJ:G_QUERY].astype(f32)
-        )
     small = total[:, SMALL:QUERY]
     small = jnp.concatenate([small, jnp.zeros((2, BLOCK), f32)], 0).T
     rows = small[:16] + small[16:32]
@@ -535,11 +558,19 @@
     mid,
     fcsum,
 ):
-    def loads(c, slot):
-        return (
-            pltpu.make_async_copy(feed_ref.at[:, columns(c)], wf.at[slot], in_sem.at[slot, 0]),
-            pltpu.make_async_copy(feed_ref.at[:, columns(c, FF)], wg.at[slot], in_sem.at[slot, 1]),
-        )
+    def load(c, slot):
+        for k in range(16):
+            rows = pl.ds((k // 4 * 4 + k % 2 * 2 + k // 2 % 2) * ROWS, ROWS)
+            for half, (buffer, first) in enumerate(((wf, 0), (wg, FF))):
+                pltpu.make_async_copy(
+                    feed_ref.at[rows, columns(c, first)],
+                    buffer.at[slot, pl.ds(k * ROWS, ROWS)],
+                    in_sem.at[slot, half],
+                ).start()
+
+    def loaded(slot):
+        pltpu.make_async_copy(wf.at[slot], wf.at[slot], in_sem.at[slot, 0]).wait()
+        pltpu.make_async_copy(wg.at[slot], wg.at[slot], in_sem.at[slot, 1]).wait()
 
     def store(c, slot):
         for k in range(16):
@@ -573,7 +604,7 @@
 
     copies = row_copies((mine_ref, other_ref), pl.ds(OUT, D), wout, last_sem)
     start(copies)
-    start(loads(0, 0))
+    load(0, 0)
     ctt[...] = ct_ref[...].T
     branch[...] = jnp.zeros_like(branch)
     gin[...] = jnp.zeros_like(gin)
@@ -591,9 +622,9 @@
 
         @pl.when(c < 3)
         def _():
-            start(loads(c + 1, 1 - slot))
-
-        finish(loads(c, slot))
+            load(c + 1, 1 - slot)
+
+        loaded(slot)
         span = columns(c)
         pre = mm(x2[...], wf[slot]) + fcb_ref[:, span]
         grad_hidden = mm(ct_ref[...], wg[slot])
@@ -768,21 +799,22 @@
     (pieces,) = call(
         piece_kernel,
         "pieces",
-        [shape(8, 6, WIDE)],
+        [shape(16, 24, FOLD)],
         [*vectors, w_attn, w_out, w_fc, w_proj],
+        [pltpu.VMEM((6, WIDE), f32)],
         smem=8,
         moved=2_000_000,
     )
     attn_block, feed_block = call(
         block_kernel,
         "blocks",
-        [shape(8, ROWS, FC), shape(ROWS, 2 * FF)],
-        [lax.all_to_all(pieces, CTX, 0, 0)],
-        [pltpu.VMEM((ROWS, WIDE), f32)],
+        [shape(4, 2 * ROWS, FC), shape(2 * ROWS, 2 * FF)],
+        [lax.all_to_all(pieces, ("zl", "y", "zh"), 0, 0)],
+        [pltpu.VMEM((2 * ROWS, WIDE), f32)],
         moved=4_000_000,
     )
-    feed = lax.all_gather(feed_block, DP, axis=0, tiled=True)
-    attn = lax.all_to_all(attn_block, ("x", "zl"), 0, 0)
+    feed = lax.all_gather(feed_block, ("x", "core"), axis=0, tiled=True)
+    attn = lax.all_to_all(attn_block, "x", 0, 0).reshape(8, ROWS, FC)
     parts = [attn, send(attn, dc=1)]
     one, kv, vec, fcb, early = call(
         first_kernel,
@@ -900,9 +932,6 @@
     grad_kv = tie(grad_kv.reshape(8, TOK, BLOCK), grad_proj)
     grad_kv = lax.all_to_all(grad_kv, CTX, 0, 0)
 
-    grad_fc = tie(grad_fc, grad_kv)
-    other_fc = lax.dynamic_index_in_dim(grad_fc, 1 - lax.axis_index("zl"), 0, False)
-    other_fc = send(other_fc, dl=1)
     small = shape(8, ROWS, 2 * BLOCK)
     grad_x, keep_pack, send_pack = call(
         last_kernel,
@@ -914,14 +943,14 @@
         moved=5_000_000,
     )
     grad_pack = add_all([keep_pack, send(send_pack, dc=1)])
-    both = jnp.concatenate([tie(grad_pack, other_fc), grad_proj, grad_q], 2)
-    both = lax.all_to_all(both, ("x", "zl"), 0, 0)
+    both = jnp.concatenate([grad_pack, grad_proj, grad_q], 2).reshape(4, 2 * ROWS, G_FC)
+    both = lax.all_to_all(both, "x", 0, 0)
     (pieces,) = call(
         unblock_kernel,
         "unblock",
-        [shape(8, 6, G_WIDE)],
-        [both, grad_fc, other_fc],
-        [pltpu.VMEM((ROWS, G_WIDE), f32)],
+        [shape(16, 24, G_FOLD)],
+        [both, grad_fc],
+        [pltpu.VMEM((2 * ROWS, 4 * G_FOLD), f32)],
     )
     results = call(
         finish_kernel,
@@ -934,7 +963,8 @@
         ]
         + [shape(1, 6, dtype=f32)] * 7
         + [shape(1, 24, dtype=f32), shape(1, HD, dtype=f32)],
-        [lax.all_to_all(pieces, CTX, 0, 0)],
+        [lax.all_to_all(pieces, ("zl", "y", "zh"), 0, 0)],
+        [pltpu.VMEM((6, 4 * G_FOLD), f32)],
     )
     grad_w_attn, grad_w_out, grad_w_fc, grad_w_proj = results[:4]
     gain_one, bias_one, bias_query, bias_out, gain_two, bias_two, bias_proj, bias_fc = (

time: 244 us -> 236 us (0.967)
  waiting for transfers between devices: 48.7 us -> 16.9 us
  blocking collectives: 100 us -> 123 us
  Pallas kernels: 58.7 us -> 69.2 us
  starting transfers between devices: 12.9 us -> 7.05 us
    all_to_all x4 -> x5, blocking collectives: 100 us -> 123 us  [the longest x2 56.7 us: local(): lax.all_to_all(pieces, ('zl', 'y', 'zh'), 0, 0)]
    ppermute x5 -> x4, waiting for transfers between devices: 18.6 us -> 6.33 us  [send(): return lax.ppermute(value, AXES, route(**shift))]
    pallas_call x9, Pallas kernels: 58.7 us -> 69.2 us  [call(): pl.pallas_call(kernel, out_shape=outs, in_specs=places, out_specs=[VMEM]...]
    all_to_all x1 -> x0, waiting for transfers between devices: 10.4 us -> none  [local(): grad_kv = lax.all_to_all(grad_kv, CTX, 0, 0)]
    all_to_all x1, waiting for transfers between devices: 5.76 us -> 0.01 us  [local(): grad_proj = add_all(list(lax.all_to_all(grad_proj, 'y', 0, 0)))]
    all_to_all x1 -> x0, starting transfers between devices: 4.4 us -> none  [local(): grad_kv = lax.all_to_all(grad_kv, CTX, 0, 0)]
    all_gather x1, waiting for transfers between devices: 2.77 us -> 0.02 us  [local(): feed = lax.all_gather(feed_block, ('x', 'core'), axis=0, tiled=True)]
  transfers between devices with their start and end apart: 10 -> 8, of which waited for: 7 -> 4; matrix products, arithmetic and copies ran while one was open for 1% -> 1% of each run, Pallas kernels for 13% -> 17%
where the time goes in v4:
time: 236 us; the launch traced here: 235 us
  blocking collectives  123 us (52%)
  Pallas kernels  69.2 us (29%)
  waiting for transfers between devices  16.9 us (7%)
  between operations  14.8 us (6%)
  starting transfers between devices  7.05 us (3%)
  local copies, waits for them, and re-layouts  2.86 us (1%)
    pallas_call x9, Pallas kernels, call(): pl.pallas_call(kernel, out_shape=outs, in_specs=places, out_specs=[VMEM]...  69.2 us
    all_to_all x2, blocking collectives, local(): lax.all_to_all(pieces, ('zl', 'y', 'zh'), 0, 0)  56.7 us
    all_to_all x1, blocking collectives, local(): attn = lax.all_to_all(attn_block, 'x', 0, 0).reshape(8, ROWS, FC)  32.9 us
    all_to_all x1, blocking collectives, local(): both = lax.all_to_all(both, 'x', 0, 0)  17 us
    all_to_all x1, blocking collectives, local(): grad_kv = lax.all_to_all(grad_kv, CTX, 0, 0)  16.1 us
    all_to_all x1, waiting for transfers between devices, local(): kv = lax.all_to_all(kv, CTX, 0, 0).reshape(LENGTH, BLOCK)  10.5 us
    ppermute x4, waiting for transfers between devices, send(): return lax.ppermute(value, AXES, route(**shift))  6.33 us
  transfers between devices with their start and end apart: 8, of which 4 were waited for; matrix products, arithmetic and copies ran while one was open for 1% of the time, Pallas kernels for 17%

profile of v4, /device:TPU:0, one launch (start us, length us, event | category | flops | bytes accessed | tf_op | source)
XLA Modules:
  0.0 234.8 jit_solution(16352977355424305628)
XLA Ops:
  7.2 2.2 pieces.1
  9.5 30.9 %all_to_all.35.piece_ref = bf16[16,24,2048]{2,1,0:T(8,128)(2,1)} all-to-all(bf16[16,24,2048]{2,1,0:T(8,128)(2,1)} %pieces.1), channel_id=1, replica_groups=mesh['x'=4,'zl'=2,'core'=2,'y'=4,'zh'=2] {'zl','y','zh'}, dimensions={0} | all-to-all | bytes 3145728 | tf_op jit(solution)/shard_map/all_to_all | solution.py:812
  40.4 3.4 %blocks.1 = (bf16[4,96,1792]{2,1,0:T(8,128)(2,1)}, bf16[96,6144]{1,0:T(8,128)(2,1)}) custom-call(bf16[16,24,2048]{2,1,0:T(8,128)(2,1)} %all_to_all.35.piece_ref), custom_call_target="tpu_custom_call" | custom-call | bytes 4000000 | tf_op jit(solution)/shard_map/blocks/pallas_call | solution.py:760
  43.8 32.9 %all_to_all.36 = bf16[4,96,1792]{2,1,0:T(8,128)(2,1)S(1)} all-to-all(bf16[4,96,1792]{2,1,0:T(8,128)(2,1)} %get-tuple-element.56), channel_id=1, replica_groups=mesh['x'=4,'zl'=2,'core'=2,'y'=4,'zh'=2] {'x'}, dimensions={0} | all-to-all | bytes 2752512 | tf_op jit(solution)/shard_map/all_to_all | solution.py:817
  76.6 3.1 %collective-permute-done.other_ref = bf16[8,48,1792]{2,1,0:T(8,128)(2,1)S(1)} collective-permute-done((bf16[8,48,1792]{2,1,0:T(8,128)(2,1)S(1)}, bf16[8,48,1792]{2,1,0:T(8,128)(2,1)S(1)}, u32[]{:S(2)}, u32[]{:S(2)}) %collective-permute-start) | collective-permute-done | bytes 1376288 | tf_op jit(solution)/shard_map/ppermute | solution.py:45
  79.8 1.1 copy-done.1
  80.9 3.4 %first.1 = (bf16[256,768]{1,0:T(8,128)(2,1)}, bf16[8,256,128]{2,1,0:T(8,128)(2,1)}, f32[16,768]{1,0:T(8,128)}, f32[1,3072]{1,0:T(1,128)}, bf16[768,256]{1,0:T(8,128)(2,1)}) custom-call(bf16[256,768]{1,0:T(8,128)(2,1)} %bitcast.28, f32[1,64]{1,0:T(1,128)} %bitcast.35, bf16[8,48,1792]{2,1,0:T(8,128)(2,1)} %bitcast.24, bf16[8,48,1792]{2,1,0:T(8,128)(2,1)} %copy-done.1), custom_call_target="tpu_custom_call" | custom-call | flops 100000000 | bytes 4000000 | tf_op jit(solution)/shard_map/first/pallas_call | solution.py:760
  84.3 3.5 %all-to-all-start.2 = ((bf16[8,256,128]{2,1,0:T(8,128)(2,1)}), bf16[8,256,128]{2,1,0:T(8,128)(2,1)S(1)}, u32[]{:S(2)}, u32[]{:S(2)}) async-start(bf16[8,256,128]{2,1,0:T(8,128)(2,1)} %get-tuple-element.59), calls=%async_computation.2 | async-start | bytes 1048576 | tf_op jit(solution)/shard_map/all_to_all | solution.py:835
  88.5 10.5 %all-to-all-done.2 = bf16[8,256,128]{2,1,0:T(8,128)(2,1)S(1)} async-done(((bf16[8,256,128]{2,1,0:T(8,128)(2,1)}), bf16[8,256,128]{2,1,0:T(8,128)(2,1)S(1)}, u32[]{:S(2)}, u32[]{:S(2)}) %all-to-all-start.2) | async-done | bytes 524320 | tf_op jit(solution)/shard_map/all_to_all | solution.py:835
  99.0 0.8 copy-done.3
  99.8 11.5 %attend.1 = (bf16[256,768]{1,0:T(8,128)(2,1)}, bf16[256,768]{1,0:T(8,128)(2,1)}, f32[2,6,8,256]{3,2,1,0:T(8,128)}, bf16[768,768]{1,0:T(8,128)(2,1)}) custom-call(s32[1]{0:T(128)S(6)} %copy.33.length_ref, s32[1,16]{1,0:T(1,128)} %order_ref.3, s32[1,2048]{1,0:T(1,128)} %files_ref.3, bf16[256,768]{1,0:T(8,128)(2,1)} %get-tuple-element.57.one_ref, ...), custom_call_target="tpu_custom_call" | custom-call | flops 10000000000 | bytes 4000000 | tf_op jit(solution)/shard_map/attend/pallas_call | solution.py:760
  111.4 17.3 %feed.1 = (bf16[256,768]{1,0:T(8,128)(2,1)}, f32[256,768]{1,0:T(8,128)}, bf16[256,768]{1,0:T(8,128)(2,1)}, f32[8,768]{1,0:T(8,128)}, bf16[4,8,48,128]{3,2,1,0:T(...) custom-call(bf16[768,6144]{1,0:T(8,128)(2,1)} %all-gather.2.cloned.1.call-done.feed_ref, ...), custom_call_target="tpu_custom_call" | custom-call | flops 8000000000 | bytes 30000000 | tf_op jit(solution)/shard_map/feed/pallas_call | solution.py:760
  128.8 1.0 copy-done.6
  129.7 1.7 collective-permute-done.1
  131.5 0.9 add_convert_fusion.1
  132.4 3.5 %all-to-all-start.3 = ((bf16[4,8,48,128]{3,2,1,0:T(8,128)(2,1)}), bf16[4,8,48,128]{3,2,1,0:T(8,128)(2,1)S(1)}, u32[]{:S(2)}, u32[]{:S(2)}) async-start(bf16[4,8,48,128]{3,2,1,0:T(8,128)(2,1)} %add_convert_fusion.1), calls=%async_computation.3 | async-start | bytes 786432 | tf_op jit(solution)/shard_map/all_to_all | solution.py:908
  135.8 21.2 %attend_back.1 = (bf16[256,768]{1,0:T(8,128)(2,1)}, bf16[8,48,768]{2,1,0:T(8,128)(2,1)}, bf16[8,48,768]{2,1,0:T(8,128)(2,1)}, bf16[16,128,128]{2,1,0:T(8,128)(2,1)}) custom-call(s32[1]{0:T(128)S(6)} %copy.33.length_ref, s32[1,16]{1,0:T(1,128)} %order_ref.3, s32[1,2048]{1,0:T(1,128)} %files_ref.3, bf16[256,768]{1,0:T(8,128)(2,1)} %get-tuple-element.63.q_ref, ...), custom_call_target="tpu_custom_call" | custom-call | flops 20000000000 | bytes 6000000 | tf_op jit(solution)/shard_map/attend_back/pallas_call | solution.py:760
  157.1 16.1 %all_to_all.37.dkv_ref = bf16[8,256,128]{2,1,0:T(8,128)(2,1)} all-to-all(bf16[8,256,128]{2,1,0:T(8,128)(2,1)} %bitcast.34), channel_id=1, replica_groups=mesh['x'=4,'zl'=2,'core'=2,'y'=4,'zh'=2] {'y','zh'}, dimensions={0} | all-to-all | bytes 1048576 | tf_op jit(solution)/shard_map/all_to_all | solution.py:933
  173.2 4.2 %last.1 = (bf16[256,768]{1,0:T(8,128)(2,1)}, bf16[8,48,256]{2,1,0:T(8,128)(2,1)}, bf16[8,48,256]{2,1,0:T(8,128)(2,1)}) custom-call(bf16[256,768]{1,0:T(8,128)(2,1)} %bitcast.30, bf16[256,768]{1,0:T(8,128)(2,1)} %get-tuple-element.57.one_ref, bf16[256,768]{1,0:T(8,128)(2,1)} %get-tuple-element.69.gq_ref, f32[256,768]{1,0:T(8,128)} %get-tuple-element.70.gmid_ref, ...), custom_call_target="tpu_custom_call" | custom-call | flops 1000000000 | bytes 5000000 | tf_op jit(solution)/shard_map/last/pallas_call | solution.py:760
  177.6 1.5 collective-permute-done.2
  179.2 17.0 %all_to_all.38.attn_ref = bf16[4,96,1152]{2,1,0:T(8,128)(2,1)} all-to-all(bf16[4,96,1152]{2,1,0:T(8,128)(2,1)S(1)} %bitcast.27), channel_id=1, replica_groups=mesh['x'=4,'zl'=2,'core'=2,'y'=4,'zh'=2] {'x'}, dimensions={0} | all-to-all | bytes 1769472 | tf_op jit(solution)/shard_map/all_to_all | solution.py:947
  196.2 3.5 %unblock.1 = bf16[16,24,1920]{2,1,0:T(8,128)(2,1)} custom-call(bf16[4,96,1152]{2,1,0:T(8,128)(2,1)} %all_to_all.38.attn_ref, bf16[2,48,6400]{2,1,0:T(8,128)(2,1)} %bitcast.31), custom_call_target="tpu_custom_call" | custom-call | tf_op jit(solution)/shard_map/unblock/pallas_call | solution.py:760
  199.7 25.8 %all_to_all.39.piece_ref = bf16[16,24,1920]{2,1,0:T(8,128)(2,1)} all-to-all(bf16[16,24,1920]{2,1,0:T(8,128)(2,1)} %unblock.1), channel_id=1, replica_groups=mesh['x'=4,'zl'=2,'core'=2,'y'=4,'zh'=2] {'zl','y','zh'}, dimensions={0} | all-to-all | bytes 2949120 | tf_op jit(solution)/shard_map/all_to_all | solution.py:966
  225.5 2.4 %finish.1 = (f32[6,896]{1,0:T(8,128)}, f32[6,768]{1,0:T(8,128)}, f32[6,3072]{1,0:T(8,128)}, f32[6,3072]{1,0:T(8,128)}, f32[1,6]{1,0:T(1,128)}, /*index=5*/f32[1,...) custom-call(bf16[16,24,1920]{2,1,0:T(8,128)(2,1)} %all_to_all.39.pie, ...), custom_call_target="tpu_custom_call" | custom-call | tf_op jit(solution)/shard_map/finish/pallas_call | solution.py:760
  (27 shorter events, 0.5 us)
Async XLA Ops:
  7.2 104.2 %all-gather.2.cloned.1.call-start = ((), (), s32[]{:S(2)}) async-start(), calls=%async_computation.8 | async-start | bytes 10616832 | tf_op jit(solution)/shard_map/all_gather | solution.py:816
  76.6 3.1 %copy-start = (bf16[4,96,1792]{2,1,0:T(8,128)(2,1)}, bf16[4,96,1792]{2,1,0:T(8,128)(2,1)S(1)}, u32[]{:S(2)}) copy-start(bf16[4,96,1792]{2,1,0:T(8,128)(2,1)S(1)} %all_to_all.36) | copy-start | bytes 4128772
  76.6 3.1 %collective-permute-start = (bf16[8,48,1792]{2,1,0:T(8,128)(2,1)S(1)}, bf16[8,48,1792]{2,1,0:T(8,128)(2,1)S(1)}, u32[]{:S(2)}, u32[]{:S(2)}) collective-permute-start(bf16[8,48,1792]{2,1,0:T(8,128)(2,1)S(1)} %bitcast.23), channel_id=1, source_target_pairs={{0,8},{1,9},{2,10},{3,11},{4,12},{5,13},{6,14},{7,15},{8,0},{9,1},... | collective-permute-start | bytes 4128776 | tf_op jit(solution)/shard_map/ppermute | solution.py:45
  79.8 1.1 copy-start.1
  84.3 14.7 %all-to-all-start.2 = ((bf16[8,256,128]{2,1,0:T(8,128)(2,1)}), bf16[8,256,128]{2,1,0:T(8,128)(2,1)S(1)}, u32[]{:S(2)}, u32[]{:S(2)}) async-start(bf16[8,256,128]{2,1,0:T(8,128)(2,1)} %get-tuple-element.59), calls=%async_computation.2 | async-start | bytes 1048576 | tf_op jit(solution)/shard_map/all_to_all | solution.py:835
  87.8 108.4 %reduce-scatter.2.cloned.1.call-start = ((), (), s32[]{:S(2)}) async-start(), calls=%async_computation.9 | async-start | bytes 11059200 | tf_op jit(solution)/shard_map/reduce_scatter | solution.py:905
  99.0 0.8 copy-start.3
  128.7 1.0 copy-start.6
  128.7 2.7 %copy-start.4 = (bf16[4,8,48,128]{3,2,1,0:T(8,128)(2,1)S(1)}, bf16[4,8,48,128]{3,2,1,0:T(8,128)(2,1)}, u32[]{:S(2)}) copy-start(bf16[4,8,48,128]{3,2,1,0:T(8,128)(2,1)} %get-tuple-element.65) | copy-start | bytes 1179652
  129.7 1.7 collective-permute-start.1
  132.4 24.7 %all-to-all-start.3 = ((bf16[4,8,48,128]{3,2,1,0:T(8,128)(2,1)}), bf16[4,8,48,128]{3,2,1,0:T(8,128)(2,1)S(1)}, u32[]{:S(2)}, u32[]{:S(2)}) async-start(bf16[4,8,48,128]{3,2,1,0:T(8,128)(2,1)} %add_convert_fusion.1), calls=%async_computation.3 | async-start | bytes 786432 | tf_op jit(solution)/shard_map/all_to_all | solution.py:908
  157.0 20.4 %collective-permute-start.3 = (bf16[8,48,768]{2,1,0:T(8,128)(2,1)}, bf16[8,48,768]{2,1,0:T(8,128)(2,1)S(1)}, u32[]{:S(2)}, u32[]{:S(2)}) collective-permute-start(bf16[8,48,768]{2,1,0:T(8,128)(2,1)} %get-tuple-element.80), channel_id=1, source_target_pairs={{0,8},{1,9},{2,10},{3,11},{4,12},{5,13},{6,14},{7,15},{8,0},{9,1},... | collective-permute-start | bytes 1769480 | tf_op jit(solution)/shard_map/ppermute | solution.py:45
  173.2 4.2 %copy-start.2 = (bf16[8,48,768]{2,1,0:T(8,128)(2,1)S(1)}, bf16[8,48,768]{2,1,0:T(8,128)(2,1)}, u32[]{:S(2)}) copy-start(bf16[8,48,768]{2,1,0:T(8,128)(2,1)} %get-tuple-element.79) | copy-start | bytes 1769476
  177.4 1.7 copy-start.5
  177.4 1.7 collective-permute-start.2
Sparse Core Ops, SparseCore 0:
  43.9 60.5 all-gather.1
  128.9 53.7 reduce-scatter.1

commit v5 on v4

--- a/solution.py
+++ b/solution.py
@@ -99,9 +99,9 @@
 SLICE = 768
 KEYS, SMALL, QUERY, OUT, FC, PROJ, WIDE = 0, 128, 256, 1024, 1792, 4864, 8192
 FOLD = WIDE // 4
-SENT = 128
+SENT = 256
 REST = SLICE - SENT
-G_PROJ, G_QUERY, G_FC, G_OUT, G_REST, G_WIDE = 256, 384, 1152, 4224, 4992, 7552
+G_PROJ, G_QUERY, G_FC, G_OUT, G_REST, G_WIDE = 256, 512, 1280, 4352, 5120, 7168
 G_FOLD = (G_WIDE + 511) // 512 * BLOCK
 REDUCED = G_WIDE - G_FC
 
@@ -153,8 +153,9 @@
     return jnp.concatenate([rows[:, k * width : (k + 1) * width] for k in range(4)], 0)
 
 
-def unblock_kernel(attn_ref, feed_ref, piece_ref, rows):
-    rows[:, :G_FC] = jnp.sum(attn_ref[...].astype(f32), 0)
+def unblock_kernel(attn_ref, query_ref, feed_ref, piece_ref, rows):
+    rows[:, :G_QUERY] = jnp.sum(attn_ref[...].astype(f32), 0)
+    rows[:, G_QUERY:G_FC] = query_ref[...].astype(f32)
     for zl in range(2):
         rows[zl * ROWS : (zl + 1) * ROWS, G_FC:G_WIDE] = feed_ref[zl].astype(f32)
     if G_WIDE < 4 * G_FOLD:
@@ -209,7 +210,7 @@
 
 
 def first_kernel(
-    x_ref, vbias_ref, mine_ref, other_ref, one_ref, kv_ref, vec_ref, fcb_ref, early_ref, sem
+    x_ref, vbias_ref, mine_ref, other_ref, one_ref, kv_ref, vec_ref, early_ref, sem
 ):
     copies = row_copies((mine_ref, other_ref), pl.ds(0, QUERY), early_ref, sem)
     start(copies)
@@ -224,15 +225,6 @@
     kv = (mm(one, early_ref[:, :BLOCK]) + bias).astype(bf16)
     for k in range(8):
         kv_ref[k] = kv
-    spread = four_apart(BLOCK, 512, 0)
-    terms = turned[0:48].astype(bf16)
-    term = lax.broadcasted_iota(jnp.int32, (48, 512), 0) % 16 - 7
-    mine = term == lax.broadcasted_iota(jnp.int32, (48, 512), 1) % 4
-    for g in range(6):
-        wide = mm(terms[:, g * BLOCK : (g + 1) * BLOCK], spread)
-        fcb_ref[:, g * 512 : (g + 1) * 512] = jnp.sum(
-            jnp.where(mine, wide, 0.0), 0, keepdims=True
-        )
 
 
 def read_plan(length_ref, order_ref, files_ref):
@@ -347,46 +339,68 @@
     return values.reshape(values.shape[0] // 8, 8, values.shape[1])
 
 
-def forward_kernel(
+def query_kernel(
     length_ref,
     order_ref,
     files_ref,
     one_ref,
     vec_ref,
-    kv_ref,
+    early_ref,
     mine_ref,
     other_ref,
     q_ref,
+    qt_ref,
+    fcb_ref,
+    wq,
+    sem,
+):
+    copies = row_copies((mine_ref, other_ref), pl.ds(QUERY, D), wq, sem)
+    start(copies)
+    plan = read_plan(length_ref, order_ref, files_ref)
+    finish(copies)
+    q = (mm(one_ref[...], wq[...]) + vec_ref[2:3]).astype(bf16)
+    q_ref[...] = q
+    terms = early_ref[:, BLOCK:].T[:48]
+    spread = four_apart(BLOCK, 512, 0)
+    term = lax.broadcasted_iota(jnp.int32, (48, 512), 0) % 16 - 7
+    mine = term == lax.broadcasted_iota(jnp.int32, (48, 512), 1) % 4
+    for g in range(6):
+        wide = mm(terms[:, g * BLOCK : (g + 1) * BLOCK], spread)
+        fcb_ref[:, g * 512 : (g + 1) * 512] = jnp.sum(
+            jnp.where(mine, wide, 0.0), 0, keepdims=True
+        )
+    empty = jnp.zeros((HD, 2 * BLOCK), bf16)
+    for b in range(2):
+        place, _, _ = block_plan(plan, order_ref, b)
+        marks = query_marks(plan, place)
+        for p in range(PAIRS):
+            block = q[b * BLOCK : (b + 1) * BLOCK, p * BLOCK : (p + 1) * BLOCK] * 0.125
+            top = jnp.concatenate([fold_heads(block), empty], 0)
+            fill(qt_ref.at[b, p], top, marks)
+
+
+def forward_kernel(
+    length_ref,
+    order_ref,
+    files_ref,
+    kv_ref,
+    qt_ref,
     att_ref,
     lse_ref,
-    wq_ref,
     keys,
-    qt,
     vt,
     scores,
     tops,
     sums,
     mixed,
-    sem,
 ):
-    copies = row_copies((mine_ref, other_ref), pl.ds(QUERY, D), wq_ref, sem)
-    start(copies)
     plan = read_plan(length_ref, order_ref, files_ref)
     place_keys(plan, order_ref, kv_ref, keys)
     for k in range(BLOCKS):
-        vt[:, k * BLOCK : (k + 1) * BLOCK] = (
-            keys[k * BLOCK : (k + 1) * BLOCK, :BLOCK].T[HD:]
-        )
-    finish(copies)
-    q = (mm(one_ref[...], wq_ref[...]) + vec_ref[2:3]).astype(bf16)
-    q_ref[...] = q
-    empty = jnp.zeros((HD, 2 * BLOCK), bf16)
+        vt[:, k * BLOCK : (k + 1) * BLOCK] = keys[k * BLOCK : (k + 1) * BLOCK, :BLOCK].T[HD:]
     for b in range(2):
         place, low, count = block_plan(plan, order_ref, b)
-        marks = query_marks(plan, place)
-        for p in range(PAIRS):
-            block = q[b * BLOCK : (b + 1) * BLOCK, p * BLOCK : (p + 1) * BLOCK] * 0.125
-            fill(qt.at[p], jnp.concatenate([fold_heads(block), empty], 0), marks)
+        qt = qt_ref.at[b]
         own = own_keys(keys, place)
         bias = own_bias(plan, place)
         for p in range(PAIRS):
@@ -512,13 +526,14 @@
 
     lax.fori_loop(0, BLOCKS, give, 0)
     gwq[...] = mm(one_ref[...].T, gq_ref[...]).astype(bf16)
-    deal_rows(gwq, keep_ref, send_ref)
-
-
-def deal_rows(source, keep_ref, send_ref):
+    deal_rows(gwq, keep_ref, send_ref, lax.axis_index("x"))
+
+
+def deal_rows(source, keep_ref, send_ref, x=0):
     for k in range(8):
-        keep_ref[k] = source[row_span(k, 0), :]
-        send_ref[k] = source[row_span(k, 1), :]
+        there = lax.rem(k // 2 - x + 4, 4) * 2 + k % 2
+        keep_ref[there] = source[row_span(k, 0), :]
+        send_ref[there] = source[row_span(k, 1), :]
 
 
 def columns(c, first=0):
@@ -816,14 +831,13 @@
     feed = lax.all_gather(feed_block, ("x", "core"), axis=0, tiled=True)
     attn = lax.all_to_all(attn_block, "x", 0, 0).reshape(8, ROWS, FC)
     parts = [attn, send(attn, dc=1)]
-    one, kv, vec, fcb, early = call(
+    one, kv, vec, early = call(
         first_kernel,
         "first",
         [
             shape(TOK, D),
             shape(8, TOK, BLOCK),
             shape(16, D, dtype=f32),
-            shape(1, FF, dtype=f32),
             shape(D, 2 * BLOCK),
         ],
         [x, value_bias[None], *parts],
@@ -836,32 +850,36 @@
 
     wide = (PAIRS, 2 * BLOCK, 2 * BLOCK)
     plan = [lengths, order, files]
-    q, att, lse, wq = call(
+    q, qt, fcb, wq = call(
+        query_kernel,
+        "query",
+        [shape(TOK, D), shape(2, *wide), shape(1, FF, dtype=f32), shape(D, D)],
+        [*plan, one, vec, early, *parts],
+        [pltpu.SemaphoreType.DMA],
+        smem=2,
+        hbm=(6, 7),
+        flops=300_000_000,
+        moved=4_000_000,
+    )
+    att, lse = call(
         forward_kernel,
         "attend",
-        [
-            shape(TOK, D),
-            shape(TOK, D),
-            shape(2, PAIRS, 8, 2 * BLOCK, dtype=f32),
-            shape(D, D),
-        ],
-        [*plan, one, vec, kv, *parts],
+        [shape(TOK, D), shape(2, PAIRS, 8, 2 * BLOCK, dtype=f32)],
+        [*plan, kv, qt],
         [
             pltpu.VMEM((LENGTH, 2 * BLOCK), bf16),
-            pltpu.VMEM(wide, bf16),
             pltpu.VMEM((HD, LENGTH), bf16),
             pltpu.VMEM((PAIRS, LENGTH, 2 * BLOCK), f32),
             pltpu.VMEM((PAIRS, 8, 2 * BLOCK), f32),
             pltpu.VMEM((PAIRS, 8, 2 * BLOCK), f32),
             pltpu.VMEM((PAIRS, HD, 2 * BLOCK), f32),
-            pltpu.SemaphoreType.DMA,
         ],
         smem=2,
-        hbm=(6, 7),
         flops=10_000_000_000,
         moved=4_000_000,
         exps=6_000_000,
     )
+
     half = shape(8, ROWS, D)
     sliced = shape(4, 8, ROWS, SENT)
     output, grad_middle, grad_att, sums, keep_proj, send_proj, grad_fc = call(
@@ -928,7 +946,10 @@
         moved=6_000_000,
         exps=6_000_000,
     )
-    grad_q = add_all([keep_q, send(send_q, dc=1)])
+    got_q = send(send_q, dc=1)
+    parts_q = [add_all([keep_q[2 * k : 2 * k + 2], got_q[2 * k : 2 * k + 2]]) for k in range(4)]
+    parts_q = [parts_q[0]] + [send(parts_q[k], dx=k) for k in (1, 2, 3)]
+    grad_q = add_all(parts_q).reshape(2 * ROWS, D)
     grad_kv = tie(grad_kv.reshape(8, TOK, BLOCK), grad_proj)
     grad_kv = lax.all_to_all(grad_kv, CTX, 0, 0)
 
@@ -943,13 +964,14 @@
         moved=5_000_000,
     )
     grad_pack = add_all([keep_pack, send(send_pack, dc=1)])
-    both = jnp.concatenate([grad_pack, grad_proj, grad_q], 2).reshape(4, 2 * ROWS, G_FC)
+    both = jnp.concatenate([grad_pack, grad_proj], 2).reshape(4, 2 * ROWS, G_QUERY)
+    both = tie(both, grad_q)
     both = lax.all_to_all(both, "x", 0, 0)
     (pieces,) = call(
         unblock_kernel,
         "unblock",
         [shape(16, 24, G_FOLD)],
-        [both, grad_fc],
+        [both, grad_q, grad_fc],
         [pltpu.VMEM((2 * ROWS, 4 * G_FOLD), f32)],
     )
     results = call(

time: 236 us -> 228 us (0.966)
  blocking collectives: 123 us -> 100 us
  starting transfers between devices: 7.05 us -> 26.7 us
  Pallas kernels: 69.2 us -> 57.1 us
  waiting for transfers between devices: 16.9 us -> 21.1 us
    all_to_all x1 -> x0, blocking collectives: 16.1 us -> none  [local(): grad_kv = lax.all_to_all(grad_kv, CTX, 0, 0)]
    all_to_all x0 -> x1, starting transfers between devices: none -> 12.7 us  [local(): grad_kv = lax.all_to_all(grad_kv, CTX, 0, 0)]
    pallas_call x9 -> x10, Pallas kernels: 69.2 us -> 57.1 us  [call(): pl.pallas_call(kernel, out_shape=outs, in_specs=places, out_specs=[VMEM]...]
    all_to_all x0 -> x1, waiting for transfers between devices: none -> 7.84 us  [local(): grad_kv = lax.all_to_all(grad_kv, CTX, 0, 0)]
    all_to_all x1, blocking collectives: 17 us -> 11.7 us  [local(): both = lax.all_to_all(both, 'x', 0, 0)]
    all_to_all x1, waiting for transfers between devices: 10.5 us -> 6.03 us  [local(): kv = lax.all_to_all(kv, CTX, 0, 0).reshape(LENGTH, BLOCK)]
    ppermute x4 -> x7, starting transfers between devices: 0.01 us -> 4.04 us  [send(): return lax.ppermute(value, AXES, route(**shift))]
    all_to_all x1, starting transfers between devices: 3.46 us -> 6.32 us  [local(): grad_proj = add_all(list(lax.all_to_all(grad_proj, 'y', 0, 0)))]
  transfers between devices with their start and end apart: 8 -> 12, of which waited for: 4 -> 6; matrix products, arithmetic and copies ran while one was open for 1% -> 1% of each run, Pallas kernels for 17% -> 13%
where the time goes in v5:
time: 228 us; the launch traced here: 227 us
  blocking collectives  100 us (44%)
  Pallas kernels  57.1 us (25%)
  starting transfers between devices  26.7 us (12%)
  waiting for transfers between devices  21.1 us (9%)
  between operations  14.8 us (6%)
  local copies, waits for them, and re-layouts  3.83 us (2%)
  other arithmetic  3.08 us (1%)
    pallas_call x10, Pallas kernels, call(): pl.pallas_call(kernel, out_shape=outs, in_specs=places, out_specs=[VMEM]...  57.1 us
    all_to_all x2, blocking collectives, local(): lax.all_to_all(pieces, ('zl', 'y', 'zh'), 0, 0)  55.7 us
    all_to_all x1, blocking collectives, local(): attn = lax.all_to_all(attn_block, 'x', 0, 0).reshape(8, ROWS, FC)  32.9 us
    all_to_all x1, starting transfers between devices, local(): grad_kv = lax.all_to_all(grad_kv, CTX, 0, 0)  12.7 us
    all_to_all x1, blocking collectives, local(): both = lax.all_to_all(both, 'x', 0, 0)  11.7 us
    all_to_all x1, waiting for transfers between devices, local(): grad_kv = lax.all_to_all(grad_kv, CTX, 0, 0)  7.84 us
    all_to_all x1, starting transfers between devices, local(): grad_proj = add_all(list(lax.all_to_all(grad_proj, 'y', 0, 0)))  6.32 us
    ppermute x7, waiting for transfers between devices, send(): return lax.ppermute(value, AXES, route(**shift))  6.28 us
  transfers between devices with their start and end apart: 12, of which 6 were waited for; matrix products, arithmetic and copies ran while one was open for 1% of the time, Pallas kernels for 13%

profile of v5, /device:TPU:0, one launch (start us, length us, event | category | flops | bytes accessed | tf_op | source)
XLA Modules:
  0.0 226.9 jit_solution(7267664879984483980)
XLA Ops:
  7.2 2.2 pieces.1
  9.5 30.9 %all_to_all.35.piece_ref = bf16[16,24,2048]{2,1,0:T(8,128)(2,1)} all-to-all(bf16[16,24,2048]{2,1,0:T(8,128)(2,1)} %pieces.1), channel_id=1, replica_groups=mesh['x'=4,'zl'=2,'core'=2,'y'=4,'zh'=2] {'zl','y','zh'}, dimensions={0} | all-to-all | bytes 3145728 | tf_op jit(solution)/shard_map/all_to_all | solution.py:827
  40.4 3.4 %blocks.1 = (bf16[4,96,1792]{2,1,0:T(8,128)(2,1)}, bf16[96,6144]{1,0:T(8,128)(2,1)}) custom-call(bf16[16,24,2048]{2,1,0:T(8,128)(2,1)} %all_to_all.35.piece_ref), custom_call_target="tpu_custom_call" | custom-call | bytes 4000000 | tf_op jit(solution)/shard_map/blocks/pallas_call | solution.py:775
  43.8 32.9 %all_to_all.36 = bf16[4,96,1792]{2,1,0:T(8,128)(2,1)S(1)} all-to-all(bf16[4,96,1792]{2,1,0:T(8,128)(2,1)} %get-tuple-element.58), channel_id=1, replica_groups=mesh['x'=4,'zl'=2,'core'=2,'y'=4,'zh'=2] {'x'}, dimensions={0} | all-to-all | bytes 2752512 | tf_op jit(solution)/shard_map/all_to_all | solution.py:832
  76.7 3.1 %collective-permute-done.other_ref = bf16[8,48,1792]{2,1,0:T(8,128)(2,1)S(1)} collective-permute-done((bf16[8,48,1792]{2,1,0:T(8,128)(2,1)S(1)}, bf16[8,48,1792]{2,1,0:T(8,128)(2,1)S(1)}, u32[]{:S(2)}, u32[]{:S(2)}) %collective-permute-start) | collective-permute-done | bytes 1376288 | tf_op jit(solution)/shard_map/ppermute | solution.py:45
  80.9 3.4 %first.1 = (bf16[256,768]{1,0:T(8,128)(2,1)}, bf16[8,256,128]{2,1,0:T(8,128)(2,1)}, f32[16,768]{1,0:T(8,128)}, bf16[768,256]{1,0:T(8,128)(2,1)}) custom-call(bf16[256,768]{1,0:T(8,128)(2,1)} %bitcast.29, f32[1,64]{1,0:T(1,128)} %bitcast.37, bf16[8,48,1792]{2,1,0:T(8,128)(2,1)} %bitcast.24, bf16[8,48,1792]{2,1,0:T(8,128)(2,1)} %copy-done.1), custom_call_target="tpu_custom_call" | custom-call | flops 100000000 | bytes 4000000 | tf_op jit(solution)/shard_map/first/pallas_call | solution.py:775
  84.2 3.5 %all-to-all-start.2 = ((bf16[8,256,128]{2,1,0:T(8,128)(2,1)}), bf16[8,256,128]{2,1,0:T(8,128)(2,1)S(1)}, u32[]{:S(2)}, u32[]{:S(2)}) async-start(bf16[8,256,128]{2,1,0:T(8,128)(2,1)} %get-tuple-element.59), calls=%async_computation.2 | async-start | bytes 1048576 | tf_op jit(solution)/shard_map/all_to_all | solution.py:849
  88.4 4.5 %query.1 = (bf16[256,768]{1,0:T(8,128)(2,1)}, bf16[2,6,256,256]{3,2,1,0:T(8,128)(2,1)}, f32[1,3072]{1,0:T(1,128)}, bf16[768,768]{1,0:T(8,128)(2,1)}) custom-call(s32[1]{0:T(128)S(6)} %copy.33.length_ref, s32[1,16]{1,0:T(1,128)} %order_ref.5, s32[1,2048]{1,0:T(1,128)} %files_ref.5, bf16[256,768]{1,0:T(8,128)(2,1)} %get-tuple-element.60.one_ref, ...), custom_call_target="tpu_custom_call" | custom-call | flops 300000000 | bytes 4000000 | tf_op jit(solution)/shard_map/query/pallas_call | solution.py:775
  92.9 6.0 %all-to-all-done.2 = bf16[8,256,128]{2,1,0:T(8,128)(2,1)S(1)} async-done(((bf16[8,256,128]{2,1,0:T(8,128)(2,1)}), bf16[8,256,128]{2,1,0:T(8,128)(2,1)S(1)}, u32[]{:S(2)}, u32[]{:S(2)}) %all-to-all-start.2) | async-done | bytes 524320 | tf_op jit(solution)/shard_map/all_to_all | solution.py:849
  99.8 5.7 %attend.1 = (bf16[256,768]{1,0:T(8,128)(2,1)}, f32[2,6,8,256]{3,2,1,0:T(8,128)}) custom-call(s32[1]{0:T(128)S(6)} %copy.33.length_ref, s32[1,16]{1,0:T(1,128)} %order_ref.5, s32[1,2048]{1,0:T(1,128)} %files_ref.5, bf16[2048,128]{1,0:T(8,128)(2,1)} %bitcast.34, bf16[2,6,256,256]{3,2,1,0:T(8,128)(2,1)} %get-tuple-element.63.qt_ref), custom_call_target="tpu_custom_call" | custom-call | flops 10000000000 | bytes 4000000 | tf_op jit(solution)/shard_map/attend/pallas_call | solution.py:775
  105.5 17.3 %feed.1 = (bf16[256,768]{1,0:T(8,128)(2,1)}, f32[256,768]{1,0:T(8,128)}, bf16[256,768]{1,0:T(8,128)(2,1)}, f32[8,768]{1,0:T(8,128)}, bf16[4,8,48,256]{3,2,1,0:T(...) custom-call(bf16[768,6144]{1,0:T(8,128)(2,1)} %all-gather.2.cloned.1.call-done.feed_ref, ...), custom_call_target="tpu_custom_call" | custom-call | flops 8000000000 | bytes 30000000 | tf_op jit(solution)/shard_map/feed/pallas_call | solution.py:775
  122.9 1.1 copy-done.6
  124.0 2.3 %collective-permute-done.1 = bf16[4,8,48,256]{3,2,1,0:T(8,128)(2,1)S(1)} collective-permute-done((bf16[4,8,48,256]{3,2,1,0:T(8,128)(2,1)S(1)}, bf16[4,8,48,256]{3,2,1,0:T(8,128)(2,1)S(1)}, u32[]{:S(2)}, u32[]{:S(2)}) %collective-permute-start.1) | collective-permute-done | bytes 786464 | tf_op jit(solution)/shard_map/ppermute | solution.py:45
  126.3 1.1 add_convert_fusion
  127.4 6.3 %all-to-all-start.3 = ((bf16[4,8,48,256]{3,2,1,0:T(8,128)(2,1)}), bf16[4,8,48,256]{3,2,1,0:T(8,128)(2,1)S(1)}, u32[]{:S(2)}, u32[]{:S(2)}) async-start(bf16[4,8,48,256]{3,2,1,0:T(8,128)(2,1)} %add_convert_fusion), calls=%async_computation.3 | async-start | bytes 1572864 | tf_op jit(solution)/shard_map/all_to_all | solution.py:926
  133.7 11.0 %attend_back.1 = (bf16[256,768]{1,0:T(8,128)(2,1)}, bf16[8,48,768]{2,1,0:T(8,128)(2,1)}, bf16[8,48,768]{2,1,0:T(8,128)(2,1)}, bf16[16,128,128]{2,1,0:T(8,128)(2,1)}) custom-call(s32[1]{0:T(128)S(6)} %copy.33.length_ref, s32[1,16]{1,0:T(1,128)} %order_ref.5, s32[1,2048]{1,0:T(1,128)} %files_ref.5, bf16[256,768]{1,0:T(8,128)(2,1)} %get-tuple-element.67.q_ref, ...), custom_call_target="tpu_custom_call" | custom-call | flops 20000000000 | bytes 6000000 | tf_op jit(solution)/shard_map/attend_back/pallas_call | solution.py:775
  146.4 12.7 %all-to-all-start.4 = ((bf16[8,256,128]{2,1,0:T(8,128)(2,1)}), bf16[8,256,128]{2,1,0:T(8,128)(2,1)S(1)}, u32[]{:S(2)}, u32[]{:S(2)}) async-start(bf16[8,256,128]{2,1,0:T(8,128)(2,1)} %bitcast.36), calls=%async_computation.4 | async-start | bytes 1048576 | tf_op jit(solution)/shard_map/all_to_all | solution.py:954
  159.3 3.2 %collective-permute-start.6 = (bf16[2,48,768]{2,1,0:T(8,128)(2,1)S(1)}, bf16[2,48,768]{2,1,0:T(8,128)(2,1)S(1)}, u32[]{:S(2)}, u32[]{:S(2)}) collective-permute-start(bf16[2,48,768]{2,1,0:T(8,128)(2,1)S(1)} %get-tuple-element.100), channel_id=1, source_target_pairs={{0,96},{1,97},{2,98},{3,99},{4,100},{5,101},{6,102},{7,103},{8,104... | collective-permute-start | bytes 442376 | tf_op jit(solution)/shard_map/ppermute | solution.py:45
  162.6 7.8 %all-to-all-done.4.dkv_ref = bf16[8,256,128]{2,1,0:T(8,128)(2,1)S(1)} async-done(((bf16[8,256,128]{2,1,0:T(8,128)(2,1)}), bf16[8,256,128]{2,1,0:T(8,128)(2,1)S(1)}, u32[]{:S(2)}, u32[]{:S(2)}) %all-to-all-start.4) | async-done | bytes 524320 | tf_op jit(solution)/shard_map/all_to_all | solution.py:954
  171.2 4.1 %last.1 = (bf16[256,768]{1,0:T(8,128)(2,1)}, bf16[8,48,256]{2,1,0:T(8,128)(2,1)}, bf16[8,48,256]{2,1,0:T(8,128)(2,1)}) custom-call(bf16[256,768]{1,0:T(8,128)(2,1)} %bitcast.31, bf16[256,768]{1,0:T(8,128)(2,1)} %get-tuple-element.60.one_ref, bf16[256,768]{1,0:T(8,128)(2,1)} %get-tuple-element.73.gq_ref, f32[256,768]{1,0:T(8,128)} %get-tuple-element.74.gmid_ref, ...), custom_call_target="tpu_custom_call" | custom-call | flops 1000000000 | bytes 5000000 | tf_op jit(solution)/shard_map/last/pallas_call | solution.py:775
  178.0 11.7 %all_to_all.37.attn_ref = bf16[4,96,512]{2,1,0:T(8,128)(2,1)} all-to-all(bf16[4,96,512]{2,1,0:T(8,128)(2,1)S(1)} %bitcast.28), channel_id=1, replica_groups=mesh['x'=4,'zl'=2,'core'=2,'y'=4,'zh'=2] {'x'}, dimensions={0} | all-to-all | bytes 786432 | tf_op jit(solution)/shard_map/all_to_all | solution.py:969
  189.7 3.2 %unblock.1 = bf16[16,24,1792]{2,1,0:T(8,128)(2,1)} custom-call(bf16[4,96,512]{2,1,0:T(8,128)(2,1)} %all_to_all.37.attn_ref, bf16[96,768]{1,0:T(8,128)(2,1)} %bitcast.33, bf16[2,48,5888]{2,1,0:T(8,128)(2,1)} %bitcast.32), custom_call_target="tpu_custom_call" | custom-call | tf_op jit(solution)/shard_map/unblock/pallas_call | solution.py:775
  192.9 24.8 %all_to_all.38.piece_ref = bf16[16,24,1792]{2,1,0:T(8,128)(2,1)} all-to-all(bf16[16,24,1792]{2,1,0:T(8,128)(2,1)} %unblock.1), channel_id=1, replica_groups=mesh['x'=4,'zl'=2,'core'=2,'y'=4,'zh'=2] {'zl','y','zh'}, dimensions={0} | all-to-all | bytes 2752512 | tf_op jit(solution)/shard_map/all_to_all | solution.py:988
  217.7 2.4 %finish.1 = (f32[6,896]{1,0:T(8,128)}, f32[6,768]{1,0:T(8,128)}, f32[6,3072]{1,0:T(8,128)}, f32[6,3072]{1,0:T(8,128)}, f32[1,6]{1,0:T(1,128)}, /*index=5*/f32[1,...) custom-call(bf16[16,24,1792]{2,1,0:T(8,128)(2,1)} %all_to_all.38.pie, ...), custom_call_target="tpu_custom_call" | custom-call | tf_op jit(solution)/shard_map/finish/pallas_call | solution.py:775
  (36 shorter events, 7.4 us)
Async XLA Ops:
  7.2 98.4 %all-gather.2.cloned.1.call-start = ((), (), s32[]{:S(2)}) async-start(), calls=%async_computation.8 | async-start | bytes 10616832 | tf_op jit(solution)/shard_map/all_gather | solution.py:831
  76.7 3.1 %copy-start = (bf16[4,96,1792]{2,1,0:T(8,128)(2,1)}, bf16[4,96,1792]{2,1,0:T(8,128)(2,1)S(1)}, u32[]{:S(2)}) copy-start(bf16[4,96,1792]{2,1,0:T(8,128)(2,1)S(1)} %all_to_all.36) | copy-start | bytes 4128772
  76.7 3.1 %collective-permute-start = (bf16[8,48,1792]{2,1,0:T(8,128)(2,1)S(1)}, bf16[8,48,1792]{2,1,0:T(8,128)(2,1)S(1)}, u32[]{:S(2)}, u32[]{:S(2)}) collective-permute-start(bf16[8,48,1792]{2,1,0:T(8,128)(2,1)S(1)} %bitcast.23), channel_id=1, source_target_pairs={{0,8},{1,9},{2,10},{3,11},{4,12},{5,13},{6,14},{7,15},{8,0},{9,1},... | collective-permute-start | bytes 4128776 | tf_op jit(solution)/shard_map/ppermute | solution.py:45
  79.8 1.1 copy-start.1
  84.2 14.7 %all-to-all-start.2 = ((bf16[8,256,128]{2,1,0:T(8,128)(2,1)}), bf16[8,256,128]{2,1,0:T(8,128)(2,1)S(1)}, u32[]{:S(2)}, u32[]{:S(2)}) async-start(bf16[8,256,128]{2,1,0:T(8,128)(2,1)} %get-tuple-element.59), calls=%async_computation.2 | async-start | bytes 1048576 | tf_op jit(solution)/shard_map/all_to_all | solution.py:849
  87.7 102.0 %reduce-scatter.2.cloned.1.call-start = ((), (), s32[]{:S(2)}) async-start(), calls=%async_computation.9 | async-start | bytes 10174464 | tf_op jit(solution)/shard_map/reduce_scatter | solution.py:923
  99.0 0.8 copy-start.5
  122.8 1.1 copy-start.6
  122.9 3.4 %copy-start.3 = (bf16[4,8,48,256]{3,2,1,0:T(8,128)(2,1)S(1)}, bf16[4,8,48,256]{3,2,1,0:T(8,128)(2,1)}, u32[]{:S(2)}) copy-start(bf16[4,8,48,256]{3,2,1,0:T(8,128)(2,1)} %get-tuple-element.69) | copy-start | bytes 2359300
  124.0 2.3 %collective-permute-start.1 = (bf16[4,8,48,256]{3,2,1,0:T(8,128)(2,1)S(1)}, bf16[4,8,48,256]{3,2,1,0:T(8,128)(2,1)S(1)}, u32[]{:S(2)}, u32[]{:S(2)}) collective-permute-start(bf16[4,8,48,256]{3,2,1,0:T(8,128)(2,1)S(1)} %copy-done.6), channel_id=1, source_target_pairs={{0,8},{1,9},{2,10},{3,11},{4,12},{5,13},{6,14},{7,15},{8,0},{9,1},... | collective-permute-start | bytes 2359304 | tf_op jit(solution)/shard_map/ppermute | solution.py:45
  127.4 18.9 %all-to-all-start.3 = ((bf16[4,8,48,256]{3,2,1,0:T(8,128)(2,1)}), bf16[4,8,48,256]{3,2,1,0:T(8,128)(2,1)S(1)}, u32[]{:S(2)}, u32[]{:S(2)}) async-start(bf16[4,8,48,256]{3,2,1,0:T(8,128)(2,1)} %add_convert_fusion), calls=%async_computation.3 | async-start | bytes 1572864 | tf_op jit(solution)/shard_map/all_to_all | solution.py:926
  144.7 14.5 %copy-start.4 = (bf16[8,48,768]{2,1,0:T(8,128)(2,1)S(1)}, bf16[8,48,768]{2,1,0:T(8,128)(2,1)}, u32[]{:S(2)}) copy-start(bf16[8,48,768]{2,1,0:T(8,128)(2,1)} %get-tuple-element.82) | copy-start | bytes 1769476
  144.7 14.5 %collective-permute-start.3 = (bf16[8,48,768]{2,1,0:T(8,128)(2,1)}, bf16[8,48,768]{2,1,0:T(8,128)(2,1)S(1)}, u32[]{:S(2)}, u32[]{:S(2)}) collective-permute-start(bf16[8,48,768]{2,1,0:T(8,128)(2,1)} %get-tuple-element.83), channel_id=1, source_target_pairs={{0,8},{1,9},{2,10},{3,11},{4,12},{5,13},{6,14},{7,15},{8,0},{9,1},... | collective-permute-start | bytes 1769480 | tf_op jit(solution)/shard_map/ppermute | solution.py:45
  146.4 24.0 %all-to-all-start.4 = ((bf16[8,256,128]{2,1,0:T(8,128)(2,1)}), bf16[8,256,128]{2,1,0:T(8,128)(2,1)S(1)}, u32[]{:S(2)}, u32[]{:S(2)}) async-start(bf16[8,256,128]{2,1,0:T(8,128)(2,1)} %bitcast.36), calls=%async_computation.4 | async-start | bytes 1048576 | tf_op jit(solution)/shard_map/all_to_all | solution.py:954
  159.3 16.0 %collective-permute-start.4 = (bf16[2,48,768]{2,1,0:T(8,128)(2,1)S(1)}, bf16[2,48,768]{2,1,0:T(8,128)(2,1)S(1)}, u32[]{:S(2)}, u32[]{:S(2)}) collective-permute-start(bf16[2,48,768]{2,1,0:T(8,128)(2,1)S(1)} %get-tuple-element.99), channel_id=1, source_target_pairs={{0,32},{1,33},{2,34},{3,35},{4,36},{5,37},{6,38},{7,39},{8,40},{9,... | collective-permute-start | bytes 442376 | tf_op jit(solution)/shard_map/ppermute | solution.py:45
  159.3 15.9 %collective-permute-start.6 = (bf16[2,48,768]{2,1,0:T(8,128)(2,1)S(1)}, bf16[2,48,768]{2,1,0:T(8,128)(2,1)S(1)}, u32[]{:S(2)}, u32[]{:S(2)}) collective-permute-start(bf16[2,48,768]{2,1,0:T(8,128)(2,1)S(1)} %get-tuple-element.100), channel_id=1, source_target_pairs={{0,96},{1,97},{2,98},{3,99},{4,100},{5,101},{6,102},{7,103},{8,104... | collective-permute-start | bytes 442376 | tf_op jit(solution)/shard_map/ppermute | solution.py:45
  162.6 12.7 %collective-permute-start.5 = (bf16[2,48,768]{2,1,0:T(8,128)(2,1)S(1)}, bf16[2,48,768]{2,1,0:T(8,128)(2,1)S(1)}, u32[]{:S(2)}, u32[]{:S(2)}) collective-permute-start(bf16[2,48,768]{2,1,0:T(8,128)(2,1)S(1)} %get-tuple-element.101), channel_id=1, source_target_pairs={{0,64},{1,65},{2,66},{3,67},{4,68},{5,69},{6,70},{7,71},{8,72},{9,... | collective-permute-start | bytes 442376 | tf_op jit(solution)/shard_map/ppermute | solution.py:45
  170.4 0.8 copy-start.2
  175.3 1.7 collective-permute-start.2
Sparse Core Ops, SparseCore 0:
  43.9 60.5 all-gather.1
  123.0 60.1 reduce-scatter.1

commit v6 on v5

--- a/solution.py
+++ b/solution.py
@@ -121,14 +121,14 @@
     middle = (small - high).astype(bf16).astype(f32)
     low = small - high - middle
     small = jnp.where(lane < 16, high, jnp.where(lane < 32, middle, low))[:6]
-    row[:, KEYS:SMALL] = attn_ref[:, D:].astype(f32)
-    row[:, SMALL:QUERY] = small
-    row[:, QUERY:OUT] = attn_ref[:, :D].astype(f32)
-    row[:, OUT:FC] = out_ref[...].astype(f32)
-    row[:, FC:PROJ] = fc_ref[...].astype(f32)
-    row[:, PROJ : PROJ + FF] = proj_ref[...].astype(f32)
-    row[:, PROJ + FF :] = jnp.zeros((6, WIDE - PROJ - FF), f32)
-    quarters = [row[:, k * FOLD : (k + 1) * FOLD] for k in range(4)]
+    row[:6, KEYS:SMALL] = attn_ref[:, D:].astype(f32)
+    row[:6, SMALL:QUERY] = small
+    row[:6, QUERY:OUT] = attn_ref[:, :D].astype(f32)
+    row[:6, OUT:FC] = out_ref[...].astype(f32)
+    row[:6, FC:PROJ] = fc_ref[...].astype(f32)
+    row[:6, PROJ : PROJ + FF] = proj_ref[...].astype(f32)
+    row[:6, PROJ + FF :] = jnp.zeros((6, WIDE - PROJ - FF), f32)
+    quarters = [row[:6, k * FOLD : (k + 1) * FOLD] for k in range(4)]
     piece = jnp.concatenate(quarters, 0).astype(bf16)
 
     def copy(k, carry):
@@ -144,8 +144,8 @@
         for k in range(4):
             rows[6 * j : 6 * j + 6, k * FOLD : (k + 1) * FOLD] = piece[6 * k : 6 * k + 6]
     for k in range(4):
-        attn_ref[k] = rows[:, :FC].astype(bf16)
-    feed_ref[...] = rows[:, FC : FC + 2 * FF].astype(bf16)
+        attn_ref[k] = rows[: 2 * ROWS, :FC].astype(bf16)
+    feed_ref[...] = rows[: 2 * ROWS, FC : FC + 2 * FF].astype(bf16)
 
 
 def fold_lanes(rows):
@@ -154,12 +154,12 @@
 
 
 def unblock_kernel(attn_ref, query_ref, feed_ref, piece_ref, rows):
-    rows[:, :G_QUERY] = jnp.sum(attn_ref[...].astype(f32), 0)
-    rows[:, G_QUERY:G_FC] = query_ref[...].astype(f32)
+    rows[: 2 * ROWS, :G_QUERY] = jnp.sum(attn_ref[...].astype(f32), 0)
+    rows[: 2 * ROWS, G_QUERY:G_FC] = query_ref[...].astype(f32)
     for zl in range(2):
         rows[zl * ROWS : (zl + 1) * ROWS, G_FC:G_WIDE] = feed_ref[zl].astype(f32)
     if G_WIDE < 4 * G_FOLD:
-        rows[:, G_WIDE:] = jnp.zeros((2 * ROWS, 4 * G_FOLD - G_WIDE), f32)
+        rows[: 2 * ROWS, G_WIDE:] = jnp.zeros((2 * ROWS, 4 * G_FOLD - G_WIDE), f32)
     for j in range(16):
         piece_ref[j] = fold_lanes(rows[6 * j : 6 * j + 6]).astype(bf16)
 
@@ -168,8 +168,8 @@
     vectors, fcb_ref, value_ref, rows = refs[:7], refs[7], refs[8], refs[9]
     total = jnp.sum(piece_ref[...].astype(f32), 0)
     for k in range(4):
-        rows[:, k * G_FOLD : (k + 1) * G_FOLD] = total[6 * k : 6 * k + 6]
-    total = rows[...]
+        rows[:6, k * G_FOLD : (k + 1) * G_FOLD] = total[6 * k : 6 * k + 6]
+    total = rows[:6]
     attn_ref[:, :D] = total[:, G_QUERY:G_FC]
     attn_ref[:, D:] = total[:, KEYS:SMALL]
     fc_ref[...] = total[:, G_FC:G_OUT]
@@ -684,7 +684,7 @@
     ]
     start(outs)
     gatt_ref[...] = mm(grad_branch, wout[...]).astype(bf16)
-    sums_ref[0:4] = jnp.concatenate(
+    sums = jnp.concatenate(
         [
             jnp.sum(grad_branch.astype(f32), 0, keepdims=True),
             jnp.sum(grad_two * normed, 0, keepdims=True),
@@ -697,9 +697,11 @@
     mine = lax.broadcasted_iota(jnp.int32, (4, 512), 0) == (
         lax.broadcasted_iota(jnp.int32, (4, 512), 1) % 4
     )
+    fc_sums = []
     for g in range(6):
         high, low = split_low(jnp.where(mine, fcsum[:, g * 512 : (g + 1) * 512], 0.0))
-        sums_ref[4:8, g * BLOCK : (g + 1) * BLOCK] = mm(high, gather) + mm(low, gather)
+        fc_sums.append(mm(high, gather) + mm(low, gather))
+    sums_ref[...] = jnp.concatenate([sums, jnp.concatenate(fc_sums, 1)], 0)
     stored(0)
     stored(1)
     finish(outs)
@@ -816,7 +818,7 @@
         "pieces",
         [shape(16, 24, FOLD)],
         [*vectors, w_attn, w_out, w_fc, w_proj],
-        [pltpu.VMEM((6, WIDE), f32)],
+        [pltpu.VMEM((8, WIDE), f32)],
         smem=8,
         moved=2_000_000,
     )
@@ -825,7 +827,7 @@
         "blocks",
         [shape(4, 2 * ROWS, FC), shape(2 * ROWS, 2 * FF)],
         [lax.all_to_all(pieces, ("zl", "y", "zh"), 0, 0)],
-        [pltpu.VMEM((2 * ROWS, WIDE), f32)],
+        [pltpu.VMEM((2 * ROWS + 8, WIDE), f32)],
         moved=4_000_000,
     )
     feed = lax.all_gather(feed_block, ("x", "core"), axis=0, tiled=True)
@@ -972,7 +974,7 @@
         "unblock",
         [shape(16, 24, G_FOLD)],
         [both, grad_q, grad_fc],
-        [pltpu.VMEM((2 * ROWS, 4 * G_FOLD), f32)],
+        [pltpu.VMEM((2 * ROWS + 8, 4 * G_FOLD), f32)],
     )
     results = call(
         finish_kernel,
@@ -986,7 +988,7 @@
         + [shape(1, 6, dtype=f32)] * 7
         + [shape(1, 24, dtype=f32), shape(1, HD, dtype=f32)],
         [lax.all_to_all(pieces, ("zl", "y", "zh"), 0, 0)],
-        [pltpu.VMEM((6, 4 * G_FOLD), f32)],
+        [pltpu.VMEM((8, 4 * G_FOLD), f32)],
     )
     grad_w_attn, grad_w_out, grad_w_fc, grad_w_proj = results[:4]
     gain_one, bias_one, bias_query, bias_out, gain_two, bias_two, bias_proj, bias_fc = (

time: 228 us -> 229 us (level)
  Pallas kernels: 57.1 us -> 65.1 us
  starting transfers between devices: 26.7 us -> 22 us
  waiting for transfers between devices: 21.1 us -> 18.1 us
    pallas_call x10, Pallas kernels: 57.1 us -> 65.1 us  [call(): pl.pallas_call(kernel, out_shape=outs, in_specs=places, out_specs=[VMEM]...]
    all_to_all x1, starting transfers between devices: 12.7 us -> 9.68 us  [local(): grad_kv = lax.all_to_all(grad_kv, CTX, 0, 0)]
    all_to_all x1, starting transfers between devices: 6.32 us -> 3.49 us  [local(): grad_proj = add_all(list(lax.all_to_all(grad_proj, 'y', 0, 0)))]
  transfers between devices with their start and end apart: 12 -> 12, of which waited for: 6 -> 5; matrix products, arithmetic and copies ran while one was open for 1% -> 1% of each run, Pallas kernels for 13% -> 16%
where the time goes in v6:
time: 229 us; the launch traced here: 228 us
  blocking collectives  101 us (44%)
  Pallas kernels  65.1 us (28%)
  starting transfers between devices  22 us (10%)
  waiting for transfers between devices  18.1 us (8%)
  between operations  14.9 us (7%)
  local copies, waits for them, and re-layouts  3.83 us (2%)
  other arithmetic  3.08 us (1%)
    pallas_call x10, Pallas kernels, call(): pl.pallas_call(kernel, out_shape=outs, in_specs=places, out_specs=[VMEM]...  65.1 us
    all_to_all x2, blocking collectives, local(): lax.all_to_all(pieces, ('zl', 'y', 'zh'), 0, 0)  55.1 us
    all_to_all x1, blocking collectives, local(): attn = lax.all_to_all(attn_block, 'x', 0, 0).reshape(8, ROWS, FC)  32.9 us
    all_to_all x1, blocking collectives, local(): both = lax.all_to_all(both, 'x', 0, 0)  12.8 us
    all_to_all x1, starting transfers between devices, local(): grad_kv = lax.all_to_all(grad_kv, CTX, 0, 0)  9.68 us
    ppermute x7, waiting for transfers between devices, send(): return lax.ppermute(value, AXES, route(**shift))  6.28 us
    all_to_all x1, waiting for transfers between devices, local(): kv = lax.all_to_all(kv, CTX, 0, 0).reshape(LENGTH, BLOCK)  6.03 us
    all_to_all x1, waiting for transfers between devices, local(): grad_kv = lax.all_to_all(grad_kv, CTX, 0, 0)  5.78 us
  transfers between devices with their start and end apart: 12, of which 5 were waited for; matrix products, arithmetic and copies ran while one was open for 1% of the time, Pallas kernels for 16%

profile of v6, /device:TPU:0, one launch (start us, length us, event | category | flops | bytes accessed | tf_op | source)
XLA Modules:
  0.0 227.7 jit_solution(15407191759799936496)
XLA Ops:
  7.2 2.2 pieces.1
  9.5 30.9 %all_to_all.35.piece_ref = bf16[16,24,2048]{2,1,0:T(8,128)(2,1)} all-to-all(bf16[16,24,2048]{2,1,0:T(8,128)(2,1)} %pieces.1), channel_id=1, replica_groups=mesh['x'=4,'zl'=2,'core'=2,'y'=4,'zh'=2] {'zl','y','zh'}, dimensions={0} | all-to-all | bytes 3145728 | tf_op jit(solution)/shard_map/all_to_all | solution.py:829
  40.4 3.4 %blocks.1 = (bf16[4,96,1792]{2,1,0:T(8,128)(2,1)}, bf16[96,6144]{1,0:T(8,128)(2,1)}) custom-call(bf16[16,24,2048]{2,1,0:T(8,128)(2,1)} %all_to_all.35.piece_ref), custom_call_target="tpu_custom_call" | custom-call | bytes 4000000 | tf_op jit(solution)/shard_map/blocks/pallas_call | solution.py:777
  43.8 32.9 %all_to_all.36 = bf16[4,96,1792]{2,1,0:T(8,128)(2,1)S(1)} all-to-all(bf16[4,96,1792]{2,1,0:T(8,128)(2,1)} %get-tuple-element.58), channel_id=1, replica_groups=mesh['x'=4,'zl'=2,'core'=2,'y'=4,'zh'=2] {'x'}, dimensions={0} | all-to-all | bytes 2752512 | tf_op jit(solution)/shard_map/all_to_all | solution.py:834
  76.7 3.1 %collective-permute-done.other_ref = bf16[8,48,1792]{2,1,0:T(8,128)(2,1)S(1)} collective-permute-done((bf16[8,48,1792]{2,1,0:T(8,128)(2,1)S(1)}, bf16[8,48,1792]{2,1,0:T(8,128)(2,1)S(1)}, u32[]{:S(2)}, u32[]{:S(2)}) %collective-permute-start) | collective-permute-done | bytes 1376288 | tf_op jit(solution)/shard_map/ppermute | solution.py:45
  80.9 3.4 %first.1 = (bf16[256,768]{1,0:T(8,128)(2,1)}, bf16[8,256,128]{2,1,0:T(8,128)(2,1)}, f32[16,768]{1,0:T(8,128)}, bf16[768,256]{1,0:T(8,128)(2,1)}) custom-call(bf16[256,768]{1,0:T(8,128)(2,1)} %bitcast.29, f32[1,64]{1,0:T(1,128)} %bitcast.37, bf16[8,48,1792]{2,1,0:T(8,128)(2,1)} %bitcast.24, bf16[8,48,1792]{2,1,0:T(8,128)(2,1)} %copy-done.1), custom_call_target="tpu_custom_call" | custom-call | flops 100000000 | bytes 4000000 | tf_op jit(solution)/shard_map/first/pallas_call | solution.py:777
  84.2 3.5 %all-to-all-start.2 = ((bf16[8,256,128]{2,1,0:T(8,128)(2,1)}), bf16[8,256,128]{2,1,0:T(8,128)(2,1)S(1)}, u32[]{:S(2)}, u32[]{:S(2)}) async-start(bf16[8,256,128]{2,1,0:T(8,128)(2,1)} %get-tuple-element.59), calls=%async_computation.2 | async-start | bytes 1048576 | tf_op jit(solution)/shard_map/all_to_all | solution.py:851
  88.4 4.5 %query.1 = (bf16[256,768]{1,0:T(8,128)(2,1)}, bf16[2,6,256,256]{3,2,1,0:T(8,128)(2,1)}, f32[1,3072]{1,0:T(1,128)}, bf16[768,768]{1,0:T(8,128)(2,1)}) custom-call(s32[1]{0:T(128)S(6)} %copy.33.length_ref, s32[1,16]{1,0:T(1,128)} %order_ref.5, s32[1,2048]{1,0:T(1,128)} %files_ref.5, bf16[256,768]{1,0:T(8,128)(2,1)} %get-tuple-element.60.one_ref, ...), custom_call_target="tpu_custom_call" | custom-call | flops 300000000 | bytes 4000000 | tf_op jit(solution)/shard_map/query/pallas_call | solution.py:777
  92.9 6.0 %all-to-all-done.2 = bf16[8,256,128]{2,1,0:T(8,128)(2,1)S(1)} async-done(((bf16[8,256,128]{2,1,0:T(8,128)(2,1)}), bf16[8,256,128]{2,1,0:T(8,128)(2,1)S(1)}, u32[]{:S(2)}, u32[]{:S(2)}) %all-to-all-start.2) | async-done | bytes 524320 | tf_op jit(solution)/shard_map/all_to_all | solution.py:851
  99.8 8.2 %attend.1 = (bf16[256,768]{1,0:T(8,128)(2,1)}, f32[2,6,8,256]{3,2,1,0:T(8,128)}) custom-call(s32[1]{0:T(128)S(6)} %copy.33.length_ref, s32[1,16]{1,0:T(1,128)} %order_ref.5, s32[1,2048]{1,0:T(1,128)} %files_ref.5, bf16[2048,128]{1,0:T(8,128)(2,1)} %bitcast.34, bf16[2,6,256,256]{3,2,1,0:T(8,128)(2,1)} %get-tuple-element.63.qt_ref), custom_call_target="tpu_custom_call" | custom-call | flops 10000000000 | bytes 4000000 | tf_op jit(solution)/shard_map/attend/pallas_call | solution.py:777
  108.0 17.2 %feed.1 = (bf16[256,768]{1,0:T(8,128)(2,1)}, f32[256,768]{1,0:T(8,128)}, bf16[256,768]{1,0:T(8,128)(2,1)}, f32[8,768]{1,0:T(8,128)}, bf16[4,8,48,256]{3,2,1,0:T(...) custom-call(bf16[768,6144]{1,0:T(8,128)(2,1)} %all-gather.2.cloned.1.call-done.feed_ref, ...), custom_call_target="tpu_custom_call" | custom-call | flops 8000000000 | bytes 30000000 | tf_op jit(solution)/shard_map/feed/pallas_call | solution.py:777
  126.4 2.3 %collective-permute-done.1 = bf16[4,8,48,256]{3,2,1,0:T(8,128)(2,1)S(1)} collective-permute-done((bf16[4,8,48,256]{3,2,1,0:T(8,128)(2,1)S(1)}, bf16[4,8,48,256]{3,2,1,0:T(8,128)(2,1)S(1)}, u32[]{:S(2)}, u32[]{:S(2)}) %collective-permute-start.1) | collective-permute-done | bytes 786464 | tf_op jit(solution)/shard_map/ppermute | solution.py:45
  128.6 1.1 add_convert_fusion
  129.7 3.5 %all-to-all-start.3 = ((bf16[4,8,48,256]{3,2,1,0:T(8,128)(2,1)}), bf16[4,8,48,256]{3,2,1,0:T(8,128)(2,1)S(1)}, u32[]{:S(2)}, u32[]{:S(2)}) async-start(bf16[4,8,48,256]{3,2,1,0:T(8,128)(2,1)} %add_convert_fusion), calls=%async_computation.3 | async-start | bytes 1572864 | tf_op jit(solution)/shard_map/all_to_all | solution.py:928
  133.2 16.5 %attend_back.1 = (bf16[256,768]{1,0:T(8,128)(2,1)}, bf16[8,48,768]{2,1,0:T(8,128)(2,1)}, bf16[8,48,768]{2,1,0:T(8,128)(2,1)}, bf16[16,128,128]{2,1,0:T(8,128)(2,1)}) custom-call(s32[1]{0:T(128)S(6)} %copy.33.length_ref, s32[1,16]{1,0:T(1,128)} %order_ref.5, s32[1,2048]{1,0:T(1,128)} %files_ref.5, bf16[256,768]{1,0:T(8,128)(2,1)} %get-tuple-element.67.q_ref, ...), custom_call_target="tpu_custom_call" | custom-call | flops 20000000000 | bytes 6000000 | tf_op jit(solution)/shard_map/attend_back/pallas_call | solution.py:777
  149.9 9.7 %all-to-all-start.4 = ((bf16[8,256,128]{2,1,0:T(8,128)(2,1)}), bf16[8,256,128]{2,1,0:T(8,128)(2,1)S(1)}, u32[]{:S(2)}, u32[]{:S(2)}) async-start(bf16[8,256,128]{2,1,0:T(8,128)(2,1)} %bitcast.36), calls=%async_computation.4 | async-start | bytes 1048576 | tf_op jit(solution)/shard_map/all_to_all | solution.py:956
  159.8 3.2 %collective-permute-start.6 = (bf16[2,48,768]{2,1,0:T(8,128)(2,1)S(1)}, bf16[2,48,768]{2,1,0:T(8,128)(2,1)S(1)}, u32[]{:S(2)}, u32[]{:S(2)}) collective-permute-start(bf16[2,48,768]{2,1,0:T(8,128)(2,1)S(1)} %get-tuple-element.100), channel_id=1, source_target_pairs={{0,96},{1,97},{2,98},{3,99},{4,100},{5,101},{6,102},{7,103},{8,104... | collective-permute-start | bytes 442376 | tf_op jit(solution)/shard_map/ppermute | solution.py:45
  163.0 2.0 collective-permute-start.5
  165.0 5.8 %all-to-all-done.4.dkv_ref = bf16[8,256,128]{2,1,0:T(8,128)(2,1)S(1)} async-done(((bf16[8,256,128]{2,1,0:T(8,128)(2,1)}), bf16[8,256,128]{2,1,0:T(8,128)(2,1)S(1)}, u32[]{:S(2)}, u32[]{:S(2)}) %all-to-all-start.4) | async-done | bytes 524320 | tf_op jit(solution)/shard_map/all_to_all | solution.py:956
  171.6 4.1 %last.1 = (bf16[256,768]{1,0:T(8,128)(2,1)}, bf16[8,48,256]{2,1,0:T(8,128)(2,1)}, bf16[8,48,256]{2,1,0:T(8,128)(2,1)}) custom-call(bf16[256,768]{1,0:T(8,128)(2,1)} %bitcast.31, bf16[256,768]{1,0:T(8,128)(2,1)} %get-tuple-element.60.one_ref, bf16[256,768]{1,0:T(8,128)(2,1)} %get-tuple-element.73.gq_ref, f32[256,768]{1,0:T(8,128)} %get-tuple-element.74.gmid_ref, ...), custom_call_target="tpu_custom_call" | custom-call | flops 1000000000 | bytes 5000000 | tf_op jit(solution)/shard_map/last/pallas_call | solution.py:777
  178.4 12.8 %all_to_all.37.attn_ref = bf16[4,96,512]{2,1,0:T(8,128)(2,1)} all-to-all(bf16[4,96,512]{2,1,0:T(8,128)(2,1)S(1)} %bitcast.28), channel_id=1, replica_groups=mesh['x'=4,'zl'=2,'core'=2,'y'=4,'zh'=2] {'x'}, dimensions={0} | all-to-all | bytes 786432 | tf_op jit(solution)/shard_map/all_to_all | solution.py:971
  191.1 3.2 %unblock.1 = bf16[16,24,1792]{2,1,0:T(8,128)(2,1)} custom-call(bf16[4,96,512]{2,1,0:T(8,128)(2,1)} %all_to_all.37.attn_ref, bf16[96,768]{1,0:T(8,128)(2,1)} %bitcast.33, bf16[2,48,5888]{2,1,0:T(8,128)(2,1)} %bitcast.32), custom_call_target="tpu_custom_call" | custom-call | tf_op jit(solution)/shard_map/unblock/pallas_call | solution.py:777
  194.4 24.2 %all_to_all.38.piece_ref = bf16[16,24,1792]{2,1,0:T(8,128)(2,1)} all-to-all(bf16[16,24,1792]{2,1,0:T(8,128)(2,1)} %unblock.1), channel_id=1, replica_groups=mesh['x'=4,'zl'=2,'core'=2,'y'=4,'zh'=2] {'zl','y','zh'}, dimensions={0} | all-to-all | bytes 2752512 | tf_op jit(solution)/shard_map/all_to_all | solution.py:990
  218.5 2.4 %finish.1 = (f32[6,896]{1,0:T(8,128)}, f32[6,768]{1,0:T(8,128)}, f32[6,3072]{1,0:T(8,128)}, f32[6,3072]{1,0:T(8,128)}, f32[1,6]{1,0:T(1,128)}, /*index=5*/f32[1,...) custom-call(bf16[16,24,1792]{2,1,0:T(8,128)(2,1)} %all_to_all.38.pie, ...), custom_call_target="tpu_custom_call" | custom-call | tf_op jit(solution)/shard_map/finish/pallas_call | solution.py:777
  (36 shorter events, 6.9 us)
Async XLA Ops:
  7.2 100.8 %all-gather.2.cloned.1.call-start = ((), (), s32[]{:S(2)}) async-start(), calls=%async_computation.8 | async-start | bytes 10616832 | tf_op jit(solution)/shard_map/all_gather | solution.py:833
  76.7 3.1 %copy-start = (bf16[4,96,1792]{2,1,0:T(8,128)(2,1)}, bf16[4,96,1792]{2,1,0:T(8,128)(2,1)S(1)}, u32[]{:S(2)}) copy-start(bf16[4,96,1792]{2,1,0:T(8,128)(2,1)S(1)} %all_to_all.36) | copy-start | bytes 4128772
  76.7 3.1 %collective-permute-start = (bf16[8,48,1792]{2,1,0:T(8,128)(2,1)S(1)}, bf16[8,48,1792]{2,1,0:T(8,128)(2,1)S(1)}, u32[]{:S(2)}, u32[]{:S(2)}) collective-permute-start(bf16[8,48,1792]{2,1,0:T(8,128)(2,1)S(1)} %bitcast.23), channel_id=1, source_target_pairs={{0,8},{1,9},{2,10},{3,11},{4,12},{5,13},{6,14},{7,15},{8,0},{9,1},... | collective-permute-start | bytes 4128776 | tf_op jit(solution)/shard_map/ppermute | solution.py:45
  79.8 1.1 copy-start.1
  84.2 14.7 %all-to-all-start.2 = ((bf16[8,256,128]{2,1,0:T(8,128)(2,1)}), bf16[8,256,128]{2,1,0:T(8,128)(2,1)S(1)}, u32[]{:S(2)}, u32[]{:S(2)}) async-start(bf16[8,256,128]{2,1,0:T(8,128)(2,1)} %get-tuple-element.59), calls=%async_computation.2 | async-start | bytes 1048576 | tf_op jit(solution)/shard_map/all_to_all | solution.py:851
  87.7 103.4 %reduce-scatter.2.cloned.1.call-start = ((), (), s32[]{:S(2)}) async-start(), calls=%async_computation.9 | async-start | bytes 10174464 | tf_op jit(solution)/shard_map/reduce_scatter | solution.py:925
  99.0 0.8 copy-start.5
  125.2 1.1 copy-start.6
  125.2 3.4 %copy-start.3 = (bf16[4,8,48,256]{3,2,1,0:T(8,128)(2,1)S(1)}, bf16[4,8,48,256]{3,2,1,0:T(8,128)(2,1)}, u32[]{:S(2)}) copy-start(bf16[4,8,48,256]{3,2,1,0:T(8,128)(2,1)} %get-tuple-element.69) | copy-start | bytes 2359300
  126.4 2.3 %collective-permute-start.1 = (bf16[4,8,48,256]{3,2,1,0:T(8,128)(2,1)S(1)}, bf16[4,8,48,256]{3,2,1,0:T(8,128)(2,1)S(1)}, u32[]{:S(2)}, u32[]{:S(2)}) collective-permute-start(bf16[4,8,48,256]{3,2,1,0:T(8,128)(2,1)S(1)} %copy-done.6), channel_id=1, source_target_pairs={{0,8},{1,9},{2,10},{3,11},{4,12},{5,13},{6,14},{7,15},{8,0},{9,1},... | collective-permute-start | bytes 2359304 | tf_op jit(solution)/shard_map/ppermute | solution.py:45
  129.7 20.0 %all-to-all-start.3 = ((bf16[4,8,48,256]{3,2,1,0:T(8,128)(2,1)}), bf16[4,8,48,256]{3,2,1,0:T(8,128)(2,1)S(1)}, u32[]{:S(2)}, u32[]{:S(2)}) async-start(bf16[4,8,48,256]{3,2,1,0:T(8,128)(2,1)} %add_convert_fusion), calls=%async_computation.3 | async-start | bytes 1572864 | tf_op jit(solution)/shard_map/all_to_all | solution.py:928
  149.8 9.8 %copy-start.4 = (bf16[8,48,768]{2,1,0:T(8,128)(2,1)S(1)}, bf16[8,48,768]{2,1,0:T(8,128)(2,1)}, u32[]{:S(2)}) copy-start(bf16[8,48,768]{2,1,0:T(8,128)(2,1)} %get-tuple-element.82) | copy-start | bytes 1769476
  149.8 9.8 %collective-permute-start.3 = (bf16[8,48,768]{2,1,0:T(8,128)(2,1)}, bf16[8,48,768]{2,1,0:T(8,128)(2,1)S(1)}, u32[]{:S(2)}, u32[]{:S(2)}) collective-permute-start(bf16[8,48,768]{2,1,0:T(8,128)(2,1)} %get-tuple-element.83), channel_id=1, source_target_pairs={{0,8},{1,9},{2,10},{3,11},{4,12},{5,13},{6,14},{7,15},{8,0},{9,1},... | collective-permute-start | bytes 1769480 | tf_op jit(solution)/shard_map/ppermute | solution.py:45
  149.9 20.9 %all-to-all-start.4 = ((bf16[8,256,128]{2,1,0:T(8,128)(2,1)}), bf16[8,256,128]{2,1,0:T(8,128)(2,1)S(1)}, u32[]{:S(2)}, u32[]{:S(2)}) async-start(bf16[8,256,128]{2,1,0:T(8,128)(2,1)} %bitcast.36), calls=%async_computation.4 | async-start | bytes 1048576 | tf_op jit(solution)/shard_map/all_to_all | solution.py:956
  159.7 16.0 %collective-permute-start.4 = (bf16[2,48,768]{2,1,0:T(8,128)(2,1)S(1)}, bf16[2,48,768]{2,1,0:T(8,128)(2,1)S(1)}, u32[]{:S(2)}, u32[]{:S(2)}) collective-permute-start(bf16[2,48,768]{2,1,0:T(8,128)(2,1)S(1)} %get-tuple-element.99), channel_id=1, source_target_pairs={{0,32},{1,33},{2,34},{3,35},{4,36},{5,37},{6,38},{7,39},{8,40},{9,... | collective-permute-start | bytes 442376 | tf_op jit(solution)/shard_map/ppermute | solution.py:45
  159.8 15.9 %collective-permute-start.6 = (bf16[2,48,768]{2,1,0:T(8,128)(2,1)S(1)}, bf16[2,48,768]{2,1,0:T(8,128)(2,1)S(1)}, u32[]{:S(2)}, u32[]{:S(2)}) collective-permute-start(bf16[2,48,768]{2,1,0:T(8,128)(2,1)S(1)} %get-tuple-element.100), channel_id=1, source_target_pairs={{0,96},{1,97},{2,98},{3,99},{4,100},{5,101},{6,102},{7,103},{8,104... | collective-permute-start | bytes 442376 | tf_op jit(solution)/shard_map/ppermute | solution.py:45
  163.0 12.7 %collective-permute-start.5 = (bf16[2,48,768]{2,1,0:T(8,128)(2,1)S(1)}, bf16[2,48,768]{2,1,0:T(8,128)(2,1)S(1)}, u32[]{:S(2)}, u32[]{:S(2)}) collective-permute-start(bf16[2,48,768]{2,1,0:T(8,128)(2,1)S(1)} %get-tuple-element.101), channel_id=1, source_target_pairs={{0,64},{1,65},{2,66},{3,67},{4,68},{5,69},{6,70},{7,71},{8,72},{9,... | collective-permute-start | bytes 442376 | tf_op jit(solution)/shard_map/ppermute | solution.py:45
  170.8 0.8 copy-start.2
  175.7 1.7 collective-permute-start.2
Sparse Core Ops, SparseCore 0:
  43.9 60.5 all-gather.1
  125.4 57.9 reduce-scatter.1
